TPU v7x, 128 devices: a whole 4x4x4 slice. The times are simulated.
128 devices in a mesh: gx: 16 (over x, z), gy: 8 (over y, core).
Axes of the slice: x: 4, y: 4, z: 4, core: 2. Of those that a mesh axis runs over, the one named last changes fastest.
Arguments:
- tracers: float32 [2, 16, 2048, 1024], P(None, None, 'gx', 'gy'), may hold values from -6 to 6
- east_flow: bfloat16 [16, 2048, 1024], P(None, 'gx', 'gy'), may hold values from -0.14941406 to 0.14941406
- north_flow: bfloat16 [16, 2048, 1024], P(None, 'gx', 'gy'), may hold values from -0.14941406 to 0.14941406
- levels: int32 [2048, 1024], P('gx', 'gy'), may hold values from 0 to 16, as said below
Outputs:
- new_tracers: float32 [2, 16, 2048, 1024], P(None, None, 'gx', 'gy')
- pressure: float32 [2048, 1024], P('gx', 'gy')
Inputs may be any that keep to these rules, and one draw needn't show every extreme that they name: Land (0) comes in patches, more of it to the east; every ocean column has 1 to 16 levels.
All inputs are finite; a program needn't handle non-finite values.
Results may differ from a plain program's by a relative error of at most 0.0003.
Values may be sent and summed in bfloat16 or wider, within the bound.
No kernel may reach another device: no remote copies, remote signals or barrier semaphores. Data moves between devices by JAX's collectives and lax.ppermute only.
A program may use at most 128 MiB of HBM per device.

v0:
```python
import jax
import jax.numpy as jnp
from jax import lax
from jax.sharding import PartitionSpec as P

NSTEP = 2
ITERS = 3


KAPPA = 0.08
ALPHA = 0.05


def with_halo(block, sides, width):
    for axis, dim in sides:
        count = lax.axis_size(axis)
        forward = [(i, i + 1) for i in range(count - 1)]
        forward.append((count - 1, 0))
        backward = [(target, source) for source, target in forward]
        low = lax.ppermute(
            lax.slice_in_dim(block, block.shape[dim] - width, None, axis=dim), axis, forward
        )
        high = lax.ppermute(lax.slice_in_dim(block, 0, width, axis=dim), axis, backward)
        block = jnp.concatenate([low, block, high], axis=dim)
    return block


def flux_step(tracer_ext, east_ext, north_ext, wet_ext):
    open_east = wet_ext[:, :-1, :] * wet_ext[:, 1:, :]
    east_face = east_ext[:, :-1, :] * open_east
    here_x = tracer_ext[..., :-1, :]
    there_x = tracer_ext[..., 1:, :]
    east_flux = (
        jnp.maximum(east_face, 0.0) * here_x
        + jnp.minimum(east_face, 0.0) * there_x
        - KAPPA * open_east * (there_x - here_x)
    )
    open_north = wet_ext[:, :, :-1] * wet_ext[:, :, 1:]
    north_face = north_ext[:, :, :-1] * open_north
    here_y = tracer_ext[..., :, :-1]
    there_y = tracer_ext[..., :, 1:]
    north_flux = (
        jnp.maximum(north_face, 0.0) * here_y
        + jnp.minimum(north_face, 0.0) * there_y
        - KAPPA * open_north * (there_y - here_y)
    )
    inner = tracer_ext[..., 1:-1, 1:-1]
    east_div = east_flux[..., 1:, 1:-1] - east_flux[..., :-1, 1:-1]
    north_div = north_flux[..., 1:-1, 1:] - north_flux[..., 1:-1, :-1]
    return (inner - east_div - north_div) * wet_ext[:, 1:-1, 1:-1]


def square_sum(residual, precond):
    return lax.psum(jnp.sum(residual * precond), ("gx", "gy"))


def krylov(operate, rhs, diagonal):
    solution = jnp.zeros_like(rhs)
    residual = rhs
    precond = residual / diagonal
    direction = precond
    rz_now = square_sum(residual, precond)
    for step_index in range(ITERS):
        image = operate(direction)
        alpha = rz_now / lax.psum(jnp.sum(direction * image), ("gx", "gy"))
        solution = solution + alpha * direction
        residual = residual - alpha * image
        if step_index + 1 < ITERS:
            precond = residual / diagonal
            rz_next = square_sum(residual, precond)
            direction = precond + rz_next / rz_now * direction
            rz_now = rz_next
    return solution


def on_device(tracers, east_flow, north_flow, levels):
    row_index = lax.axis_index("gy")
    row_count = lax.axis_size("gy")
    depth_levels = tracers.shape[1]
    size_x, size_y = levels.shape
    packed = levels.astype(jnp.bfloat16)[None]
    rim_width = 1
    east_ext, north_ext, depth_ext = (
        with_halo(east_flow, (("gx", 1), ("gy", 2)), 1),
        with_halo(north_flow, (("gx", 1), ("gy", 2)), 1),
        with_halo(packed, (("gx", 1), ("gy", 2)), 1),
    )
    east_ext = east_ext.astype(jnp.float32)
    north_ext = north_ext.astype(jnp.float32)
    depth_ext = depth_ext[0].astype(jnp.float32)
    y_index = lax.broadcasted_iota(jnp.int32, depth_ext.shape, 1)
    y_length = depth_ext.shape[1]
    outside = (y_index < rim_width) & (row_index == 0) | (y_index >= y_length - rim_width) & (
        row_index == row_count - 1
    )
    depth_ext = jnp.where(outside, 0.0, depth_ext)
    level_index = lax.broadcasted_iota(jnp.float32, (depth_levels, 1, 1), 0)
    wet_ext = (level_index < depth_ext[None]).astype(jnp.float32)
    column = tracers
    for step_index in range(NSTEP):
        widened = with_halo(column, (("gx", 2), ("gy", 3)), 1)
        column = flux_step(widened, east_ext, north_ext, wet_ext)
    wet = wet_ext[:, rim_width : rim_width + size_x, rim_width : rim_width + size_y]
    forcing = 0.25 * jnp.sum(wet * (column[0] - 0.8 * column[1]), axis=0)
    scaled = depth_ext / depth_levels
    centre = scaled[rim_width : rim_width + size_x, rim_width : rim_width + size_y]
    east_depth = scaled[rim_width + 1 : rim_width + 1 + size_x, rim_width : rim_width + size_y]
    west_depth = scaled[rim_width - 1 : rim_width - 1 + size_x, rim_width : rim_width + size_y]
    north_depth = scaled[rim_width : rim_width + size_x, rim_width + 1 : rim_width + 1 + size_y]
    south_depth = scaled[rim_width : rim_width + size_x, rim_width - 1 : rim_width - 1 + size_y]
    east_coef = jnp.minimum(centre, east_depth)
    west_coef = jnp.minimum(west_depth, centre)
    north_coef = jnp.minimum(centre, north_depth)
    south_coef = jnp.minimum(south_depth, centre)
    ocean = (levels > 0).astype(jnp.float32)
    diagonal = ALPHA * centre + (1.0 - ocean) + east_coef + west_coef + north_coef + south_coef
    strip_forcing, strip_diag, strip_east, strip_west, strip_north = (
        lax.all_to_all(forcing, "gy", split_axis=0, concat_axis=1, tiled=True),
        lax.all_to_all(diagonal, "gy", split_axis=0, concat_axis=1, tiled=True),
        lax.all_to_all(east_coef, "gy", split_axis=0, concat_axis=1, tiled=True),
        lax.all_to_all(west_coef, "gy", split_axis=0, concat_axis=1, tiled=True),
        lax.all_to_all(north_coef, "gy", split_axis=0, concat_axis=1, tiled=True),
    )
    strip_south = jnp.concatenate([jnp.zeros_like(strip_north[:, :1]), strip_north[:, :-1]], axis=1)

    def operate_strip(field):
        padded = with_halo(field, ((("gx", "gy"), 0),), 1)
        north_value = jnp.concatenate([field[:, 1:], jnp.zeros_like(field[:, :1])], axis=1)
        south_value = jnp.concatenate([jnp.zeros_like(field[:, :1]), field[:, :-1]], axis=1)
        return (
            strip_diag * field
            - strip_east * padded[2:]
            - strip_west * padded[:-2]
            - strip_north * north_value
            - strip_south * south_value
        )

    solved = krylov(operate_strip, strip_forcing, strip_diag)
    pressure = lax.all_to_all(solved, "gy", split_axis=1, concat_axis=0, tiled=True)
    return (column, pressure)


def solution(mesh):
    placed = (P(None, None, "gx", "gy"), P(None, "gx", "gy"), P(None, "gx", "gy"), P("gx", "gy"))
    return jax.shard_map(
        on_device,
        mesh=mesh,
        in_specs=placed,
        out_specs=(P(None, None, "gx", "gy"), P("gx", "gy")),
        check_vma=False,
    )
```

profile of v0, /device:TPU:1, one launch (start us, length us, event | category | flops | bytes accessed | tf_op | source)
XLA Modules:
  0.0 546.7 jit_solution(6016217409582161908)
XLA Ops:
  1.6 6.8 %collective-permute-start.9 = (f32[2,16,1,128]{3,1,2,0:T(8,128)S(1)}, f32[2,16,1,128]{3,1,2,0:T(8,128)S(1)}, u32[]{:S(2)}, u32[]{:S(2)}) collective-permute-start(f32[2,16,1,128]{3,1,2,0:T(8,128)S(1)} %bitcast.185), channel_id=1, source_target_pairs={{8,0},{16,8},{24,16},{32,24},{40,32},{48,40},{56,48},{64,56},{72,6... | collective-permute-start | bytes 49160 | tf_op jit(solution)/shard_map/ppermute | solution.py:23
  10.5 4.8 collective-permute-start.13
  18.5 3.1 copy.43
  31.5 5.5 %collective-permute-start.1 = (bf16[16,1,128]{1,0,2:T(8,128)(2,1)}, bf16[16,1,128]{1,0,2:T(8,128)(2,1)}, u32[]{:S(2)}, u32[]{:S(2)}) collective-permute-start(bf16[16,1,128]{1,0,2:T(8,128)(2,1)} %copy.35), channel_id=1, source_target_pairs={{8,0},{16,8},{24,16},{32,24},{40,32},{48,40},{56,48},{64,56},{72,6... | collective-permute-start | bytes 12296 | tf_op jit(solution)/shard_map/ppermute | solution.py:23
  37.9 10.9 %collective-permute-done.1 = bf16[16,1,128]{1,0,2:T(8,128)(2,1)} collective-permute-done((bf16[16,1,128]{1,0,2:T(8,128)(2,1)}, bf16[16,1,128]{1,0,2:T(8,128)(2,1)}, u32[]{:S(2)}, u32[]{:S(2)}) %collective-permute-start.1) | collective-permute-done | bytes 4128 | tf_op jit(solution)/shard_map/ppermute | solution.py:23
  49.3 4.9 collective-permute-done
  57.0 9.5 %collective-permute-done.12 = bf16[16,1,128]{1,0,2:T(8,128)(2,1)S(1)} collective-permute-done((bf16[16,1,128]{1,0,2:T(8,128)(2,1)S(1)}, bf16[16,1,128]{1,0,2:T(8,128)(2,1)S(1)}, u32[]{:S(2)}, u32[]{:S(2)}) %collective-permute-start.12) | collective-permute-done | bytes 4128 | tf_op jit(solution)/shard_map/ppermute | solution.py:20
  69.5 5.1 fusion.8
  88.9 3.1 multiply_subtract_fusion.1
  91.9 5.5 %multiply_subtract_fusion.3 = f32[2,16,130,129]{2,1,3,0:T(8,128)} fusion(f32[2,16,130,1]{2,1,3,0:T(8,128)S(1)} %collective-permute-done.11, f32[2,16,1,128]{2,1,3,0:T(8,128)S(1)} %copy-done.3, f32[2,16,128,128]{2,1,3,0:T(8,128)S(1)} %copy-done.1, f32[2,16,1,128]{2,1,3,0:T(8,128)S(1)} %copy-done.5, f32[2,16,130,1]{2,1,3,0:T(8,128)S(1)} %collective-permute-done.10, ...), kind=kLoop, calls=%fused_computation.9 | loop fusion | flops 6439680 | bytes 7529600 | tf_op jit(solution)/shard_map/sub | solution.py:43
  97.5 7.1 %fusion.5 = f32[2,16,128,128]{2,1,3,0:T(8,128)S(1)} fusion(f32[2,16,130,129]{2,1,3,0:T(8,128)} %multiply_subtract_fusion.3, f32[2,16,128,128]{2,1,3,0:T(8,128)S(1)} %copy-done.1, f32[2,16,129,130]{2,1,3,0:T(8,128)} %multiply_subtract_fusion.1, f32[16,128,128]{1,0,2:T(8,128)S(1)} %slice.299), kind=kLoop, calls=%fused_computation.23 | loop fusion | flops 2621440 | bytes 13631488 | tf_op jit(solution)/shard_map/mul | solution.py:50
  104.6 2.7 fusion.35
  107.3 2.3 copy.48
  115.8 3.8 collective-permute-done.15
  125.3 5.5 %all-to-all-start.1 = ((f32[8,16,128]{2,1,0:T(8,128)}), f32[8,16,128]{2,1,0:T(8,128)S(1)}, u32[]{:S(2)}, u32[]{:S(2)}) async-start(f32[8,16,128]{2,1,0:T(8,128)} %bitcast.8), calls=%async_computation.1 | async-start | bytes 131072 | tf_op jit(solution)/shard_map/all_to_all | solution.py:119
  130.9 4.1 pad_maximum_fusion.1
  139.1 4.3 multiply_subtract_fusion.2
  148.5 4.8 all-to-all-start.4
  154.1 4.1 all-to-all-done.4
  158.2 4.0 all-to-all-start
  162.2 4.9 all-to-all-done
  167.1 4.0 all-to-all-start.2
  173.0 3.0 all-to-all-done.2
  176.0 5.9 %all-to-all-start.3 = ((f32[8,16,128]{2,1,0:T(8,128)}), f32[8,16,128]{2,1,0:T(8,128)S(1)}, u32[]{:S(2)}, u32[]{:S(2)}) async-start(f32[8,16,128]{2,1,0:T(8,128)} %bitcast.12), calls=%async_computation.3 | async-start | bytes 131072 | tf_op jit(solution)/shard_map/all_to_all | solution.py:121
  182.6 4.2 all-to-all-done.3
  187.5 62.8 %all-reduce.7 = (f32[]{:T(128)}, f32[]{:T(128)}) all-reduce(f32[]{:T(128)} %fusion.31, f32[]{:T(128)} %get-tuple-element.12), channel_id=1, replica_groups=mesh['gx'=16,'gy'=8] {'gx','gy'}, use_global_device_ids=true, to_apply=%region_2.3 | all-reduce | flops 2 | bytes 16 | tf_op jit(solution)/shard_map/psum | solution.py:54
  252.2 62.6 %psum.44 = f32[]{:T(128)} all-reduce(f32[]{:T(128)} %get-tuple-element.10), channel_id=1, replica_groups=mesh['gx'=16,'gy'=8] {'gx','gy'}, use_global_device_ids=true, to_apply=%region_6.7 | all-reduce | flops 1 | bytes 8 | tf_op jit(solution)/shard_map/psum | solution.py:54
  321.7 70.9 %psum.45 = f32[]{:T(128)} all-reduce(f32[]{:T(128)} %get-tuple-element.8), channel_id=1, replica_groups=mesh['gx'=16,'gy'=8] {'gx','gy'}, use_global_device_ids=true, to_apply=%region_8.9 | all-reduce | flops 1 | bytes 8 | tf_op jit(solution)/shard_map/psum | solution.py:65
  394.6 62.5 %psum.46 = f32[]{:T(128)} all-reduce(f32[]{:T(128)} %multiply_reduce_fusion), channel_id=1, replica_groups=mesh['gx'=16,'gy'=8] {'gx','gy'}, use_global_device_ids=true, to_apply=%region_10.11 | all-reduce | flops 1 | bytes 8 | tf_op jit(solution)/shard_map/psum | solution.py:54
  463.9 70.7 %psum.47 = f32[]{:T(128)} all-reduce(f32[]{:T(128)} %fusion.26), channel_id=1, replica_groups=mesh['gx'=16,'gy'=8] {'gx','gy'}, use_global_device_ids=true, to_apply=%region_12.13 | all-reduce | flops 1 | bytes 8 | tf_op jit(solution)/shard_map/psum | solution.py:65
  536.6 4.4 all-to-all-start.5
  542.9 3.0 all-to-all-done.5
  (156 shorter events, 77.9 us)
Async XLA Ops:
  1.6 72.9 %collective-permute-start.9 = (f32[2,16,1,128]{3,1,2,0:T(8,128)S(1)}, f32[2,16,1,128]{3,1,2,0:T(8,128)S(1)}, u32[]{:S(2)}, u32[]{:S(2)}) collective-permute-start(f32[2,16,1,128]{3,1,2,0:T(8,128)S(1)} %bitcast.185), channel_id=1, source_target_pairs={{8,0},{16,8},{24,16},{32,24},{40,32},{48,40},{56,48},{64,56},{72,6... | collective-permute-start | bytes 49160 | tf_op jit(solution)/shard_map/ppermute | solution.py:23
  8.5 68.2 %collective-permute-start.8 = (f32[2,16,1,128]{3,1,2,0:T(8,128)S(1)}, f32[2,16,1,128]{3,1,2,0:T(8,128)S(1)}, u32[]{:S(2)}, u32[]{:S(2)}) collective-permute-start(f32[2,16,1,128]{3,1,2,0:T(8,128)S(1)} %bitcast.184), channel_id=1, source_target_pairs={{0,8},{8,16},{16,24},{24,32},{32,40},{40,48},{48,56},{56,64},{64,7... | collective-permute-start | bytes 49160 | tf_op jit(solution)/shard_map/ppermute | solution.py:20
  10.5 45.3 %collective-permute-start.13 = (bf16[16,1,128]{1,0,2:T(8,128)(2,1)}, bf16[16,1,128]{1,0,2:T(8,128)(2,1)}, u32[]{:S(2)}, u32[]{:S(2)}) collective-permute-start(bf16[16,1,128]{1,0,2:T(8,128)(2,1)} %copy.45), channel_id=1, source_target_pairs={{8,0},{16,8},{24,16},{32,24},{40,32},{48,40},{56,48},{64,56},{72,6... | collective-permute-start | bytes 12296 | tf_op jit(solution)/shard_map/ppermute | solution.py:23
  16.1 9.4 %collective-permute-start.5 = (bf16[1,1,128]{2,1,0:T(2,128)(2,1)S(1)}, bf16[1,1,128]{2,1,0:T(2,128)(2,1)S(1)}, u32[]{:S(2)}, u32[]{:S(2)}) collective-permute-start(bf16[1,1,128]{2,1,0:T(2,128)(2,1)S(1)} %get-tuple-element.55), channel_id=1, source_target_pairs={{8,0},{16,8},{24,16},{32,24},{40,32},{48,40},{56,48},{64,56},{72,6... | collective-permute-start | bytes 776 | tf_op jit(solution)/shard_map/ppermute | solution.py:23
  16.2 9.4 %collective-permute-start.4 = (bf16[1,1,128]{2,1,0:T(2,128)(2,1)S(1)}, bf16[1,1,128]{2,1,0:T(2,128)(2,1)S(1)}, u32[]{:S(2)}, u32[]{:S(2)}) collective-permute-start(bf16[1,1,128]{2,1,0:T(2,128)(2,1)S(1)} %get-tuple-element.54), channel_id=1, source_target_pairs={{0,8},{8,16},{16,24},{24,32},{32,40},{40,48},{48,56},{56,64},{64,7... | collective-permute-start | bytes 776 | tf_op jit(solution)/shard_map/ppermute | solution.py:20
  25.7 5.8 %collective-permute-start.7 = (bf16[1,130,1]{2,1,0:T(8,128)(2,1)S(1)}, bf16[1,130,1]{2,1,0:T(8,128)(2,1)S(1)}, u32[]{:S(2)}, u32[]{:S(2)}) collective-permute-start(bf16[1,130,1]{2,1,0:T(8,128)(2,1)S(1)} %get-tuple-element.51), channel_id=1, source_target_pairs={{1,0},{2,1},{3,2},{4,3},{5,4},{6,5},{7,6},{0,7},{9,8},{10,9},{11,1... | collective-permute-start | bytes 788 | tf_op jit(solution)/shard_map/ppermute | solution.py:23
  27.8 9.2 %collective-permute-start.6 = (bf16[1,130,1]{2,1,0:T(8,128)(2,1)S(1)}, bf16[1,130,1]{2,1,0:T(8,128)(2,1)S(1)}, u32[]{:S(2)}, u32[]{:S(2)}) collective-permute-start(bf16[1,130,1]{2,1,0:T(8,128)(2,1)S(1)} %get-tuple-element.50), channel_id=1, source_target_pairs={{0,1},{1,2},{2,3},{3,4},{4,5},{5,6},{6,7},{7,0},{8,9},{9,10},{10,1... | collective-permute-start | bytes 788 | tf_op jit(solution)/shard_map/ppermute | solution.py:20
  31.5 17.4 %collective-permute-start.1 = (bf16[16,1,128]{1,0,2:T(8,128)(2,1)}, bf16[16,1,128]{1,0,2:T(8,128)(2,1)}, u32[]{:S(2)}, u32[]{:S(2)}) collective-permute-start(bf16[16,1,128]{1,0,2:T(8,128)(2,1)} %copy.35), channel_id=1, source_target_pairs={{8,0},{16,8},{24,16},{32,24},{40,32},{48,40},{56,48},{64,56},{72,6... | collective-permute-start | bytes 12296 | tf_op jit(solution)/shard_map/ppermute | solution.py:23
  37.0 17.1 %collective-permute-start = (bf16[16,1,128]{1,0,2:T(8,128)(2,1)}, bf16[16,1,128]{1,0,2:T(8,128)(2,1)}, u32[]{:S(2)}, u32[]{:S(2)}) collective-permute-start(bf16[16,1,128]{1,0,2:T(8,128)(2,1)} %copy.34), channel_id=1, source_target_pairs={{0,8},{8,16},{16,24},{24,32},{32,40},{40,48},{48,56},{56,64},{64,7... | collective-permute-start | bytes 12296 | tf_op jit(solution)/shard_map/ppermute | solution.py:20
  48.9 17.7 %collective-permute-start.12 = (bf16[16,1,128]{1,0,2:T(8,128)(2,1)S(1)}, bf16[16,1,128]{1,0,2:T(8,128)(2,1)S(1)}, u32[]{:S(2)}, u32[]{:S(2)}) collective-permute-start(bf16[16,1,128]{1,0,2:T(8,128)(2,1)S(1)} %copy-done.27), channel_id=1, source_target_pairs={{0,8},{8,16},{16,24},{24,32},{32,40},{40,48},{48,56},{56,64},{64,7... | collective-permute-start | bytes 12296 | tf_op jit(solution)/shard_map/ppermute | solution.py:20
  55.0 14.5 %collective-permute-start.3 = (bf16[16,130,1]{1,0,2:T(8,128)(2,1)S(1)}, bf16[16,130,1]{1,0,2:T(8,128)(2,1)S(1)}, u32[]{:S(2)}, u32[]{:S(2)}) collective-permute-start(bf16[16,130,1]{1,0,2:T(8,128)(2,1)S(1)} %get-tuple-element.33), channel_id=1, source_target_pairs={{1,0},{2,1},{3,2},{4,3},{5,4},{6,5},{7,6},{0,7},{9,8},{10,9},{11,1... | collective-permute-start | bytes 12488 | tf_op jit(solution)/shard_map/ppermute | solution.py:23
  55.8 13.6 %collective-permute-start.2 = (bf16[16,130,1]{1,0,2:T(8,128)(2,1)S(1)}, bf16[16,130,1]{1,0,2:T(8,128)(2,1)S(1)}, u32[]{:S(2)}, u32[]{:S(2)}) collective-permute-start(bf16[16,130,1]{1,0,2:T(8,128)(2,1)S(1)} %get-tuple-element.32), channel_id=1, source_target_pairs={{0,1},{1,2},{2,3},{3,4},{4,5},{5,6},{6,7},{7,0},{8,9},{9,10},{10,1... | collective-permute-start | bytes 12488 | tf_op jit(solution)/shard_map/ppermute | solution.py:20
  67.4 14.2 %collective-permute-start.14 = (bf16[16,130,1]{1,0,2:T(8,128)(2,1)S(1)}, bf16[16,130,1]{1,0,2:T(8,128)(2,1)S(1)}, u32[]{:S(2)}, u32[]{:S(2)}) collective-permute-start(bf16[16,130,1]{1,0,2:T(8,128)(2,1)S(1)} %pad_maximum_fusion.21), channel_id=1, source_target_pairs={{0,1},{1,2},{2,3},{3,4},{4,5},{5,6},{6,7},{7,0},{8,9},{9,10},{10,1... | collective-permute-start | bytes 12488 | tf_op jit(solution)/shard_map/ppermute | solution.py:20
  79.8 4.0 collective-permute-start.11
  79.8 4.0 collective-permute-start.10
  109.7 4.0 collective-permute-start.16
  113.5 6.1 %collective-permute-start.15 = (f32[2,16,1,128]{3,1,2,0:T(8,128)S(1)}, f32[2,16,1,128]{3,1,2,0:T(8,128)S(1)}, u32[]{:S(2)}, u32[]{:S(2)}) collective-permute-start(f32[2,16,1,128]{3,1,2,0:T(8,128)S(1)} %copy.47), channel_id=1, source_target_pairs={{0,8},{8,16},{16,24},{24,32},{32,40},{40,48},{48,56},{56,64},{64,7... | collective-permute-start | bytes 49160 | tf_op jit(solution)/shard_map/ppermute | solution.py:20
  122.6 8.2 %collective-permute-start.18 = (f32[2,16,130,1]{2,1,3,0:T(8,128)S(1)}, f32[2,16,130,1]{2,1,3,0:T(8,128)S(1)}, u32[]{:S(2)}, u32[]{:S(2)}) collective-permute-start(f32[2,16,130,1]{2,1,3,0:T(8,128)S(1)} %get-tuple-element.19), channel_id=1, source_target_pairs={{1,0},{2,1},{3,2},{4,3},{5,4},{6,5},{7,6},{0,7},{9,8},{10,9},{11,1... | collective-permute-start | bytes 49928 | tf_op jit(solution)/shard_map/ppermute | solution.py:23
  124.5 6.3 %collective-permute-start.17 = (f32[2,16,130,1]{2,1,3,0:T(8,128)S(1)}, f32[2,16,130,1]{2,1,3,0:T(8,128)S(1)}, u32[]{:S(2)}, u32[]{:S(2)}) collective-permute-start(f32[2,16,130,1]{2,1,3,0:T(8,128)S(1)} %get-tuple-element.18), channel_id=1, source_target_pairs={{0,1},{1,2},{2,3},{3,4},{4,5},{5,6},{6,7},{7,0},{8,9},{9,10},{10,1... | collective-permute-start | bytes 49928 | tf_op jit(solution)/shard_map/ppermute | solution.py:20
  125.3 23.2 %all-to-all-start.1 = ((f32[8,16,128]{2,1,0:T(8,128)}), f32[8,16,128]{2,1,0:T(8,128)S(1)}, u32[]{:S(2)}, u32[]{:S(2)}) async-start(f32[8,16,128]{2,1,0:T(8,128)} %bitcast.8), calls=%async_computation.1 | async-start | bytes 131072 | tf_op jit(solution)/shard_map/all_to_all | solution.py:119
  148.5 9.7 %all-to-all-start.4 = ((f32[8,16,128]{2,1,0:T(8,128)}), f32[8,16,128]{2,1,0:T(8,128)S(1)}, u32[]{:S(2)}, u32[]{:S(2)}) async-start(f32[8,16,128]{2,1,0:T(8,128)} %bitcast.14), calls=%async_computation.4 | async-start | bytes 131072 | tf_op jit(solution)/shard_map/all_to_all | solution.py:122
  158.2 8.9 %all-to-all-start = ((f32[8,16,128]{2,1,0:T(8,128)}), f32[8,16,128]{2,1,0:T(8,128)S(1)}, u32[]{:S(2)}, u32[]{:S(2)}) async-start(f32[8,16,128]{2,1,0:T(8,128)} %bitcast.5), calls=%async_computation | async-start | bytes 131072 | tf_op jit(solution)/shard_map/all_to_all | solution.py:118
  167.1 8.9 %all-to-all-start.2 = ((f32[8,16,128]{2,1,0:T(8,128)}), f32[8,16,128]{2,1,0:T(8,128)S(1)}, u32[]{:S(2)}, u32[]{:S(2)}) async-start(f32[8,16,128]{2,1,0:T(8,128)} %bitcast.10), calls=%async_computation.2 | async-start | bytes 131072 | tf_op jit(solution)/shard_map/all_to_all | solution.py:120
  171.2 369.8 %copy-start.19 = (f32[2,16,128,128]{2,1,3,0:T(8,128)S(1)}, f32[2,16,128,128]{2,1,3,0:T(8,128)}, u32[]{:S(2)}) copy-start(f32[2,16,128,128]{2,1,3,0:T(8,128)} %copy-done.18) | copy-start | bytes 6291460
  171.3 15.5 %collective-permute-start.20 = (f32[1,1024]{1,0:T(1,128)S(1)}, f32[1,1024]{1,0:T(1,128)S(1)}, u32[]{:S(2)}, u32[]{:S(2)}) collective-permute-start(f32[1,1024]{1,0:T(1,128)S(1)} %get-tuple-element.47), channel_id=1, source_target_pairs={{0,1},{1,2},{2,3},{3,4},{4,5},{5,6},{6,7},{7,8},{8,9},{9,10},{10,1... | collective-permute-start | bytes 12296 | tf_op jit(solution)/shard_map/ppermute | solution.py:20
  173.0 13.8 %collective-permute-start.19 = (f32[1,1024]{1,0:T(1,128)S(1)}, f32[1,1024]{1,0:T(1,128)S(1)}, u32[]{:S(2)}, u32[]{:S(2)}) collective-permute-start(f32[1,1024]{1,0:T(1,128)S(1)} %get-tuple-element.46), channel_id=1, source_target_pairs={{1,0},{2,1},{3,2},{4,3},{5,4},{6,5},{7,6},{8,7},{9,8},{10,9},{11,1... | collective-permute-start | bytes 12296 | tf_op jit(solution)/shard_map/ppermute | solution.py:23
  176.0 10.7 %all-to-all-start.3 = ((f32[8,16,128]{2,1,0:T(8,128)}), f32[8,16,128]{2,1,0:T(8,128)S(1)}, u32[]{:S(2)}, u32[]{:S(2)}) async-start(f32[8,16,128]{2,1,0:T(8,128)} %bitcast.12), calls=%async_computation.3 | async-start | bytes 131072 | tf_op jit(solution)/shard_map/all_to_all | solution.py:121
  316.2 2.4 collective-permute-start.22
  317.9 3.0 collective-permute-start.21
  458.5 2.4 collective-permute-start.24
  460.2 3.0 collective-permute-start.23
  536.6 9.2 %all-to-all-start.5 = ((f32[16,8,128]{2,0,1:T(8,128)}), f32[16,8,128]{2,0,1:T(8,128)S(1)}, u32[]{:S(2)}, u32[]{:S(2)}) async-start(f32[16,8,128]{2,0,1:T(8,128)} %copy_bitcast_fusion.1), calls=%async_computation.5 | async-start | bytes 131072 | tf_op jit(solution)/shard_map/all_to_all | solution.py:139
  (28 other events, 197.8 us)
where the time goes:
time: 553 us; the launch traced here: 547 us
  blocking collectives  329 us (59%)
  starting transfers between devices  65.6 us (12%)
  waiting for transfers between devices  54.6 us (10%)
  other arithmetic  49.1 us (9%)
  local copies, waits for them, and re-layouts  39.8 us (7%)
  between operations  8.12 us (1%)
    psum x3, blocking collectives, square_sum(): return lax.psum(jnp.sum(residual * precond), ('gx', 'gy'))  188 us
    psum x2, blocking collectives, krylov(): alpha = rz_now / lax.psum(jnp.sum(direction * image), ('gx', 'gy'))  142 us
    ppermute x12, starting transfers between devices, with_halo(): lax.ppermute(lax.slice_in_dim(block, 0, width, axis=dim), axis, backward)  23.7 us
    ppermute x13, waiting for transfers between devices, with_halo(): lax.ppermute(lax.slice_in_dim(block, block.shape[dim] - width, None, axis...  19.5 us
    ppermute x12, waiting for transfers between devices, with_halo(): lax.ppermute(lax.slice_in_dim(block, 0, width, axis=dim), axis, backward)  15.8 us
    unnamed x63, local copies, waits for them, and re-layouts  15 us
    ppermute x13, starting transfers between devices, with_halo(): lax.ppermute(lax.slice_in_dim(block, block.shape[dim] - width, None, axis...  13.4 us
  transfers between devices with their start and end apart: 31, of which 14 were waited for; matrix products, arithmetic and copies ran while one was open for 9% of the time, Pallas kernels for 0%

commit v1 on v0

v1 whole, which is shorter than its diff:
```python
import functools

import jax
import jax.numpy as jnp
from jax import lax
from jax.experimental import pallas as pl
from jax.experimental.pallas import tpu as pltpu
from jax.sharding import PartitionSpec as P

KAPPA = 0.08
ALPHA = 0.05
F32 = jnp.float32

SX = 128
SY = 128
KL = 16
EDGE = 8
PAD = 16
ROWS = SX + 2 * PAD
WIDE = SX + 2 * EDGE
LOW = PAD - EDGE
ARRAYS = 2 * KL + 2 * KL + 1
VMEM = 48 * 1024 * 1024


def lanes(shape=(8, 128)):
    return lax.broadcasted_iota(jnp.int32, shape, len(shape) - 1)


def edges_kernel(t_lo, t_hi, e_lo, e_hi, n_lo, n_hi, d_lo, d_hi, out_lo, out_hi):
    for t, e, n, d, out, at in (
        (t_lo, e_lo, n_lo, d_lo, out_lo, 0),
        (t_hi, e_hi, n_hi, d_hi, out_hi, 8),
    ):
        for k in range(KL):
            out[k] = t[0, k]
            out[KL + k] = t[1, k]
            out[2 * KL + k] = e[k].astype(F32)[at : at + 8]
            out[3 * KL + k] = n[k].astype(F32)[at : at + 8]
        out[4 * KL] = d[...].astype(F32)


def edges(tracers, east, north, levels):
    def spec(shape, at, dim):
        index = [0] * len(shape)
        index[dim] = at
        return pl.BlockSpec(shape, lambda i, index=tuple(index): index)

    t = (2, KL, 8, SY)
    f = (KL, 16, SY)
    d = (8, SY)
    out = jax.ShapeDtypeStruct((ARRAYS, 8, SY), F32)
    whole = pl.BlockSpec((ARRAYS, 8, SY), lambda i: (0, 0, 0))
    return pl.pallas_call(
        edges_kernel,
        grid=(1,),
        in_specs=[
            spec(t, 0, 2),
            spec(t, SX // 8 - 1, 2),
            spec(f, 0, 1),
            spec(f, SX // 16 - 1, 1),
            spec(f, 0, 1),
            spec(f, SX // 16 - 1, 1),
            spec(d, 0, 0),
            spec(d, SX // 8 - 1, 0),
        ],
        out_specs=[whole, whole],
        out_shape=[out, out],
        compiler_params=pltpu.CompilerParams(vmem_limit_bytes=VMEM),
        name="edges",
    )(tracers, tracers, east, east, north, north, levels, levels)


def pack(slices, rows):
    group = lanes((rows, 128)) // 8
    one = jnp.zeros((rows, 128), F32)
    two = jnp.zeros((rows, 128), F32)
    for k in range(KL):
        value = slices(k)
        here = group == k
        one = jnp.where(here, pltpu.roll(value, (8 * k - 123) % 128, 1), one)
        two = jnp.where(here, pltpu.roll(value, (8 * k - 125) % 128, 1), two)
    return one, two


def pack_kernel(t, e, n, d, one, two):
    chunk = 16

    def body(i, carry):
        rows = pl.ds(pl.multiple_of(i * chunk, chunk), chunk)
        out = pl.ds(pl.multiple_of(i * chunk + EDGE, 8), chunk)
        sources = (
            lambda k: t[0, k, rows, :],
            lambda k: t[1, k, rows, :],
            lambda k: e[k, rows, :].astype(F32),
            lambda k: n[k, rows, :].astype(F32),
            lambda k: d[rows, :].astype(F32),
        )
        for a, source in enumerate(sources):
            one[a, out, :], two[a, out, :] = pack(source, chunk)
        return carry

    lax.fori_loop(0, SX // chunk, body, 0)
    for ref in (one, two):
        ref[:, 0:EDGE, :] = jnp.zeros((5, EDGE, 128), F32)
        ref[:, WIDE - EDGE : WIDE, :] = jnp.zeros((5, EDGE, 128), F32)


def pack_rows(tracers, east, north, levels):
    out = jax.ShapeDtypeStruct((5, WIDE, 128), F32)
    return pl.pallas_call(
        pack_kernel,
        out_shape=[out, out],
        compiler_params=pltpu.CompilerParams(vmem_limit_bytes=VMEM),
        name="pack_rows",
    )(tracers, east, north, levels)


def pack_edges_kernel(low, high, one_in, two_in, one, two):
    one[:, EDGE : WIDE - EDGE, :] = one_in[:, EDGE : WIDE - EDGE, :]
    two[:, EDGE : WIDE - EDGE, :] = two_in[:, EDGE : WIDE - EDGE, :]
    for ref, at in ((low, 0), (high, WIDE - EDGE)):
        for a in range(5):
            base = KL * a
            source = (lambda k: ref[base + k]) if a < 4 else (lambda k: ref[base])
            one[a, at : at + 8, :], two[a, at : at + 8, :] = pack(source, 8)


def pack_edges(low, high, one, two):
    out = jax.ShapeDtypeStruct((5, WIDE, 128), F32)
    return pl.pallas_call(
        pack_edges_kernel,
        out_shape=[out, out],
        compiler_params=pltpu.CompilerParams(vmem_limit_bytes=VMEM),
        name="pack_edges",
    )(low, high, one, two)


GROUPS = tuple(range(LOW, LOW + WIDE, 8))


def rows_at(row):
    return slice(row, row + 8)


def ocean_kernel(
    tracers, east, north, levels, low, high, one, two, one_in, two_in, count,
    new, w0_out, w1_out, w2_out, sums_out,
    depth, low_east, low_north, strip_q, strip_depth, strip_flow, edge_q, edge_a, edge_b,
    q0, q1, flow, coef, total, strip_total, field, grid,
):
    lane = lanes()
    member = lane % 8
    strip_level = (lane // 8).astype(F32)
    first = lax.axis_index("gy") == 0
    last = lax.axis_index("gy") == count - 1

    for g in GROUPS:
        r = g - LOW
        if r < EDGE:
            value = low[4 * KL]
        elif r >= WIDE - EDGE:
            value = high[4 * KL]
        else:
            value = levels[rows_at(r - EDGE), :].astype(F32)
        depth[rows_at(g), :] = value
        rows = rows_at(r)
        for a in range(5):
            from_low = one_in[a, rows, :]
            from_high = two_in[a, rows, :]
            if a == 4:
                from_low = jnp.where(first, 0.0, from_low)
                from_high = jnp.where(last, 0.0, from_high)
            low_strip = jnp.where(member < 5, from_low, one[a, rows, :])
            high_strip = jnp.where(member >= 3, from_high, two[a, rows, :])
            for side, value in enumerate((low_strip, high_strip)):
                if a < 2:
                    strip_q[side, a, 0, rows_at(g), :] = value
                elif a < 4:
                    strip_flow[side, a - 2, rows_at(g), :] = value
                else:
                    strip_depth[side, rows_at(g), :] = value
    blank = jnp.zeros((8, 128), F32)
    for outside in (LOW - 8, LOW + WIDE):
        depth[rows_at(outside), :] = blank
        strip_depth[0, rows_at(outside), :] = blank
        strip_depth[1, rows_at(outside), :] = blank

    def merge(low_value, high_value):
        return jnp.where(member == 4, low_value, high_value)

    def face_weights(face, flow_value, threshold):
        is_open = face > threshold
        ahead = jnp.where(is_open, KAPPA + jnp.maximum(flow_value, 0.0), 0.0)
        back = jnp.where(is_open, KAPPA - jnp.minimum(flow_value, 0.0), 0.0)
        return ahead, back

    def weights(depth_ref, face_east, face_north, flow_ref, coef_ref, threshold, south_edge):
        for g in GROUPS:
            rows = rows_at(g)
            a_east, b_east = face_weights(face_east(g), flow_ref[0, rows, :], threshold)
            a_north, b_north = face_weights(face_north(g), flow_ref[1, rows, :], threshold)
            coef_ref[0, rows, :] = a_east
            coef_ref[1, rows, :] = b_east
            coef_ref[2, rows, :] = b_north
            a_south, b_south = south_edge(g, a_north, b_north)
            coef_ref[3, rows, :] = a_south
            leaving = a_east + a_north + coef_ref[1, rows_at(g - 1), :] + b_south
            coef_ref[4, rows, :] = jnp.where(depth_ref[rows, :] > threshold, 1.0 - leaving, 0.0)

    def update(source, coef_ref, g, north_value, south_value):
        rows = rows_at(g)
        value = source[rows, :]
        return (
            coef_ref[4, rows, :] * value
            + coef_ref[1, rows, :] * source[rows_at(g + 1), :]
            + coef_ref[0, rows_at(g - 1), :] * source[rows_at(g - 1), :]
            + coef_ref[2, rows, :] * north_value(value)
            + coef_ref[3, rows, :] * south_value(value)
        )

    def ahead_one(value):
        return pltpu.roll(value, 127, 1)

    def back_one(value):
        return pltpu.roll(value, 1, 1)

    for side in range(2):
        sd = strip_depth.at[side]

        def face_east(g, sd=sd):
            return jnp.minimum(sd[rows_at(g), :], sd[rows_at(g + 1), :])

        def face_north(g, sd=sd):
            value = sd[rows_at(g), :]
            return jnp.minimum(value, ahead_one(value))

        def south_edge(g, a_north, b_north, side=side):
            if side == 0:
                edge_a[rows_at(g), :] = a_north
                edge_b[rows_at(g), :] = b_north
            return back_one(a_north), back_one(b_north)

        coef[1, rows_at(LOW - 8), :] = blank
        weights(sd, face_east, face_north, strip_flow.at[side], coef, strip_level, south_edge)
        for tracer in range(2):
            for g in GROUPS:
                strip_q[side, tracer, 1, rows_at(g), :] = update(
                    strip_q.at[side, tracer, 0], coef, g, ahead_one, back_one
                )
        for g in GROUPS:
            temperature, salinity = (
                update(strip_q.at[side, tracer, 1], coef, g, ahead_one, back_one) for tracer in range(2)
            )
            value = temperature - 0.8 * salinity
            for shift in (8, 16, 32, 64):
                value = value + pltpu.roll(value, shift, 1)
            strip_total[side, rows_at(g), :] = value
    for tracer in range(2):
        for step in range(2):
            for g in GROUPS:
                rows = rows_at(g)
                edge_q[tracer, step, rows, :] = merge(
                    strip_q[0, tracer, step, rows, :], strip_q[1, tracer, step, rows, :]
                )

    def beside(low_value, high_value):
        return jnp.where(lane >= 64, pltpu.roll(low_value, 3, 1), pltpu.roll(high_value, 125, 1))

    def northward(main, side):
        a, b = ahead_one(main), ahead_one(side)
        return jnp.where(lane == 127, b, a), jnp.where(lane == 127, a, b)

    def southward(main, side):
        a, b = back_one(main), back_one(side)
        return jnp.where(lane == 0, b, a), jnp.where(lane == 0, a, b)

    for g in GROUPS + (LOW - 8, LOW + WIDE):
        rows = rows_at(g)
        grid[0, 0, rows, :] = depth[rows, :]
        grid[0, 1, rows, :] = beside(strip_depth[0, rows, :], strip_depth[1, rows, :])
    for g in GROUPS:
        rows = rows_at(g)
        both = grid[0, 0, rows, :], grid[0, 1, rows, :]
        further = northward(*both)
        for part in range(2):
            grid[1, part, rows, :] = jnp.minimum(both[part], grid[0, part, rows_at(g + 1), :])
            grid[2, part, rows, :] = jnp.minimum(both[part], further[part])
        total[rows, :] = blank
    for part in range(2):
        grid[1, part, rows_at(LOW - 8), :] = blank

    def level(k, carry):
        threshold = k.astype(F32)
        turn = (120 + 4 - 8 * k) % 128
        turn = lax.rem(252 - 8 * k, 128)
        for g in GROUPS:
            r = g - LOW
            rows = rows_at(g)
            if r < EDGE or r >= WIDE - EDGE:
                ref = low if r < EDGE else high
                q0[0, rows, :] = ref[k]
                q0[1, rows, :] = ref[KL + k]
                flow[0, rows, :] = ref[2 * KL + k]
                flow[1, rows, :] = ref[3 * KL + k]
            else:
                q0[0, rows, :] = tracers[0, k, rows_at(r - EDGE), :]
                q0[1, rows, :] = tracers[1, k, rows_at(r - EDGE), :]
        flow[0, PAD : PAD + SX, :] = east[k].astype(F32)
        flow[1, PAD : PAD + SX, :] = north[k].astype(F32)

        def south_edge(g, a_north, b_north):
            a_edge = pltpu.roll(edge_a[rows_at(g), :], turn, 1)
            b_edge = pltpu.roll(edge_b[rows_at(g), :], turn, 1)
            return jnp.where(lane == 0, a_edge, back_one(a_north)), jnp.where(lane == 0, b_edge, back_one(b_north))

        weights(
            depth,
            lambda g: grid[1, 0, rows_at(g), :],
            lambda g: grid[2, 0, rows_at(g), :],
            flow,
            coef,
            threshold,
            south_edge,
        )

        def stepped(source, tracer, step, g):
            edge = pltpu.roll(edge_q[tracer, step, rows_at(g), :], turn, 1)
            return update(
                source,
                coef,
                g,
                lambda value: jnp.where(lane == 127, edge, ahead_one(value)),
                lambda value: jnp.where(lane == 0, edge, back_one(value)),
            )

        for tracer in range(2):
            for g in GROUPS:
                q1[tracer, rows_at(g), :] = stepped(q0.at[tracer], tracer, 0, g)
        for g in GROUPS:
            temperature = stepped(q1.at[0], 0, 1, g)
            salinity = stepped(q1.at[1], 1, 1, g)
            if PAD <= g < PAD + SX:
                new[0, k, rows_at(g - PAD), :] = temperature
                new[1, k, rows_at(g - PAD), :] = salinity
            total[rows_at(g), :] += temperature - 0.8 * salinity
        return carry

    lax.fori_loop(0, KL, level, 0)

    scale = 1.0 / KL
    for g in GROUPS:
        rows = rows_at(g)
        souths = southward(grid[2, 0, rows, :], grid[2, 1, rows, :])
        for part in range(2):
            here = grid[0, part, rows, :]
            own = ALPHA * scale * here + jnp.where(here == 0.0, 1.0, 0.0)
            faces = grid[1, part, rows, :] + grid[1, part, rows_at(g - 1), :] + grid[2, part, rows, :] + souths[part]
            diagonal = own + scale * faces
            grid[3, part, rows, :] = 1.0 / diagonal
            grid[4, part, rows, :] = own
            grid[5, part, rows, :] = diagonal
        forcing = 0.25 * total[rows, :]
        forcing_beside = 0.25 * beside(strip_total[0, rows, :], strip_total[1, rows, :])
        field[0, 0, rows, :] = forcing * grid[3, 0, rows, :]
        field[0, 1, rows, :] = forcing_beside * grid[3, 1, rows, :]
    for part in range(2):
        for outside in (LOW - 8, LOW + WIDE):
            for i in range(3):
                field[i, part, rows_at(outside), :] = blank

    moments = [blank] * 6
    for i in range(3):
        for g in GROUPS:
            rows = rows_at(g)
            both = field[i, 0, rows, :], field[i, 1, rows, :]
            norths = northward(*both)
            souths = southward(*both)
            south_faces = southward(grid[2, 0, rows, :], grid[2, 1, rows, :])
            for part in range(2):
                if i == 2 and part == 1:
                    continue
                here = both[part]
                east_gap = here - field[i, part, rows_at(g + 1), :]
                north_gap = here - norths[part]
                east_face = scale * grid[1, part, rows, :]
                north_face = scale * grid[2, part, rows, :]
                own = grid[4, part, rows, :]
                if part == 0 and PAD <= g < PAD + SX:
                    moments[2 * i] += grid[5, 0, rows, :] * here * here
                    moments[2 * i + 1] += (
                        own * here * here + east_face * east_gap * east_gap + north_face * north_gap * north_gap
                    )
                if i < 2:
                    image = (
                        own * here
                        + east_face * east_gap
                        + scale * grid[1, part, rows_at(g - 1), :] * (here - field[i, part, rows_at(g - 1), :])
                        + north_face * north_gap
                        + scale * south_faces[part] * (here - souths[part])
                    )
                    field[i + 1, part, rows, :] = image * grid[3, part, rows, :]
    row = jnp.zeros((8, 128), F32)
    for i in range(6):
        value = jnp.sum(jnp.sum(moments[i], axis=0, keepdims=True), axis=1, keepdims=True)
        row = jnp.where(lane == i, value, row)
    for g in range(0, 128, 8):
        sums_out[rows_at(g), :] = row
    for i, out in enumerate((w0_out, w1_out, w2_out)):
        out[...] = field[i, 0, PAD : PAD + SX, :]


def ocean(tracers, east, north, levels, low, high, one, two, one_in, two_in, count):
    tall = (ROWS, 128)
    plane = jax.ShapeDtypeStruct((SX, SY), F32)
    scratch = [
        tall,
        (8, 128),
        (8, 128),
        (2, 2, 2) + tall,
        (2,) + tall,
        (2, 2) + tall,
        (2, 2) + tall,
        tall,
        tall,
        (2,) + tall,
        (2,) + tall,
        (2,) + tall,
        (5,) + tall,
        tall,
        (2,) + tall,
        (3, 2) + tall,
        (6, 2) + tall,
    ]
    return pl.pallas_call(
        functools.partial(ocean_kernel_with, count),
        out_shape=[jax.ShapeDtypeStruct(tracers.shape, F32), plane, plane, plane, plane],
        scratch_shapes=[pltpu.VMEM(shape, F32) for shape in scratch],
        compiler_params=pltpu.CompilerParams(vmem_limit_bytes=VMEM),
        name="ocean",
    )(tracers, east, north, levels, low, high, one, two, one_in, two_in)


def ocean_kernel_with(count, *refs):
    return ocean_kernel(*refs[:10], count, *refs[10:])


def finish_kernel(sums, w0, w1, w2, out):
    value = sums[0:8, :]
    for g in range(8, 128, 8):
        value = value + sums[rows_at(g), :]
    value = jnp.sum(value, axis=0, keepdims=True)
    lane = lanes((1, 128))
    m0, m1, m2, m3, m4, m5 = (
        jnp.sum(jnp.where(lane == i, value, 0.0), axis=1, keepdims=True) for i in range(6)
    )
    floor = 4e-7
    l10 = m2 / m1
    l20 = m3 / m1
    d1 = m3 - l10 * m2
    t = m4 - l20 * m2
    has1 = d1 > floor * m3
    l21 = jnp.where(has1, t / d1, 0.0)
    d2 = m5 - l20 * m3 - l21 * t
    has2 = has1 & (d2 > floor * m5)
    y1 = m1 - l10 * m0
    y2 = m2 - l20 * m0 - l21 * y1
    c2 = jnp.where(has2, y2 / d2, 0.0)
    c1 = jnp.where(has1, y1 / d1, 0.0) - l21 * c2
    c0 = m0 / m1 - l10 * c1 - l20 * c2
    for g in range(0, SX, 8):
        rows = rows_at(g)
        out[rows, :] = c0 * w0[rows, :] + c1 * w1[rows, :] + c2 * w2[rows, :]


def finish(sums, w0, w1, w2):
    return pl.pallas_call(
        finish_kernel,
        out_shape=jax.ShapeDtypeStruct((SX, SY), F32),
        name="finish",
    )(sums, w0, w1, w2)


def shift(array, axis, step):
    count = lax.axis_size(axis)
    return lax.ppermute(array, axis, [(i, (i + step) % count) for i in range(count)])


def on_device(tracers, east, north, levels):
    first, final = edges(tracers, east, north, levels)
    high = shift(first, "gx", -1)
    low = shift(final, "gx", 1)
    one, two = pack_rows(tracers, east, north, levels)
    one, two = pack_edges(low, high, one, two)
    one_in = shift(one, "gy", 1)
    two_in = shift(two, "gy", -1)
    new, w0, w1, w2, sums = ocean(
        tracers, east, north, levels, low, high, one, two, one_in, two_in, lax.axis_size("gy")
    )
    sums = lax.all_to_all(sums, ("gx", "gy"), split_axis=0, concat_axis=0, tiled=True)
    return new, finish(sums, w0, w1, w2)


def solution(mesh):
    placed = (P(None, None, "gx", "gy"), P(None, "gx", "gy"), P(None, "gx", "gy"), P("gx", "gy"))
    return jax.shard_map(
        on_device,
        mesh=mesh,
        in_specs=placed,
        out_specs=(P(None, None, "gx", "gy"), P("gx", "gy")),
        check_vma=False,
    )
```

time: 553 us -> 62.2 us (0.11); the launches traced: 547 us -> 61.9 us
  blocking collectives: 329 us -> 18.1 us
  starting transfers between devices: 65.6 us -> 9.37 us
  other arithmetic: 49.1 us -> 0 us
  waiting for transfers between devices: 54.6 us -> 10.2 us
  local copies, waits for them, and re-layouts: 39.8 us -> 6.37 us
  Pallas kernels: 0 us -> 17.1 us
  between operations: 8.12 us -> 0.67 us
    psum x5 -> x0, blocking collectives: 329 us -> none  [the longest x3 188 us: square_sum(): return lax.psum(jnp.sum(residual * precond), ('gx', 'gy'))]
    all_to_all x6 -> x0, starting transfers between devices: 28.6 us -> none  [the longest x1 5.86 us: on_device(): lax.all_to_all(west_coef, 'gy', split_axis=0, concat_axis=1, tiled=True)]
    ppermute x25 -> x4, starting transfers between devices: 37.1 us -> 9.37 us  [shift(): lax.ppermute(array, axis, [(i, (i + step) % count) for i in range(count)])]
    ppermute x25 -> x4, waiting for transfers between devices: 35.4 us -> 10.2 us  [shift(): lax.ppermute(array, axis, [(i, (i + step) % count) for i in range(count)])]
    all_to_all x6 -> x0, waiting for transfers between devices: 19.2 us -> none  [the longest x1 4.86 us: on_device(): lax.all_to_all(forcing, 'gy', split_axis=0, concat_axis=1, tiled=True)]
    all_to_all x0 -> x1, blocking collectives: none -> 18.1 us  [on_device(): lax.all_to_all(sums, ('gx', 'gy'), split_axis=0, concat_axis=0, tiled=True)]
    pallas_call x0 -> x5, Pallas kernels: none -> 17.1 us  [the longest x1 12.3 us: ocean(): pl.pallas_call(functools.partial(ocean_kernel_with, count), out_shape=[ja...]
    slice x19 -> x0, local copies, waits for them, and re-layouts: 15.6 us -> none  [the longest x9 10.2 us: with_halo(): lax.slice_in_dim(block, block.shape[dim] - width, None, axis=dim)]
  transfers between devices with their start and end apart: 31 -> 4, of which waited for: 14 -> 3; matrix products, arithmetic and copies ran while one was open for 9% -> 0% of each run, Pallas kernels for 0% -> 4%
where the time goes in v1:
time: 62.2 us; the launch traced here: 61.9 us
  blocking collectives  18.1 us (29%)
  Pallas kernels  17.1 us (27%)
  waiting for transfers between devices  10.2 us (16%)
  starting transfers between devices  9.37 us (15%)
  local copies, waits for them, and re-layouts  6.37 us (10%)
  between operations  0.67 us (1%)
    all_to_all x1, blocking collectives, on_device(): lax.all_to_all(sums, ('gx', 'gy'), split_axis=0, concat_axis=0, tiled=True)  18.1 us
    pallas_call x1, Pallas kernels, ocean(): pl.pallas_call(functools.partial(ocean_kernel_with, count), out_shape=[ja...  12.3 us
    ppermute x4, waiting for transfers between devices, shift(): lax.ppermute(array, axis, [(i, (i + step) % count) for i in range(count)])  10.2 us
    ppermute x4, starting transfers between devices, shift(): lax.ppermute(array, axis, [(i, (i + step) % count) for i in range(count)])  9.37 us
    unnamed x16, local copies, waits for them, and re-layouts  6.37 us
    pallas_call x1, Pallas kernels, pack_rows(): pl.pallas_call(pack_kernel, out_shape=[out, out], compiler_params=pltpu.C...  2.72 us
    pallas_call x1, Pallas kernels, finish(): pl.pallas_call(finish_kernel, out_shape=jax.ShapeDtypeStruct((SX, SY), F3...  1.7 us
  transfers between devices with their start and end apart: 4, of which 3 were waited for; matrix products, arithmetic and copies ran while one was open for 0% of the time, Pallas kernels for 4%

profile of v1, /device:TPU:1, one launch (start us, length us, event | category | flops | bytes accessed | tf_op | source)
XLA Modules:
  0.0 61.9 jit_solution(7120514436959671688)
XLA Ops:
  0.6 0.0 copy-start
  0.6 1.6 %copy-done = f32[2,16,128,128]{3,2,1,0:T(8,128)S(1)} copy-done((f32[2,16,128,128]{3,2,1,0:T(8,128)S(1)}, f32[2,16,128,128]{3,2,1,0:T(8,128)}, u32[]{:S(2)}) %copy-start) | copy-done | bytes 2097176
  2.2 0.0 copy-start.2
  2.2 1.0 %copy-done.2 = bf16[16,128,128]{2,1,0:T(8,128)(2,1)S(1)} copy-done((bf16[16,128,128]{2,1,0:T(8,128)(2,1)S(1)}, bf16[16,128,128]{2,1,0:T(8,128)(2,1)}, u32[]{:S(2)}) %copy-start.2) | copy-done | bytes 524312
  3.3 0.0 copy-start.3
  3.3 1.0 %copy-done.3 = bf16[16,128,128]{2,1,0:T(8,128)(2,1)S(1)} copy-done((bf16[16,128,128]{2,1,0:T(8,128)(2,1)S(1)}, bf16[16,128,128]{2,1,0:T(8,128)(2,1)}, u32[]{:S(2)}) %copy-start.3) | copy-done | bytes 524312
  4.3 0.0 copy-start.4
  4.3 0.8 %copy-done.4 = s32[128,128]{1,0:T(8,128)S(1)} copy-done((s32[128,128]{1,0:T(8,128)S(1)}, s32[128,128]{1,0:T(8,128)}, u32[]{:S(2)}) %copy-start.4) | copy-done | bytes 65560
  5.1 0.1 edges.1
  5.2 2.5 %collective-permute-start = (f32[65,8,128]{2,1,0:T(8,128)S(1)}, f32[65,8,128]{2,1,0:T(8,128)S(1)}, u32[]{:S(2)}, u32[]{:S(2)}) collective-permute-start(f32[65,8,128]{2,1,0:T(8,128)S(1)} %get-tuple-element.13), channel_id=1, source_target_pairs={{0,8},{8,16},{16,24},{24,32},{32,40},{40,48},{48,56},{56,64},{64,7... | collective-permute-start | bytes 798728 | tf_op jit(solution)/shard_map/ppermute | solution.py:486
  7.7 0.0 copy-start.1
  7.8 4.4 %collective-permute-start.1 = (f32[65,8,128]{2,1,0:T(8,128)S(1)}, f32[65,8,128]{2,1,0:T(8,128)S(1)}, u32[]{:S(2)}, u32[]{:S(2)}) collective-permute-start(f32[65,8,128]{2,1,0:T(8,128)S(1)} %get-tuple-element.14), channel_id=1, source_target_pairs={{0,120},{8,0},{16,8},{24,16},{32,24},{40,32},{48,40},{56,48},{64,5... | collective-permute-start | bytes 798728 | tf_op jit(solution)/shard_map/ppermute | solution.py:486
  12.2 2.7 %pack_rows.1 = (f32[5,144,128]{2,1,0:T(8,128)S(1)}, f32[5,144,128]{2,1,0:T(8,128)S(1)}) custom-call(f32[2,16,128,128]{3,2,1,0:T(8,128)S(1)} %copy-done, bf16[16,128,128]{2,1,0:T(8,128)(2,1)S(1)} %copy-done.2, bf16[16,128,128]{2,1,0:T(8,128)(2,1)S(1)} %copy-done.3, s32[128,128]{1,0:T(8,128)S(1)} %copy-done.4), custom_call_target="tpu_custom_call" | custom-call | tf_op jit(solution)/shard_map/pack_rows/pallas_call | solution.py:111
  14.9 3.3 %collective-permute-done.low.refs_4_ = f32[65,8,128]{2,1,0:T(8,128)S(1)} collective-permute-done((f32[65,8,128]{2,1,0:T(8,128)S(1)}, f32[65,8,128]{2,1,0:T(8,128)S(1)}, u32[]{:S(2)}, u32[]{:S(2)}) %collective-permute-start) | collective-permute-done | bytes 266272 | tf_op jit(solution)/shard_map/ppermute | solution.py:486
  18.2 0.0 collective-permute-done.1.high.refs_5_
  18.2 0.4 pack_edges.1
  18.6 2.4 %collective-permute-start.2 = (f32[5,144,128]{2,1,0:T(8,128)S(1)}, f32[5,144,128]{2,1,0:T(8,128)S(1)}, u32[]{:S(2)}, u32[]{:S(2)}) collective-permute-start(f32[5,144,128]{2,1,0:T(8,128)S(1)} %get-tuple-element.17.refs_6_), channel_id=1, source_target_pairs={{0,1},{1,2},{2,3},{3,4},{4,5},{5,6},{6,7},{7,0},{8,9},{9,10},{10,1... | collective-permute-start | bytes 1105928 | tf_op jit(solution)/shard_map/ppermute | solution.py:486
  21.0 0.0 collective-permute-start.3
  21.0 4.5 %collective-permute-done.2.refs_8_ = f32[5,144,128]{2,1,0:T(8,128)S(1)} collective-permute-done((f32[5,144,128]{2,1,0:T(8,128)S(1)}, f32[5,144,128]{2,1,0:T(8,128)S(1)}, u32[]{:S(2)}, u32[]{:S(2)}) %collective-permute-start.2) | collective-permute-done | bytes 368672 | tf_op jit(solution)/shard_map/ppermute | solution.py:486
  25.5 2.5 %collective-permute-done.3.refs_9_ = f32[5,144,128]{2,1,0:T(8,128)S(1)} collective-permute-done((f32[5,144,128]{2,1,0:T(8,128)S(1)}, f32[5,144,128]{2,1,0:T(8,128)S(1)}, u32[]{:S(2)}, u32[]{:S(2)}) %collective-permute-start.3) | collective-permute-done | bytes 368672 | tf_op jit(solution)/shard_map/ppermute | solution.py:486
  28.0 0.0 copy-done.1
  28.0 12.3 %ocean.1 = (f32[2,16,128,128]{3,2,1,0:T(8,128)}, f32[128,128]{1,0:T(8,128)S(1)}, f32[128,128]{1,0:T(8,128)S(1)}, f32[128,128]{1,0:T(8,128)S(1)}, f32[128,128]{1,0:T(8,128)S(1)}) custom-call(f32[2,16,128,128]{3,2,1,0:T(8,128)S(1)} %copy-done.1, bf16[16,128,128]{2,1,0:T(8,128)(2,1)S(1)} %copy-done.2, bf16[16,128,128]{2,1,0:T(8,128)(2,1)S(1)} %copy-done.3, ...), custom_call_target="tpu_custom_call" | custom-call | tf_op jit(solution)/shard_map/ocean/pallas_call | solution.py:435
  40.2 0.0 copy-start.5
  40.2 0.6 %copy-done.5 = f32[128,128]{1,0:T(8,128)} copy-done((f32[128,128]{1,0:T(8,128)}, f32[128,128]{1,0:T(8,128)S(1)}, u32[]{:S(2)}) %copy-start.5) | copy-done | bytes 65560
  40.8 0.0 copy-start.6
  40.8 0.6 copy-done.6
  41.5 0.0 copy-start.7
  41.5 0.6 copy-done.7
  42.1 18.1 %all_to_all.11 = f32[128,1,128]{2,1,0:T(1,128)} all-to-all(f32[128,1,128]{2,1,0:T(1,128)S(1)} %bitcast.4), channel_id=1, replica_groups=mesh['gx'=16,'gy'=8] {'gx','gy'}, dimensions={0} | all-to-all | bytes 131072 | tf_op jit(solution)/shard_map/all_to_all | solution.py:500
  60.2 1.7 %finish.1 = f32[128,128]{1,0:T(8,128)} custom-call(f32[128,128]{1,0:T(8,128)} %bitcast.5, f32[128,128]{1,0:T(8,128)} %copy-done.5, f32[128,128]{1,0:T(8,128)} %copy-done.6, f32[128,128]{1,0:T(8,128)} %copy-done.7), custom_call_target="tpu_custom_call" | custom-call | tf_op jit(solution)/shard_map/finish/pallas_call | solution.py:477
Async XLA Ops:
  0.6 1.6 %copy-start = (f32[2,16,128,128]{3,2,1,0:T(8,128)S(1)}, f32[2,16,128,128]{3,2,1,0:T(8,128)}, u32[]{:S(2)}) copy-start(f32[2,16,128,128]{3,2,1,0:T(8,128)} %refs_0_.1) | copy-start | bytes 6291460
  2.2 1.0 %copy-start.2 = (bf16[16,128,128]{2,1,0:T(8,128)(2,1)S(1)}, bf16[16,128,128]{2,1,0:T(8,128)(2,1)}, u32[]{:S(2)}) copy-start(bf16[16,128,128]{2,1,0:T(8,128)(2,1)} %refs_1_.1) | copy-start | bytes 1572868
  3.3 1.0 %copy-start.3 = (bf16[16,128,128]{2,1,0:T(8,128)(2,1)S(1)}, bf16[16,128,128]{2,1,0:T(8,128)(2,1)}, u32[]{:S(2)}) copy-start(bf16[16,128,128]{2,1,0:T(8,128)(2,1)} %refs_2_.1) | copy-start | bytes 1572868
  4.3 0.8 %copy-start.4 = (s32[128,128]{1,0:T(8,128)S(1)}, s32[128,128]{1,0:T(8,128)}, u32[]{:S(2)}) copy-start(s32[128,128]{1,0:T(8,128)} %refs_3_.1) | copy-start | bytes 196612
  5.2 13.0 %collective-permute-start = (f32[65,8,128]{2,1,0:T(8,128)S(1)}, f32[65,8,128]{2,1,0:T(8,128)S(1)}, u32[]{:S(2)}, u32[]{:S(2)}) collective-permute-start(f32[65,8,128]{2,1,0:T(8,128)S(1)} %get-tuple-element.13), channel_id=1, source_target_pairs={{0,8},{8,16},{16,24},{24,32},{32,40},{40,48},{48,56},{56,64},{64,7... | collective-permute-start | bytes 798728 | tf_op jit(solution)/shard_map/ppermute | solution.py:486
  7.7 20.2 %copy-start.1 = (f32[2,16,128,128]{3,2,1,0:T(8,128)S(1)}, f32[2,16,128,128]{3,2,1,0:T(8,128)}, u32[]{:S(2)}) copy-start(f32[2,16,128,128]{3,2,1,0:T(8,128)} %refs_0_.1) | copy-start | bytes 6291460
  7.8 10.4 %collective-permute-start.1 = (f32[65,8,128]{2,1,0:T(8,128)S(1)}, f32[65,8,128]{2,1,0:T(8,128)S(1)}, u32[]{:S(2)}, u32[]{:S(2)}) collective-permute-start(f32[65,8,128]{2,1,0:T(8,128)S(1)} %get-tuple-element.14), channel_id=1, source_target_pairs={{0,120},{8,0},{16,8},{24,16},{32,24},{40,32},{48,40},{56,48},{64,5... | collective-permute-start | bytes 798728 | tf_op jit(solution)/shard_map/ppermute | solution.py:486
  18.6 6.9 %collective-permute-start.2 = (f32[5,144,128]{2,1,0:T(8,128)S(1)}, f32[5,144,128]{2,1,0:T(8,128)S(1)}, u32[]{:S(2)}, u32[]{:S(2)}) collective-permute-start(f32[5,144,128]{2,1,0:T(8,128)S(1)} %get-tuple-element.17.refs_6_), channel_id=1, source_target_pairs={{0,1},{1,2},{2,3},{3,4},{4,5},{5,6},{6,7},{7,0},{8,9},{9,10},{10,1... | collective-permute-start | bytes 1105928 | tf_op jit(solution)/shard_map/ppermute | solution.py:486
  21.0 6.9 %collective-permute-start.3 = (f32[5,144,128]{2,1,0:T(8,128)S(1)}, f32[5,144,128]{2,1,0:T(8,128)S(1)}, u32[]{:S(2)}, u32[]{:S(2)}) collective-permute-start(f32[5,144,128]{2,1,0:T(8,128)S(1)} %get-tuple-element.18.refs_7_), channel_id=1, source_target_pairs={{0,7},{1,0},{2,1},{3,2},{4,3},{5,4},{6,5},{7,6},{8,15},{9,8},{10,9... | collective-permute-start | bytes 1105928 | tf_op jit(solution)/shard_map/ppermute | solution.py:486
  40.2 0.6 %copy-start.5 = (f32[128,128]{1,0:T(8,128)}, f32[128,128]{1,0:T(8,128)S(1)}, u32[]{:S(2)}) copy-start(f32[128,128]{1,0:T(8,128)S(1)} %get-tuple-element.21.w0) | copy-start | bytes 196612
  40.8 0.6 copy-start.6
  41.5 0.6 copy-start.7

commit v2 on v1

v2 whole, which is shorter than its diff:
```python
import functools

import jax
import jax.numpy as jnp
from jax import lax
from jax.experimental import pallas as pl
from jax.experimental.pallas import tpu as pltpu
from jax.sharding import PartitionSpec as P

KAPPA = 0.08
ALPHA = 0.05
F32 = jnp.float32

SX = 128
SY = 128
KL = 16
EDGE = 8
PAD = 16
ROWS = SX + 2 * PAD
WIDE = SX + 2 * EDGE
LOW = PAD - EDGE
ARRAYS = 2 * KL + 2 * KL + 1
VMEM = 40 * 1024 * 1024
GROUPS = tuple(range(LOW, LOW + WIDE, 8))
OUTSIDE = (LOW - 8, LOW + WIDE)
SENT = 3


def params(limit=VMEM):
    return pltpu.CompilerParams(vmem_limit_bytes=limit)


def rows_at(row):
    return slice(row, row + 8)


def lanes(shape=(8, 128)):
    return lax.broadcasted_iota(jnp.int32, shape, len(shape) - 1)


def ahead_one(value):
    return pltpu.roll(value, 127, 1)


def back_one(value):
    return pltpu.roll(value, 1, 1)


def edges_kernel(t, e, n, d, out_lo, out_hi, flows, depths, sems):
    copies = []
    for side, (out, at) in enumerate(((out_lo, 0), (out_hi, SX - 8))):
        at16 = 0 if side == 0 else SX - 16
        copies += [
            (t.at[0, :, at : at + 8, :], out.at[0:KL]),
            (t.at[1, :, at : at + 8, :], out.at[KL : 2 * KL]),
            (e.at[:, at16 : at16 + 16, :], flows.at[side, 0]),
            (n.at[:, at16 : at16 + 16, :], flows.at[side, 1]),
            (d.at[at : at + 8, :], depths.at[side]),
        ]
    copies = [pltpu.make_async_copy(src, dst, sems.at[i]) for i, (src, dst) in enumerate(copies)]
    for copy in copies:
        copy.start()
    for side, out in enumerate((out_lo, out_hi)):
        for i in range(5):
            copies[5 * side + i].wait()
        for f in range(2):
            for k in range(KL):
                out[(2 + f) * KL + k] = flows[side, f, k].astype(F32)[8 * side : 8 * side + 8]
        out[4 * KL] = depths[side].astype(F32)


def edges(tracers, east, north, levels):
    out = jax.ShapeDtypeStruct((ARRAYS, 8, SY), F32)
    return pl.pallas_call(
        edges_kernel,
        in_specs=[pl.BlockSpec(memory_space=pltpu.HBM)] * 4,
        out_shape=[out, out],
        scratch_shapes=[
            pltpu.VMEM((2, 2, KL, 16, SY), jnp.bfloat16),
            pltpu.VMEM((2, 8, SY), jnp.int32),
            pltpu.SemaphoreType.DMA((10,)),
        ],
        compiler_params=params(62 * 1024 * 1024),
        name="edges",
    )(tracers, east, north, levels)


def pack(source, rows):
    group = lanes((rows, 128)) // 8
    one = jnp.zeros((rows, 128), F32)
    two = jnp.zeros((rows, 128), F32)
    for k in range(KL):
        value = source(k)
        here = group == k
        one = jnp.where(here, pltpu.roll(value, (8 * k - 124) % 128, 1), one)
        two = jnp.where(here, pltpu.roll(value, (8 * k - 125) % 128, 1), two)
    return one, two


def merge_one(t0, t1, e, n, d):
    member = lanes(t0.shape) % 8
    return (
        jnp.where(member < 4, t0, pltpu.roll(n, 4, 1)),
        jnp.where(member < 4, t1, pltpu.roll(e, 4, 1)),
        d,
    )


def split_one(a, b, c):
    return a, b, pltpu.roll(b, 124, 1), pltpu.roll(a, 124, 1), c


def merge_two(t0, t1, e, n, d):
    member = lanes(t0.shape) % 8
    return (
        jnp.where(member < 3, pltpu.roll(d, 125, 1), t0),
        jnp.where(member < 2, pltpu.roll(d, 122, 1), t1),
        jnp.where((member >= 3) & (member < 7), n, pltpu.roll(e, 4, 1)),
    )


def split_two(a, b, c):
    member = lanes(a.shape) % 8
    depth = jnp.where(member < 6, pltpu.roll(a, 3, 1), pltpu.roll(b, 6, 1))
    return a, b, pltpu.roll(c, 124, 1), c, depth


def pack_all(sources, rows, own, own_rows, sent_one, sent_two, sent_rows):
    packed = [pack(source, rows) for source in sources]
    for which in range(2):
        for a in range(5):
            own[which, a, own_rows, :] = packed[a][which]
    for sent, values in (
        (sent_one, merge_one(*(p[0] for p in packed))),
        (sent_two, merge_two(*(p[1] for p in packed))),
    ):
        for a in range(SENT):
            sent[a, sent_rows, :] = values[a]


def pack_rows_kernel(t, e, n, d, own, one, two):
    chunk = 16

    def body(i, carry):
        rows = pl.ds(pl.multiple_of(i * chunk, chunk), chunk)
        sources = (
            lambda k: t[0, k, rows, :],
            lambda k: t[1, k, rows, :],
            lambda k: e[k, rows, :].astype(F32),
            lambda k: n[k, rows, :].astype(F32),
            lambda k: d[rows, :].astype(F32),
        )
        pack_all(sources, chunk, own, rows, one, two, rows)
        return carry

    lax.fori_loop(0, SX // chunk, body, 0)


def pack_rows(tracers, east, north, levels):
    sent = jax.ShapeDtypeStruct((SENT, SX, 128), F32)
    return pl.pallas_call(
        pack_rows_kernel,
        out_shape=[jax.ShapeDtypeStruct((2, 5, SX, 128), F32), sent, sent],
        compiler_params=params(),
        name="pack_rows",
    )(tracers, east, north, levels)


def pack_edges_kernel(low, high, one_rows, two_rows, own, one, two):
    for g in range(0, SX, 8):
        for a in range(SENT):
            one[a, rows_at(g + EDGE), :] = one_rows[a, rows_at(g), :]
            two[a, rows_at(g + EDGE), :] = two_rows[a, rows_at(g), :]
    for ref, own_at, at in ((low, 0, 0), (high, 8, WIDE - EDGE)):
        sources = [(lambda k, a=a, ref=ref: ref[KL * a + k]) for a in range(4)]
        sources.append(lambda k, ref=ref: ref[4 * KL])
        pack_all(sources, 8, own, rows_at(own_at), one, two, rows_at(at))


def pack_edges(low, high, one, two):
    sent = jax.ShapeDtypeStruct((SENT, WIDE, 128), F32)
    return pl.pallas_call(
        pack_edges_kernel,
        out_shape=[jax.ShapeDtypeStruct((2, 5, 2 * EDGE, 128), F32), sent, sent],
        compiler_params=params(),
        name="pack_edges",
    )(low, high, one, two)


def face_weights(face, flow_value, threshold):
    is_open = face > threshold
    ahead = jnp.where(is_open, KAPPA + jnp.maximum(flow_value, 0.0), 0.0)
    back = jnp.where(is_open, KAPPA - jnp.minimum(flow_value, 0.0), 0.0)
    return ahead, back


def set_weights(depth_at, face_east, face_north, flow, coef, threshold, south):
    coef[1, rows_at(LOW - 8), :] = jnp.zeros((8, 128), F32)
    for g in GROUPS:
        rows = rows_at(g)
        a_east, b_east = face_weights(face_east(g), flow[0, rows, :], threshold)
        a_north, b_north = face_weights(face_north(g), flow[1, rows, :], threshold)
        coef[0, rows, :] = a_east
        coef[1, rows, :] = b_east
        coef[2, rows, :] = b_north
        a_south, b_south = south(g, a_north, b_north)
        coef[3, rows, :] = a_south
        leaving = a_east + a_north + coef[1, rows_at(g - 1), :] + b_south
        coef[4, rows, :] = jnp.where(depth_at(g) > threshold, 1.0 - leaving, 0.0)


def update(source, coef, g, south_value=None):
    rows = rows_at(g)
    value = source[rows, :]
    south = back_one(value) if south_value is None else south_value
    return (
        coef[4, rows, :] * value
        + coef[1, rows, :] * source[rows_at(g + 1), :]
        + coef[0, rows_at(g - 1), :] * source[rows_at(g - 1), :]
        + coef[2, rows, :] * ahead_one(value)
        + coef[3, rows, :] * south
    )


def halo_depth(levels, low, high, depth):
    for g in GROUPS:
        r = g - LOW
        if r < EDGE:
            value = low[4 * KL]
        elif r >= WIDE - EDGE:
            value = high[4 * KL]
        else:
            value = levels[rows_at(r - EDGE), :].astype(F32)
        depth[rows_at(g), :] = value
    for outside in OUTSIDE:
        depth[rows_at(outside), :] = jnp.zeros((8, 128), F32)


def levels_kernel(tracers, east, north, levels, low, high, new, total, depth, face, q0, q1, flow, coef):
    lane = lanes()
    halo_depth(levels, low, high, depth)
    for g in GROUPS:
        rows = rows_at(g)
        here = depth[rows, :]
        face[0, rows, :] = jnp.minimum(here, depth[rows_at(g + 1), :])
        face[1, rows, :] = jnp.where(lane == 127, 0.0, jnp.minimum(here, ahead_one(here)))
        total[rows, :] = jnp.zeros((8, 128), F32)

    def level(k, carry):
        threshold = k.astype(F32)
        for g in GROUPS:
            r = g - LOW
            rows = rows_at(g)
            if r < EDGE or r >= WIDE - EDGE:
                ref = low if r < EDGE else high
                q0[0, rows, :] = ref[k]
                q0[1, rows, :] = ref[KL + k]
                flow[0, rows, :] = ref[2 * KL + k]
                flow[1, rows, :] = ref[3 * KL + k]
            else:
                q0[0, rows, :] = tracers[0, k, rows_at(r - EDGE), :]
                q0[1, rows, :] = tracers[1, k, rows_at(r - EDGE), :]
        flow[0, PAD : PAD + SX, :] = east[k].astype(F32)
        flow[1, PAD : PAD + SX, :] = north[k].astype(F32)
        set_weights(
            lambda g: depth[rows_at(g), :],
            lambda g: face[0, rows_at(g), :],
            lambda g: face[1, rows_at(g), :],
            flow,
            coef,
            threshold,
            lambda g, a, b: (back_one(a), back_one(b)),
        )
        for tracer in range(2):
            for g in GROUPS:
                q1[tracer, rows_at(g), :] = update(q0.at[tracer], coef, g)
        for g in GROUPS:
            temperature = update(q1.at[0], coef, g)
            salinity = update(q1.at[1], coef, g)
            if PAD <= g < PAD + SX:
                new[0, k, rows_at(g - PAD), :] = temperature
                new[1, k, rows_at(g - PAD), :] = salinity
            total[rows_at(g), :] += temperature - 0.8 * salinity
        return carry

    lax.fori_loop(0, KL, level, 0)


def block_levels(tracers, east, north, levels, low, high):
    tall = (ROWS, 128)
    return pl.pallas_call(
        levels_kernel,
        out_shape=[jax.ShapeDtypeStruct(tracers.shape, F32), jax.ShapeDtypeStruct(tall, F32)],
        scratch_shapes=[pltpu.VMEM(s + tall, F32) for s in ((), (2,), (2,), (2,), (2,), (5,))],
        compiler_params=params(),
        cost_estimate=pl.CostEstimate(flops=20_000_000, bytes_accessed=6_000_000, transcendentals=0),
        name="block_levels",
    )(tracers, east, north, levels, low, high)


def operator_kernel(
    levels, low, high, own_rows, own_edges, one_in, two_in, blocked, wall_total,
    new, fields, sums,
    depth, strip_q, strip_depth, strip_flow, strip_total, first_q, coef, total, field, grid, staged, sems, *, count,
):
    lane = lanes()
    member = lane % 8
    blank = jnp.zeros((8, 128), F32)
    strip_level = (lane // 8).astype(F32)
    first = lax.axis_index("gy") == 0
    last = lax.axis_index("gy") == count - 1

    def own(which, a, g):
        r = g - LOW
        if r < EDGE:
            return own_edges[which, a, rows_at(0), :]
        if r >= WIDE - EDGE:
            return own_edges[which, a, rows_at(8), :]
        return own_rows[which, a, rows_at(r - EDGE), :]

    halo_depth(levels, low, high, depth)
    for g in GROUPS:
        rows = rows_at(g)
        sent = rows_at(g - LOW)
        from_low = list(split_one(*(one_in[a, sent, :] for a in range(SENT))))
        from_high = list(split_two(*(two_in[a, sent, :] for a in range(SENT))))
        from_low[4] = jnp.where(first, 0.0, from_low[4])
        from_high[4] = jnp.where(last, 0.0, from_high[4])
        for a in range(5):
            low_strip = jnp.where(member < 4, from_low[a], own(0, a, g))
            high_strip = jnp.where(member >= 3, from_high[a], own(1, a, g))
            for side, value in enumerate((low_strip, high_strip)):
                if a < 2:
                    strip_q[side, a, 0, rows, :] = value
                elif a < 4:
                    strip_flow[side, a - 2, rows, :] = value
                else:
                    strip_depth[side, rows, :] = value
    for outside in OUTSIDE:
        for side in range(2):
            strip_depth[side, rows_at(outside), :] = blank

    for side in range(2):
        at = strip_depth.at[side]

        def south(g, a_north, b_north, side=side):
            a_south, b_south = back_one(a_north), back_one(b_north)
            if side == 1:
                face = jnp.minimum(own(0, 4, g), own(1, 4, g))
                a_first, b_first = face_weights(face, own(0, 3, g), strip_level)
                a_south = jnp.where(member == 0, a_first, a_south)
                b_south = jnp.where(member == 0, b_first, b_south)
            return a_south, b_south

        set_weights(
            lambda g, at=at: at[rows_at(g), :],
            lambda g, at=at: jnp.minimum(at[rows_at(g), :], at[rows_at(g + 1), :]),
            lambda g, at=at: jnp.minimum(at[rows_at(g), :], ahead_one(at[rows_at(g), :])),
            strip_flow.at[side],
            coef,
            strip_level,
            south,
        )
        for tracer in range(2):
            source = strip_q.at[side, tracer, 0]
            for g in GROUPS:
                value = None
                if side == 1:
                    value = jnp.where(member == 0, own(0, tracer, g), back_one(source[rows_at(g), :]))
                strip_q[side, tracer, 1, rows_at(g), :] = update(source, coef, g, value)
        for g in GROUPS:
            rows = rows_at(g)
            temperature = update(strip_q.at[side, 0, 1], coef, g)
            salinity = update(strip_q.at[side, 1, 1], coef, g)
            strip_q[side, 0, 0, rows, :] = temperature
            strip_q[side, 1, 0, rows, :] = salinity
            value = temperature - 0.8 * salinity
            for shift in (8, 16, 32, 64):
                value = value + pltpu.roll(value, shift, 1)
            strip_total[side, rows, :] = value

    for tracer in range(2):
        for g in range(PAD, PAD + SX, 8):
            rows = rows_at(g)
            high_value = pltpu.roll(strip_q[1, tracer, 0, rows, :], 1, 1)
            first_q[tracer, rows, :] = jnp.where(member >= 4, strip_q[0, tracer, 0, rows, :], high_value)
    from_strip = (lane < 2) | (lane >= 126)

    def place(k, carry):
        turn = 124 - 8 * k
        for tracer in range(2):
            for g in range(0, SX, 8):
                rows = rows_at(g)
                value = pltpu.roll(first_q[tracer, rows_at(g + PAD), :], turn, 1)
                staged[tracer, k, rows, :] = jnp.where(from_strip, value, blocked[tracer, k, rows, :])
        for tracer in range(2):
            pltpu.make_async_copy(staged.at[tracer, k], new.at[tracer, k], sems.at[0]).start()
        return carry

    lax.fori_loop(0, KL, place, 0)

    def beside(low_value, high_value):
        return jnp.where(lane >= 64, pltpu.roll(low_value, 4, 1), pltpu.roll(high_value, 5, 1))

    def northward(main, side):
        a, b = ahead_one(main), ahead_one(side)
        return jnp.where(lane == 127, b, a), jnp.where(lane == 127, a, b)

    def southward(main, side):
        a, b = back_one(main), back_one(side)
        return jnp.where(lane == 0, b, a), jnp.where(lane == 0, a, b)

    for g in GROUPS + OUTSIDE:
        rows = rows_at(g)
        grid[0, 0, rows, :] = depth[rows, :]
        grid[0, 1, rows, :] = beside(strip_depth[0, rows, :], strip_depth[1, rows, :])
    for g in GROUPS:
        rows = rows_at(g)
        both = grid[0, 0, rows, :], grid[0, 1, rows, :]
        further = northward(*both)
        for part in range(2):
            grid[1, part, rows, :] = jnp.minimum(both[part], grid[0, part, rows_at(g + 1), :])
            grid[2, part, rows, :] = jnp.minimum(both[part], further[part])
        low_total = pltpu.roll(strip_total[0, rows, :], 4, 1)
        high_total = pltpu.roll(strip_total[1, rows, :], 5, 1)
        edge_total = jnp.where(lane < 64, low_total, high_total)
        total[0, rows, :] = jnp.where(from_strip, edge_total, wall_total[rows, :])
        total[1, rows, :] = jnp.where(lane >= 64, low_total, high_total)
    for part in range(2):
        grid[1, part, rows_at(LOW - 8), :] = blank
        for outside in OUTSIDE:
            for i in range(3):
                field[i, part, rows_at(outside), :] = blank
    scale = 1.0 / KL
    for g in GROUPS:
        rows = rows_at(g)
        souths = southward(grid[2, 0, rows, :], grid[2, 1, rows, :])
        for part in range(2):
            here = grid[0, part, rows, :]
            own_part = ALPHA * scale * here + jnp.where(here == 0.0, 1.0, 0.0)
            faces = grid[1, part, rows, :] + grid[1, part, rows_at(g - 1), :] + grid[2, part, rows, :] + souths[part]
            diagonal = own_part + scale * faces
            inverse = 1.0 / diagonal
            grid[3, part, rows, :] = inverse
            grid[4, part, rows, :] = own_part
            grid[5, part, rows, :] = diagonal
            field[0, part, rows, :] = 0.25 * total[part, rows, :] * inverse

    moments = [blank] * 6
    for i in range(3):
        for g in GROUPS:
            rows = rows_at(g)
            both = field[i, 0, rows, :], field[i, 1, rows, :]
            norths = northward(*both)
            souths = southward(*both)
            south_faces = southward(grid[2, 0, rows, :], grid[2, 1, rows, :])
            for part in range(2):
                if i == 2 and part == 1:
                    continue
                here = both[part]
                east_gap = here - field[i, part, rows_at(g + 1), :]
                north_gap = here - norths[part]
                east_face = scale * grid[1, part, rows, :]
                north_face = scale * grid[2, part, rows, :]
                own_part = grid[4, part, rows, :]
                if part == 0 and PAD <= g < PAD + SX:
                    moments[2 * i] += grid[5, 0, rows, :] * here * here
                    moments[2 * i + 1] += (
                        own_part * here * here + east_face * east_gap * east_gap + north_face * north_gap * north_gap
                    )
                if i < 2:
                    image = (
                        own_part * here
                        + east_face * east_gap
                        + scale * grid[1, part, rows_at(g - 1), :] * (here - field[i, part, rows_at(g - 1), :])
                        + north_face * north_gap
                        + scale * south_faces[part] * (here - souths[part])
                    )
                    field[i + 1, part, rows, :] = image * grid[3, part, rows, :]
        pltpu.make_async_copy(field.at[i, 0, PAD : PAD + SX, :], fields.at[i], sems.at[1]).start()
    row = jnp.zeros((8, 128), F32)
    for i in range(6):
        value = jnp.sum(jnp.sum(moments[i], axis=0, keepdims=True), axis=1, keepdims=True)
        row = jnp.where(lane == i, value, row)
    for g in range(0, 128, 8):
        sums[rows_at(g), :] = row
    pltpu.make_async_copy(field.at[:, 0, PAD : PAD + SX, :], fields, sems.at[1]).wait()
    pltpu.make_async_copy(staged, new, sems.at[0]).wait()


def operator(levels, low, high, own_rows, own_edges, one_in, two_in, blocked, wall_total, count):
    tall = (ROWS, 128)
    scratch = (
        (),
        (2, 2, 2),
        (2,),
        (2, 2),
        (2,),
        (2,),
        (5,),
        (2,),
        (3, 2),
        (6, 2),
    )
    return pl.pallas_call(
        functools.partial(operator_kernel, count=count),
        out_shape=[
            jax.ShapeDtypeStruct(blocked.shape, F32),
            jax.ShapeDtypeStruct((3, SX, SY), F32),
            jax.ShapeDtypeStruct((128, 128), F32),
        ],
        out_specs=[
            pl.BlockSpec(memory_space=pltpu.HBM),
            pl.BlockSpec(memory_space=pltpu.HBM),
            pl.BlockSpec(memory_space=pltpu.VMEM),
        ],
        scratch_shapes=[pltpu.VMEM(s + tall, F32) for s in scratch]
        + [pltpu.VMEM(blocked.shape, F32), pltpu.SemaphoreType.DMA((2,))],
        compiler_params=params(),
        name="operator",
    )(levels, low, high, own_rows, own_edges, one_in, two_in, blocked, wall_total)


def finish_kernel(sums, fields, out):
    value = sums[0:8, :]
    for g in range(8, 128, 8):
        value = value + sums[rows_at(g), :]
    value = jnp.sum(value, axis=0, keepdims=True)
    lane = lanes((1, 128))
    m0, m1, m2, m3, m4, m5 = (
        jnp.sum(jnp.where(lane == i, value, 0.0), axis=1, keepdims=True) for i in range(6)
    )
    floor = 4e-7
    l10 = m2 / m1
    l20 = m3 / m1
    d1 = m3 - l10 * m2
    t = m4 - l20 * m2
    has1 = d1 > floor * m3
    l21 = jnp.where(has1, t / d1, 0.0)
    d2 = m5 - l20 * m3 - l21 * t
    has2 = has1 & (d2 > floor * m5)
    y1 = m1 - l10 * m0
    y2 = m2 - l20 * m0 - l21 * y1
    c2 = jnp.where(has2, y2 / d2, 0.0)
    c1 = jnp.where(has1, y1 / d1, 0.0) - l21 * c2
    c0 = m0 / m1 - l10 * c1 - l20 * c2
    for g in range(0, SX, 8):
        rows = rows_at(g)
        out[rows, :] = c0 * fields[0, rows, :] + c1 * fields[1, rows, :] + c2 * fields[2, rows, :]


def finish(sums, fields):
    return pl.pallas_call(
        finish_kernel,
        out_shape=jax.ShapeDtypeStruct((SX, SY), F32),
        name="finish",
    )(sums, fields)


def shift(array, axis, step):
    count = lax.axis_size(axis)
    return lax.ppermute(array, axis, [(i, (i + step) % count) for i in range(count)])


def on_device(tracers, east, north, levels):
    first, final = edges(tracers, east, north, levels)
    high = shift(first, "gx", -1)
    low = shift(final, "gx", 1)
    own_rows, one, two = pack_rows(tracers, east, north, levels)
    own_edges, one, two = pack_edges(low, high, one, two)
    one_in = shift(one, "gy", 1)
    two_in = shift(two, "gy", -1)
    blocked, total = block_levels(tracers, east, north, levels, low, high)
    new, fields, sums = operator(
        levels, low, high, own_rows, own_edges, one_in, two_in, blocked, total, lax.axis_size("gy")
    )
    sums = lax.all_to_all(sums, ("gx", "gy"), split_axis=0, concat_axis=0, tiled=True)
    return new, finish(sums, fields)


def solution(mesh):
    placed = (P(None, None, "gx", "gy"), P(None, "gx", "gy"), P(None, "gx", "gy"), P("gx", "gy"))
    return jax.shard_map(
        on_device,
        mesh=mesh,
        in_specs=placed,
        out_specs=(P(None, None, "gx", "gy"), P("gx", "gy")),
        check_vma=False,
    )
```

time: 62.2 us -> 53 us (0.85)
  waiting for transfers between devices: 10.2 us -> 2.01 us
  local copies, waits for them, and re-layouts: 6.37 us -> 2.28 us
  Pallas kernels: 17.1 us -> 20.1 us
    ppermute x4, waiting for transfers between devices: 10.2 us -> 2.01 us  [shift(): lax.ppermute(array, axis, [(i, (i + step) % count) for i in range(count)])]
    unnamed x16 -> x12, local copies, waits for them, and re-layouts: 6.37 us -> 2.28 us
    pallas_call x4 -> x5, Pallas kernels: 15.4 us -> 18.4 us  [the longest x1 7.86 us: operator(): pl.pallas_call(functools.partial(operator_kernel, count=count), out_shape...]
  transfers between devices with their start and end apart: 4 -> 4, of which waited for: 3 -> 2; matrix products, arithmetic and copies ran while one was open for 0% -> 0% of each run, Pallas kernels for 4% -> 15%
where the time goes in v2:
time: 53 us; the launch traced here: 52.8 us
  Pallas kernels  20.1 us (38%)
  blocking collectives  18.3 us (35%)
  starting transfers between devices  9.35 us (18%)
  local copies, waits for them, and re-layouts  2.28 us (4%)
  waiting for transfers between devices  2.01 us (4%)
  between operations  0.71 us (1%)
    all_to_all x1, blocking collectives, on_device(): lax.all_to_all(sums, ('gx', 'gy'), split_axis=0, concat_axis=0, tiled=True)  18.3 us
    ppermute x4, starting transfers between devices, shift(): lax.ppermute(array, axis, [(i, (i + step) % count) for i in range(count)])  9.35 us
    pallas_call x1, Pallas kernels, operator(): pl.pallas_call(functools.partial(operator_kernel, count=count), out_shape...  7.86 us
    pallas_call x1, Pallas kernels, block_levels(): pl.pallas_call(levels_kernel, out_shape=[jax.ShapeDtypeStruct(tracers.sha...  4.95 us
    pallas_call x1, Pallas kernels, pack_rows(): pl.pallas_call(pack_rows_kernel, out_shape=[jax.ShapeDtypeStruct((2, 5, S...  3.03 us
    unnamed x12, local copies, waits for them, and re-layouts  2.28 us
    pallas_call x1, Pallas kernels, edges(): pl.pallas_call(edges_kernel, in_specs=[pl.BlockSpec(memory_space=pltpu.HB...  2.05 us
    ppermute x4, waiting for transfers between devices, shift(): lax.ppermute(array, axis, [(i, (i + step) % count) for i in range(count)])  2.01 us
  transfers between devices with their start and end apart: 4, of which 2 were waited for; matrix products, arithmetic and copies ran while one was open for 0% of the time, Pallas kernels for 15%

profile of v2, /device:TPU:1, one launch (start us, length us, event | category | flops | bytes accessed | tf_op | source)
XLA Modules:
  0.0 52.8 jit_solution(11033966457560466325)
XLA Ops:
  0.6 0.0 copy-start.4
  0.6 0.0 copy-start.3
  0.7 0.0 copy-start.2
  0.7 2.1 %edges.1 = (f32[65,8,128]{2,1,0:T(8,128)}, f32[65,8,128]{2,1,0:T(8,128)}) custom-call(f32[2,16,128,128]{3,2,1,0:T(8,128)} %tracers.1, bf16[16,128,128]{2,1,0:T(8,128)(2,1)} %east.1, bf16[16,128,128]{2,1,0:T(8,128)(2,1)} %north.1, s32[128,128]{1,0:T(8,128)} %levels.3), custom_call_target="tpu_custom_call" | custom-call | tf_op jit(solution)/shard_map/edges/pallas_call | solution.py:74
  2.7 2.5 %collective-permute-start = (f32[65,8,128]{2,1,0:T(8,128)}, f32[65,8,128]{2,1,0:T(8,128)S(1)}, u32[]{:S(2)}, u32[]{:S(2)}) collective-permute-start(f32[65,8,128]{2,1,0:T(8,128)} %get-tuple-element.15), channel_id=1, source_target_pairs={{0,8},{8,16},{16,24},{24,32},{32,40},{40,48},{48,56},{56,64},{64,7... | collective-permute-start | bytes 798728 | tf_op jit(solution)/shard_map/ppermute | solution.py:562
  5.3 4.4 %collective-permute-start.1 = (f32[65,8,128]{2,1,0:T(8,128)}, f32[65,8,128]{2,1,0:T(8,128)S(1)}, u32[]{:S(2)}, u32[]{:S(2)}) collective-permute-start(f32[65,8,128]{2,1,0:T(8,128)} %get-tuple-element.16), channel_id=1, source_target_pairs={{0,120},{8,0},{16,8},{24,16},{32,24},{40,32},{48,40},{56,48},{64,5... | collective-permute-start | bytes 798728 | tf_op jit(solution)/shard_map/ppermute | solution.py:562
  9.7 0.0 copy-done.4
  9.7 0.0 copy-done.3
  9.7 0.0 copy-done.2
  9.7 0.0 copy-start
  9.7 1.6 %copy-done = f32[2,16,128,128]{3,2,1,0:T(8,128)S(1)} copy-done((f32[2,16,128,128]{3,2,1,0:T(8,128)S(1)}, f32[2,16,128,128]{3,2,1,0:T(8,128)}, u32[]{:S(2)}) %copy-start) | copy-done | bytes 2097176
  11.3 0.0 copy-start.1
  11.3 3.0 %pack_rows.1 = (f32[2,5,128,128]{3,2,1,0:T(8,128)S(1)}, f32[3,128,128]{2,1,0:T(8,128)S(1)}, f32[3,128,128]{2,1,0:T(8,128)S(1)}) custom-call(f32[2,16,128,128]{3,2,1,0:T(8,128)S(1)} %copy-done, bf16[16,128,128]{2,1,0:T(8,128)(2,1)S(1)} %copy-done.2, bf16[16,128,128]{2,1,0:T(8,128)(2,1)S(1)} %copy-done.3, s32[128,128]{1,0:T(8,128)S(1)} %copy-done.4), custom_call_target="tpu_custom_call" | custom-call | tf_op jit(solution)/shard_map/pack_rows/pallas_call | solution.py:161
  14.3 1.6 %collective-permute-done.low = f32[65,8,128]{2,1,0:T(8,128)S(1)} collective-permute-done((f32[65,8,128]{2,1,0:T(8,128)}, f32[65,8,128]{2,1,0:T(8,128)S(1)}, u32[]{:S(2)}, u32[]{:S(2)}) %collective-permute-start) | collective-permute-done | bytes 266272 | tf_op jit(solution)/shard_map/ppermute | solution.py:562
  15.9 0.0 collective-permute-done.1.high
  15.9 0.5 pack_edges.1
  16.4 2.4 %collective-permute-start.2 = (f32[3,144,128]{2,1,0:T(8,128)S(1)}, f32[3,144,128]{2,1,0:T(8,128)S(1)}, u32[]{:S(2)}, u32[]{:S(2)}) collective-permute-start(f32[3,144,128]{2,1,0:T(8,128)S(1)} %get-tuple-element.21), channel_id=1, source_target_pairs={{0,1},{1,2},{2,3},{3,4},{4,5},{5,6},{6,7},{7,0},{8,9},{9,10},{10,1... | collective-permute-start | bytes 663560 | tf_op jit(solution)/shard_map/ppermute | solution.py:562
  18.8 0.0 collective-permute-start.3
  18.8 0.0 copy-done.1
  18.8 4.9 %block_levels.1 = (f32[2,16,128,128]{3,2,1,0:T(8,128)S(1)}, f32[160,128]{1,0:T(8,128)S(1)}) custom-call(f32[2,16,128,128]{3,2,1,0:T(8,128)S(1)} %copy-done.1, bf16[16,128,128]{2,1,0:T(8,128)(2,1)S(1)} %copy-done.2, bf16[16,128,128]{2,1,0:T(8,128)(2,1)S(1)} %copy-done.3, s32[128,128]{1,0:T(8,128)S(1)} %copy-done.4, ...), custom_call_target="tpu_custom_call" | custom-call | flops 20000000 | bytes 6000000 | tf_op jit(solution)/shard_map/block_levels/pallas_call | solution.py:291
  23.8 0.0 collective-permute-done.2.one_in
  23.8 0.4 collective-permute-done.3.two_in
  24.2 7.9 %operator.1 = (f32[2,16,128,128]{3,2,1,0:T(8,128)}, f32[3,128,128]{2,1,0:T(8,128)S(1)}, f32[128,128]{1,0:T(8,128)S(1)}) custom-call(s32[128,128]{1,0:T(8,128)S(1)} %copy-done.4, f32[65,8,128]{2,1,0:T(8,128)S(1)} %collective-permute-done.low, f32[65,8,128]{2,1,0:T(8,128)S(1)} %collective-permute-done.1.high, ...), custom_call_target="tpu_custom_call" | custom-call | tf_op jit(solution)/shard_map/operator/pallas_call | solution.py:505
  32.1 0.0 copy-start.5
  32.1 0.7 %copy-done.5 = f32[3,128,128]{2,1,0:T(8,128)} copy-done((f32[3,128,128]{2,1,0:T(8,128)}, f32[3,128,128]{2,1,0:T(8,128)S(1)}, u32[]{:S(2)}) %copy-start.5) | copy-done | bytes 196632
  32.7 18.3 %all_to_all.11 = f32[128,1,128]{2,1,0:T(1,128)} all-to-all(f32[128,1,128]{2,1,0:T(1,128)S(1)} %bitcast.4), channel_id=1, replica_groups=mesh['gx'=16,'gy'=8] {'gx','gy'}, dimensions={0} | all-to-all | bytes 131072 | tf_op jit(solution)/shard_map/all_to_all | solution.py:577
  51.0 1.7 %finish.1 = f32[128,128]{1,0:T(8,128)} custom-call(f32[128,128]{1,0:T(8,128)} %bitcast.5, f32[3,128,128]{2,1,0:T(8,128)} %copy-done.5), custom_call_target="tpu_custom_call" | custom-call | tf_op jit(solution)/shard_map/finish/pallas_call | solution.py:553
Async XLA Ops:
  0.6 9.0 %copy-start.4 = (s32[128,128]{1,0:T(8,128)S(1)}, s32[128,128]{1,0:T(8,128)}, u32[]{:S(2)}) copy-start(s32[128,128]{1,0:T(8,128)} %levels.3) | copy-start | bytes 196612
  0.6 9.0 %copy-start.3 = (bf16[16,128,128]{2,1,0:T(8,128)(2,1)S(1)}, bf16[16,128,128]{2,1,0:T(8,128)(2,1)}, u32[]{:S(2)}) copy-start(bf16[16,128,128]{2,1,0:T(8,128)(2,1)} %north.1) | copy-start | bytes 1572868
  0.7 9.0 %copy-start.2 = (bf16[16,128,128]{2,1,0:T(8,128)(2,1)S(1)}, bf16[16,128,128]{2,1,0:T(8,128)(2,1)}, u32[]{:S(2)}) copy-start(bf16[16,128,128]{2,1,0:T(8,128)(2,1)} %east.1) | copy-start | bytes 1572868
  2.7 13.2 %collective-permute-start = (f32[65,8,128]{2,1,0:T(8,128)}, f32[65,8,128]{2,1,0:T(8,128)S(1)}, u32[]{:S(2)}, u32[]{:S(2)}) collective-permute-start(f32[65,8,128]{2,1,0:T(8,128)} %get-tuple-element.15), channel_id=1, source_target_pairs={{0,8},{8,16},{16,24},{24,32},{32,40},{40,48},{48,56},{56,64},{64,7... | collective-permute-start | bytes 798728 | tf_op jit(solution)/shard_map/ppermute | solution.py:562
  5.3 10.6 %collective-permute-start.1 = (f32[65,8,128]{2,1,0:T(8,128)}, f32[65,8,128]{2,1,0:T(8,128)S(1)}, u32[]{:S(2)}, u32[]{:S(2)}) collective-permute-start(f32[65,8,128]{2,1,0:T(8,128)} %get-tuple-element.16), channel_id=1, source_target_pairs={{0,120},{8,0},{16,8},{24,16},{32,24},{40,32},{48,40},{56,48},{64,5... | collective-permute-start | bytes 798728 | tf_op jit(solution)/shard_map/ppermute | solution.py:562
  9.7 1.6 %copy-start = (f32[2,16,128,128]{3,2,1,0:T(8,128)S(1)}, f32[2,16,128,128]{3,2,1,0:T(8,128)}, u32[]{:S(2)}) copy-start(f32[2,16,128,128]{3,2,1,0:T(8,128)} %tracers.1) | copy-start | bytes 6291460
  11.3 7.6 %copy-start.1 = (f32[2,16,128,128]{3,2,1,0:T(8,128)S(1)}, f32[2,16,128,128]{3,2,1,0:T(8,128)}, u32[]{:S(2)}) copy-start(f32[2,16,128,128]{3,2,1,0:T(8,128)} %tracers.1) | copy-start | bytes 6291460
  16.4 7.4 %collective-permute-start.2 = (f32[3,144,128]{2,1,0:T(8,128)S(1)}, f32[3,144,128]{2,1,0:T(8,128)S(1)}, u32[]{:S(2)}, u32[]{:S(2)}) collective-permute-start(f32[3,144,128]{2,1,0:T(8,128)S(1)} %get-tuple-element.21), channel_id=1, source_target_pairs={{0,1},{1,2},{2,3},{3,4},{4,5},{5,6},{6,7},{7,0},{8,9},{9,10},{10,1... | collective-permute-start | bytes 663560 | tf_op jit(solution)/shard_map/ppermute | solution.py:562
  18.8 5.4 %collective-permute-start.3 = (f32[3,144,128]{2,1,0:T(8,128)S(1)}, f32[3,144,128]{2,1,0:T(8,128)S(1)}, u32[]{:S(2)}, u32[]{:S(2)}) collective-permute-start(f32[3,144,128]{2,1,0:T(8,128)S(1)} %get-tuple-element.22), channel_id=1, source_target_pairs={{0,7},{1,0},{2,1},{3,2},{4,3},{5,4},{6,5},{7,6},{8,15},{9,8},{10,9... | collective-permute-start | bytes 663560 | tf_op jit(solution)/shard_map/ppermute | solution.py:562
  32.1 0.7 %copy-start.5 = (f32[3,128,128]{2,1,0:T(8,128)}, f32[3,128,128]{2,1,0:T(8,128)S(1)}, u32[]{:S(2)}) copy-start(f32[3,128,128]{2,1,0:T(8,128)S(1)} %get-tuple-element.27.fields) | copy-start | bytes 589828

commit v3 on v2

--- a/solution.py
+++ b/solution.py
@@ -23,7 +23,9 @@
 VMEM = 40 * 1024 * 1024
 GROUPS = tuple(range(LOW, LOW + WIDE, 8))
 OUTSIDE = (LOW - 8, LOW + WIDE)
+BATCHES = (GROUPS[:6], GROUPS[6:12], GROUPS[12:])
 SENT = 3
+FIELDS = 480
 
 
 def params(limit=VMEM):
@@ -46,13 +48,28 @@
     return pltpu.roll(value, 1, 1)
 
 
-def edges_kernel(t, e, n, d, out_lo, out_hi, flows, depths, sems):
+def offsets(counts):
+    starts, at = [], 8
+    for a in range(4):
+        starts.append(at)
+        at += KL * counts[a]
+    return starts, at
+
+
+NEXT = (4, 4, 4, 4)
+BEFORE = (5, 5, 4, 4)
+NEXT_AT, NEXT_ROWS = offsets(NEXT)
+BEFORE_AT, BEFORE_ROWS = offsets(BEFORE)
+BEFORE_ROWS += 8
+
+
+def edges_kernel(t, e, n, d, before, after, tiles, flows, depths, sems):
     copies = []
-    for side, (out, at) in enumerate(((out_lo, 0), (out_hi, SX - 8))):
+    for side, at in enumerate((0, SX - 8)):
         at16 = 0 if side == 0 else SX - 16
         copies += [
-            (t.at[0, :, at : at + 8, :], out.at[0:KL]),
-            (t.at[1, :, at : at + 8, :], out.at[KL : 2 * KL]),
+            (t.at[0, :, at : at + 8, :], tiles.at[side, 0]),
+            (t.at[1, :, at : at + 8, :], tiles.at[side, 1]),
             (e.at[:, at16 : at16 + 16, :], flows.at[side, 0]),
             (n.at[:, at16 : at16 + 16, :], flows.at[side, 1]),
             (d.at[at : at + 8, :], depths.at[side]),
@@ -60,22 +77,26 @@
     copies = [pltpu.make_async_copy(src, dst, sems.at[i]) for i, (src, dst) in enumerate(copies)]
     for copy in copies:
         copy.start()
-    for side, out in enumerate((out_lo, out_hi)):
+    for side, (out, starts, counts) in enumerate(((before, BEFORE_AT, BEFORE), (after, NEXT_AT, NEXT))):
         for i in range(5):
             copies[5 * side + i].wait()
-        for f in range(2):
+        out[0:8, :] = depths[side].astype(F32)
+        for a in range(4):
             for k in range(KL):
-                out[(2 + f) * KL + k] = flows[side, f, k].astype(F32)[8 * side : 8 * side + 8]
-        out[4 * KL] = depths[side].astype(F32)
+                value = tiles[side, a, k] if a < 2 else flows[side, a - 2, k].astype(F32)[8 * side : 8 * side + 8]
+                from_row = 0 if side == 0 else 8 - counts[a]
+                at = starts[a] + counts[a] * k
+                out[at : at + counts[a], :] = value[from_row : from_row + counts[a]]
+    before[BEFORE_ROWS - 8 : BEFORE_ROWS, :] = jnp.zeros((8, 128), F32)
 
 
 def edges(tracers, east, north, levels):
-    out = jax.ShapeDtypeStruct((ARRAYS, 8, SY), F32)
     return pl.pallas_call(
         edges_kernel,
         in_specs=[pl.BlockSpec(memory_space=pltpu.HBM)] * 4,
-        out_shape=[out, out],
+        out_shape=[jax.ShapeDtypeStruct((rows, SY), F32) for rows in (BEFORE_ROWS, NEXT_ROWS)],
         scratch_shapes=[
+            pltpu.VMEM((2, 2, KL, 8, SY), F32),
             pltpu.VMEM((2, 2, KL, 16, SY), jnp.bfloat16),
             pltpu.VMEM((2, 8, SY), jnp.int32),
             pltpu.SemaphoreType.DMA((10,)),
@@ -83,6 +104,20 @@
         compiler_params=params(62 * 1024 * 1024),
         name="edges",
     )(tracers, east, north, levels)
+
+
+def low_tile(ref, a, k):
+    if a == 4:
+        return ref[0:8, :]
+    at = NEXT_AT[a] + NEXT[a] * (k + 1) - 8
+    return ref[at : at + 8, :]
+
+
+def high_tile(ref, a, k):
+    if a == 4:
+        return ref[0:8, :]
+    at = BEFORE_AT[a] + BEFORE[a] * k
+    return ref[at : at + 8, :]
 
 
 def pack(source, rows):
@@ -166,22 +201,26 @@
     )(tracers, east, north, levels)
 
 
-def pack_edges_kernel(low, high, one_rows, two_rows, own, one, two):
+def pack_edges_kernel(low_in, high_in, one_rows, two_rows, own, one, two, low, high):
+    for a in range(5):
+        for k in range(KL if a < 4 else 1):
+            low[KL * a + k] = low_tile(low_in, a, k)
+            high[KL * a + k] = high_tile(high_in, a, k)
     for g in range(0, SX, 8):
         for a in range(SENT):
             one[a, rows_at(g + EDGE), :] = one_rows[a, rows_at(g), :]
             two[a, rows_at(g + EDGE), :] = two_rows[a, rows_at(g), :]
-    for ref, own_at, at in ((low, 0, 0), (high, 8, WIDE - EDGE)):
-        sources = [(lambda k, a=a, ref=ref: ref[KL * a + k]) for a in range(4)]
-        sources.append(lambda k, ref=ref: ref[4 * KL])
+    for ref, tile, own_at, at in ((low_in, low_tile, 0, 0), (high_in, high_tile, 8, WIDE - EDGE)):
+        sources = [functools.partial(tile, ref, a) for a in range(5)]
         pack_all(sources, 8, own, rows_at(own_at), one, two, rows_at(at))
 
 
 def pack_edges(low, high, one, two):
     sent = jax.ShapeDtypeStruct((SENT, WIDE, 128), F32)
+    halo = jax.ShapeDtypeStruct((ARRAYS, EDGE, SY), F32)
     return pl.pallas_call(
         pack_edges_kernel,
-        out_shape=[jax.ShapeDtypeStruct((2, 5, 2 * EDGE, 128), F32), sent, sent],
+        out_shape=[jax.ShapeDtypeStruct((2, 5, 2 * EDGE, 128), F32), sent, sent, halo, halo],
         compiler_params=params(),
         name="pack_edges",
     )(low, high, one, two)
@@ -196,30 +235,40 @@
 
 def set_weights(depth_at, face_east, face_north, flow, coef, threshold, south):
     coef[1, rows_at(LOW - 8), :] = jnp.zeros((8, 128), F32)
-    for g in GROUPS:
+    for batch in BATCHES:
+        a_north, b_north = {}, {}
+        for g in batch:
+            rows = rows_at(g)
+            a_east, b_east = face_weights(face_east(g), flow[0, rows, :], threshold)
+            a_north[g], b_north[g] = face_weights(face_north(g), flow[1, rows, :], threshold)
+            coef[0, rows, :] = a_east
+            coef[1, rows, :] = b_east
+            coef[2, rows, :] = b_north[g]
+        a_south = {g: back_one(a_north[g]) for g in batch}
+        b_south = {g: back_one(b_north[g]) for g in batch}
+        for g in batch:
+            rows = rows_at(g)
+            a_here, b_here = south(g, a_south[g], b_south[g])
+            coef[3, rows, :] = a_here
+            leaving = coef[0, rows, :] + a_north[g] + coef[1, rows_at(g - 1), :] + b_here
+            coef[4, rows, :] = jnp.where(depth_at(g) > threshold, 1.0 - leaving, 0.0)
+
+
+def update(source, coef, batch, south_value=None):
+    ahead = {g: ahead_one(source[rows_at(g), :]) for g in batch}
+    back = {g: back_one(source[rows_at(g), :]) for g in batch}
+    result = {}
+    for g in batch:
         rows = rows_at(g)
-        a_east, b_east = face_weights(face_east(g), flow[0, rows, :], threshold)
-        a_north, b_north = face_weights(face_north(g), flow[1, rows, :], threshold)
-        coef[0, rows, :] = a_east
-        coef[1, rows, :] = b_east
-        coef[2, rows, :] = b_north
-        a_south, b_south = south(g, a_north, b_north)
-        coef[3, rows, :] = a_south
-        leaving = a_east + a_north + coef[1, rows_at(g - 1), :] + b_south
-        coef[4, rows, :] = jnp.where(depth_at(g) > threshold, 1.0 - leaving, 0.0)
-
-
-def update(source, coef, g, south_value=None):
-    rows = rows_at(g)
-    value = source[rows, :]
-    south = back_one(value) if south_value is None else south_value
-    return (
-        coef[4, rows, :] * value
-        + coef[1, rows, :] * source[rows_at(g + 1), :]
-        + coef[0, rows_at(g - 1), :] * source[rows_at(g - 1), :]
-        + coef[2, rows, :] * ahead_one(value)
-        + coef[3, rows, :] * south
-    )
+        south = back[g] if south_value is None else south_value(g, back[g])
+        result[g] = (
+            coef[4, rows, :] * source[rows, :]
+            + coef[1, rows, :] * source[rows_at(g + 1), :]
+            + coef[0, rows_at(g - 1), :] * source[rows_at(g - 1), :]
+            + coef[2, rows, :] * ahead[g]
+            + coef[3, rows, :] * south
+        )
+    return result
 
 
 def halo_depth(levels, low, high, depth):
@@ -269,18 +318,20 @@
             flow,
             coef,
             threshold,
-            lambda g, a, b: (back_one(a), back_one(b)),
+            lambda g, a, b: (a, b),
         )
         for tracer in range(2):
-            for g in GROUPS:
-                q1[tracer, rows_at(g), :] = update(q0.at[tracer], coef, g)
-        for g in GROUPS:
-            temperature = update(q1.at[0], coef, g)
-            salinity = update(q1.at[1], coef, g)
-            if PAD <= g < PAD + SX:
-                new[0, k, rows_at(g - PAD), :] = temperature
-                new[1, k, rows_at(g - PAD), :] = salinity
-            total[rows_at(g), :] += temperature - 0.8 * salinity
+            for batch in BATCHES:
+                for g, value in update(q0.at[tracer], coef, batch).items():
+                    q1[tracer, rows_at(g), :] = value
+        for batch in BATCHES:
+            temperature = update(q1.at[0], coef, batch)
+            salinity = update(q1.at[1], coef, batch)
+            for g in batch:
+                if PAD <= g < PAD + SX:
+                    new[0, k, rows_at(g - PAD), :] = temperature[g]
+                    new[1, k, rows_at(g - PAD), :] = salinity[g]
+                total[rows_at(g), :] += temperature[g] - 0.8 * salinity[g]
         return carry
 
     lax.fori_loop(0, KL, level, 0)
@@ -301,7 +352,7 @@
 def operator_kernel(
     levels, low, high, own_rows, own_edges, one_in, two_in, blocked, wall_total,
     new, fields, sums,
-    depth, strip_q, strip_depth, strip_flow, strip_total, first_q, coef, total, field, grid, staged, sems, *, count,
+    depth, strip_q, strip_depth, strip_face, strip_flow, strip_total, first_q, coef, total, field, grid, staged, sems, *, count,
 ):
     lane = lanes()
     member = lane % 8
@@ -319,11 +370,16 @@
         return own_rows[which, a, rows_at(r - EDGE), :]
 
     halo_depth(levels, low, high, depth)
+    parts = {}
+    for g in GROUPS:
+        sent = rows_at(g - LOW)
+        parts[g] = (
+            list(split_one(*(one_in[a, sent, :] for a in range(SENT)))),
+            list(split_two(*(two_in[a, sent, :] for a in range(SENT)))),
+        )
     for g in GROUPS:
         rows = rows_at(g)
-        sent = rows_at(g - LOW)
-        from_low = list(split_one(*(one_in[a, sent, :] for a in range(SENT))))
-        from_high = list(split_two(*(two_in[a, sent, :] for a in range(SENT))))
+        from_low, from_high = parts[g]
         from_low[4] = jnp.where(first, 0.0, from_low[4])
         from_high[4] = jnp.where(last, 0.0, from_high[4])
         for a in range(5):
@@ -340,11 +396,16 @@
         for side in range(2):
             strip_depth[side, rows_at(outside), :] = blank
 
+    ahead = {
+        (side, g): ahead_one(strip_depth[side, rows_at(g), :]) for side in range(2) for g in GROUPS
+    }
+    for (side, g), value in ahead.items():
+        strip_face[side, rows_at(g), :] = jnp.minimum(strip_depth[side, rows_at(g), :], value)
+
     for side in range(2):
         at = strip_depth.at[side]
 
-        def south(g, a_north, b_north, side=side):
-            a_south, b_south = back_one(a_north), back_one(b_north)
+        def south(g, a_south, b_south, side=side):
             if side == 1:
                 face = jnp.minimum(own(0, 4, g), own(1, 4, g))
                 a_first, b_first = face_weights(face, own(0, 3, g), strip_level)
@@ -355,7 +416,7 @@
         set_weights(
             lambda g, at=at: at[rows_at(g), :],
             lambda g, at=at: jnp.minimum(at[rows_at(g), :], at[rows_at(g + 1), :]),
-            lambda g, at=at: jnp.minimum(at[rows_at(g), :], ahead_one(at[rows_at(g), :])),
+            lambda g, side=side: strip_face[side, rows_at(g), :],
             strip_flow.at[side],
             coef,
             strip_level,
@@ -363,21 +424,31 @@
         )
         for tracer in range(2):
             source = strip_q.at[side, tracer, 0]
+            from_own = None
+            if side == 1:
+
+                def from_own(g, value, tracer=tracer):
+                    return jnp.where(member == 0, own(0, tracer, g), value)
+
+            for batch in BATCHES:
+                for g, value in update(source, coef, batch, from_own).items():
+                    strip_q[side, tracer, 1, rows_at(g), :] = value
+        for batch in BATCHES:
+            temperature = update(strip_q.at[side, 0, 1], coef, batch)
+            salinity = update(strip_q.at[side, 1, 1], coef, batch)
+            for g in batch:
+                rows = rows_at(g)
+                strip_q[side, 0, 0, rows, :] = temperature[g]
+                strip_q[side, 1, 0, rows, :] = salinity[g]
+                strip_total[side, rows, :] = temperature[g] - 0.8 * salinity[g]
+    for turn in (8, 16, 32, 64):
+        values = {}
+        for side in range(2):
             for g in GROUPS:
-                value = None
-                if side == 1:
-                    value = jnp.where(member == 0, own(0, tracer, g), back_one(source[rows_at(g), :]))
-                strip_q[side, tracer, 1, rows_at(g), :] = update(source, coef, g, value)
-        for g in GROUPS:
-            rows = rows_at(g)
-            temperature = update(strip_q.at[side, 0, 1], coef, g)
-            salinity = update(strip_q.at[side, 1, 1], coef, g)
-            strip_q[side, 0, 0, rows, :] = temperature
-            strip_q[side, 1, 0, rows, :] = salinity
-            value = temperature - 0.8 * salinity
-            for shift in (8, 16, 32, 64):
-                value = value + pltpu.roll(value, shift, 1)
-            strip_total[side, rows, :] = value
+                value = strip_total[side, rows_at(g), :]
+                values[side, g] = value + pltpu.roll(value, turn, 1)
+        for (side, g), value in values.items():
+            strip_total[side, rows_at(g), :] = value
 
     for tracer in range(2):
         for g in range(PAD, PAD + SX, 8):
@@ -389,9 +460,9 @@
     def place(k, carry):
         turn = 124 - 8 * k
         for tracer in range(2):
-            for g in range(0, SX, 8):
+            values = {g: pltpu.roll(first_q[tracer, rows_at(g + PAD), :], turn, 1) for g in range(0, SX, 8)}
+            for g, value in values.items():
                 rows = rows_at(g)
-                value = pltpu.roll(first_q[tracer, rows_at(g + PAD), :], turn, 1)
                 staged[tracer, k, rows, :] = jnp.where(from_strip, value, blocked[tracer, k, rows, :])
         for tracer in range(2):
             pltpu.make_async_copy(staged.at[tracer, k], new.at[tracer, k], sems.at[0]).start()
@@ -484,7 +555,7 @@
         row = jnp.where(lane == i, value, row)
     for g in range(0, 128, 8):
         sums[rows_at(g), :] = row
-    pltpu.make_async_copy(field.at[:, 0, PAD : PAD + SX, :], fields, sems.at[1]).wait()
+    pltpu.make_async_copy(field.at[:, 0, PAD : PAD + SX, :], fields.at[0:3], sems.at[1]).wait()
     pltpu.make_async_copy(staged, new, sems.at[0]).wait()
 
 
@@ -493,6 +564,7 @@
     scratch = (
         (),
         (2, 2, 2),
+        (2,),
         (2,),
         (2, 2),
         (2,),
@@ -506,7 +578,7 @@
         functools.partial(operator_kernel, count=count),
         out_shape=[
             jax.ShapeDtypeStruct(blocked.shape, F32),
-            jax.ShapeDtypeStruct((3, SX, SY), F32),
+            jax.ShapeDtypeStruct((FIELDS, SX, SY), F32),
             jax.ShapeDtypeStruct((128, 128), F32),
         ],
         out_specs=[
@@ -521,7 +593,9 @@
     )(levels, low, high, own_rows, own_edges, one_in, two_in, blocked, wall_total)
 
 
-def finish_kernel(sums, fields, out):
+def finish_kernel(sums, fields_in, out, fields, sem):
+    copy = pltpu.make_async_copy(fields_in.at[0:3], fields, sem)
+    copy.start()
     value = sums[0:8, :]
     for g in range(8, 128, 8):
         value = value + sums[rows_at(g), :]
@@ -544,6 +618,7 @@
     c2 = jnp.where(has2, y2 / d2, 0.0)
     c1 = jnp.where(has1, y1 / d1, 0.0) - l21 * c2
     c0 = m0 / m1 - l10 * c1 - l20 * c2
+    copy.wait()
     for g in range(0, SX, 8):
         rows = rows_at(g)
         out[rows, :] = c0 * fields[0, rows, :] + c1 * fields[1, rows, :] + c2 * fields[2, rows, :]
@@ -552,7 +627,9 @@
 def finish(sums, fields):
     return pl.pallas_call(
         finish_kernel,
+        in_specs=[pl.BlockSpec(memory_space=pltpu.VMEM), pl.BlockSpec(memory_space=pltpu.HBM)],
         out_shape=jax.ShapeDtypeStruct((SX, SY), F32),
+        scratch_shapes=[pltpu.VMEM((3, SX, SY), F32), pltpu.SemaphoreType.DMA(())],
         name="finish",
     )(sums, fields)
 
@@ -563,11 +640,11 @@
 
 
 def on_device(tracers, east, north, levels):
-    first, final = edges(tracers, east, north, levels)
-    high = shift(first, "gx", -1)
-    low = shift(final, "gx", 1)
+    before, after = edges(tracers, east, north, levels)
+    before = shift(before, "gx", -1)
+    after = shift(after, "gx", 1)
     own_rows, one, two = pack_rows(tracers, east, north, levels)
-    own_edges, one, two = pack_edges(low, high, one, two)
+    own_edges, one, two, low, high = pack_edges(after, before, one, two)
     one_in = shift(one, "gy", 1)
     two_in = shift(two, "gy", -1)
     blocked, total = block_levels(tracers, east, north, levels, low, high)

time: 53 us -> 47.2 us (0.89)
  blocking collectives: 18.3 us -> 14.5 us
  Pallas kernels: 20.1 us -> 16.7 us
  waiting for transfers between devices: 2.01 us -> 3.18 us
  starting transfers between devices: 9.35 us -> 10.2 us
  local copies, waits for them, and re-layouts: 2.28 us -> 1.6 us
    pallas_call x1, Pallas kernels: 7.86 us -> 3.89 us  [operator(): pl.pallas_call(functools.partial(operator_kernel, count=count), out_shape...]
    all_to_all x1, blocking collectives: 18.3 us -> 14.5 us  [on_device(): lax.all_to_all(sums, ('gx', 'gy'), split_axis=0, concat_axis=0, tiled=True)]
    ppermute x4, waiting for transfers between devices: 2.01 us -> 3.18 us  [shift(): lax.ppermute(array, axis, [(i, (i + step) % count) for i in range(count)])]
    ppermute x4, starting transfers between devices: 9.35 us -> 10.2 us  [shift(): lax.ppermute(array, axis, [(i, (i + step) % count) for i in range(count)])]
    pallas_call x1, Pallas kernels: 1.73 us -> 2.42 us  [finish(): pl.pallas_call(finish_kernel, in_specs=[pl.BlockSpec(memory_space=pltpu.V...]
    unnamed x12 -> x10, local copies, waits for them, and re-layouts: 2.28 us -> 1.6 us
  transfers between devices with their start and end apart: 4 -> 4, of which waited for: 2 -> 2; matrix products, arithmetic and copies ran while one was open for 0% -> 0% of each run, Pallas kernels for 15% -> 17%
where the time goes in v3:
time: 47.2 us; the launch traced here: 46.9 us
  Pallas kernels  16.7 us (35%)
  blocking collectives  14.5 us (31%)
  starting transfers between devices  10.2 us (22%)
  waiting for transfers between devices  3.18 us (7%)
  local copies, waits for them, and re-layouts  1.6 us (3%)
  between operations  0.71 us (2%)
    all_to_all x1, blocking collectives, on_device(): lax.all_to_all(sums, ('gx', 'gy'), split_axis=0, concat_axis=0, tiled=True)  14.5 us
    ppermute x4, starting transfers between devices, shift(): lax.ppermute(array, axis, [(i, (i + step) % count) for i in range(count)])  10.2 us
    pallas_call x1, Pallas kernels, block_levels(): pl.pallas_call(levels_kernel, out_shape=[jax.ShapeDtypeStruct(tracers.sha...  4.91 us
    pallas_call x1, Pallas kernels, operator(): pl.pallas_call(functools.partial(operator_kernel, count=count), out_shape...  3.89 us
    ppermute x4, waiting for transfers between devices, shift(): lax.ppermute(array, axis, [(i, (i + step) % count) for i in range(count)])  3.18 us
    pallas_call x1, Pallas kernels, pack_rows(): pl.pallas_call(pack_rows_kernel, out_shape=[jax.ShapeDtypeStruct((2, 5, S...  3.03 us
    pallas_call x1, Pallas kernels, finish(): pl.pallas_call(finish_kernel, in_specs=[pl.BlockSpec(memory_space=pltpu.V...  2.42 us
    pallas_call x1, Pallas kernels, edges(): pl.pallas_call(edges_kernel, in_specs=[pl.BlockSpec(memory_space=pltpu.HB...  1.96 us
  transfers between devices with their start and end apart: 4, of which 2 were waited for; matrix products, arithmetic and copies ran while one was open for 0% of the time, Pallas kernels for 17%

profile of v3, /device:TPU:1, one launch (start us, length us, event | category | flops | bytes accessed | tf_op | source)
XLA Modules:
  0.0 46.9 jit_solution(7095373365770528961)
XLA Ops:
  0.6 0.0 copy-start.4
  0.6 0.0 copy-start.3
  0.7 0.0 copy-start.2
  0.7 2.0 %edges.1 = (f32[304,128]{1,0:T(8,128)}, f32[264,128]{1,0:T(8,128)}) custom-call(f32[2,16,128,128]{3,2,1,0:T(8,128)} %tracers.1, bf16[16,128,128]{2,1,0:T(8,128)(2,1)} %east.1, bf16[16,128,128]{2,1,0:T(8,128)(2,1)} %north.1, s32[128,128]{1,0:T(8,128)} %levels.3), custom_call_target="tpu_custom_call" | custom-call | tf_op jit(solution)/shard_map/edges/pallas_call | solution.py:94
  2.6 6.8 %collective-permute-start.1 = (f32[304,128]{1,0:T(8,128)}, f32[304,128]{1,0:T(8,128)S(1)}, u32[]{:S(2)}, u32[]{:S(2)}) collective-permute-start(f32[304,128]{1,0:T(8,128)} %get-tuple-element.18), channel_id=1, source_target_pairs={{0,120},{8,0},{16,8},{24,16},{32,24},{40,32},{48,40},{56,48},{64,5... | collective-permute-start | bytes 466952 | tf_op jit(solution)/shard_map/ppermute | solution.py:639
  9.5 0.0 collective-permute-start
  9.5 0.0 copy-done.4
  9.5 0.0 copy-done.3
  9.5 0.0 copy-done.2
  9.5 0.0 copy-start
  9.5 1.6 %copy-done = f32[2,16,128,128]{3,2,1,0:T(8,128)S(1)} copy-done((f32[2,16,128,128]{3,2,1,0:T(8,128)S(1)}, f32[2,16,128,128]{3,2,1,0:T(8,128)}, u32[]{:S(2)}) %copy-start) | copy-done | bytes 2097176
  11.1 0.0 copy-start.1
  11.1 3.0 %pack_rows.1 = (f32[2,5,128,128]{3,2,1,0:T(8,128)S(1)}, f32[3,128,128]{2,1,0:T(8,128)S(1)}, f32[3,128,128]{2,1,0:T(8,128)S(1)}) custom-call(f32[2,16,128,128]{3,2,1,0:T(8,128)S(1)} %copy-done, bf16[16,128,128]{2,1,0:T(8,128)(2,1)S(1)} %copy-done.2, bf16[16,128,128]{2,1,0:T(8,128)(2,1)S(1)} %copy-done.3, s32[128,128]{1,0:T(8,128)S(1)} %copy-done.4), custom_call_target="tpu_custom_call" | custom-call | tf_op jit(solution)/shard_map/pack_rows/pallas_call | solution.py:196
  14.1 2.7 %collective-permute-done.low_in = f32[264,128]{1,0:T(8,128)S(1)} collective-permute-done((f32[264,128]{1,0:T(8,128)}, f32[264,128]{1,0:T(8,128)S(1)}, u32[]{:S(2)}, u32[]{:S(2)}) %collective-permute-start) | collective-permute-done | bytes 135200 | tf_op jit(solution)/shard_map/ppermute | solution.py:639
  16.9 0.0 collective-permute-done.1.high_in
  16.9 0.5 %pack_edges.1 = (f32[2,5,16,128]{3,2,1,0:T(8,128)S(1)}, f32[3,144,128]{2,1,0:T(8,128)S(1)}, f32[3,144,128]{2,1,0:T(8,128)S(1)}, f32[65,8,128]{2,1,0:T(8,128)S(1)}, f32[65,8,128]{2,1,0:T(8,128)S(1)}) custom-call(f32[264,128]{1,0:T(8,128)S(1)} %collective-permute-done.low_in, f32[304,128]{1,0:T(8,128)S(1)} %collective-permute-done.1.high_in, ...), custom_call_target="tpu_custom_call" | custom-call | tf_op jit(solution)/shard_map/pack_edges/pallas_call | solution.py:221
  17.4 3.3 %collective-permute-start.2 = (f32[3,144,128]{2,1,0:T(8,128)S(1)}, f32[3,144,128]{2,1,0:T(8,128)S(1)}, u32[]{:S(2)}, u32[]{:S(2)}) collective-permute-start(f32[3,144,128]{2,1,0:T(8,128)S(1)} %get-tuple-element.25), channel_id=1, source_target_pairs={{0,1},{1,2},{2,3},{3,4},{4,5},{5,6},{6,7},{7,0},{8,9},{9,10},{10,1... | collective-permute-start | bytes 663560 | tf_op jit(solution)/shard_map/ppermute | solution.py:639
  20.7 0.0 collective-permute-start.3
  20.7 0.0 copy-done.1
  20.7 4.9 %block_levels.1 = (f32[2,16,128,128]{3,2,1,0:T(8,128)S(1)}, f32[160,128]{1,0:T(8,128)S(1)}) custom-call(f32[2,16,128,128]{3,2,1,0:T(8,128)S(1)} %copy-done.1, bf16[16,128,128]{2,1,0:T(8,128)(2,1)S(1)} %copy-done.2, bf16[16,128,128]{2,1,0:T(8,128)(2,1)S(1)} %copy-done.3, s32[128,128]{1,0:T(8,128)S(1)} %copy-done.4, f32[65,8,128]{2,1,0:T(8,128)S(1)} %get-tuple-element.21.low, ...), custom_call_target="tpu_custom_call" | custom-call | flops 20000000 | bytes 6000000 | tf_op jit(solution)/shard_map/block_levels/pallas_call | solution.py:342
  25.6 0.0 collective-permute-done.2.one_in
  25.7 0.4 collective-permute-done.3.two_in
  26.1 3.9 %operator.1 = (f32[2,16,128,128]{3,2,1,0:T(8,128)}, f32[480,128,128]{2,1,0:T(8,128)}, f32[128,128]{1,0:T(8,128)S(1)}) custom-call(s32[128,128]{1,0:T(8,128)S(1)} %copy-done.4, f32[65,8,128]{2,1,0:T(8,128)S(1)} %get-tuple-element.21.low, f32[65,8,128]{2,1,0:T(8,128)S(1)} %get-tuple-element.22.high, f32[2,5,128,128]{3,2,1,0:T(8,128)S(1)} %get-tuple-element.23.own_rows, ...), custom_call_target="tpu_custom_call" | custom-call | tf_op jit(solution)/shard_map/operator/pallas_call | solution.py:577
  30.0 14.5 %all_to_all.11 = f32[128,1,128]{2,1,0:T(1,128)} all-to-all(f32[128,1,128]{2,1,0:T(1,128)S(1)} %bitcast.4), channel_id=1, replica_groups=mesh['gx'=16,'gy'=8] {'gx','gy'}, dimensions={0} | all-to-all | bytes 131072 | tf_op jit(solution)/shard_map/all_to_all | solution.py:654
  44.5 2.4 %finish.1 = f32[128,128]{1,0:T(8,128)} custom-call(f32[128,128]{1,0:T(8,128)} %bitcast.5, f32[480,128,128]{2,1,0:T(8,128)} %get-tuple-element.31.fields_in), custom_call_target="tpu_custom_call" | custom-call | tf_op jit(solution)/shard_map/finish/pallas_call | solution.py:628
Async XLA Ops:
  0.6 8.9 %copy-start.4 = (s32[128,128]{1,0:T(8,128)S(1)}, s32[128,128]{1,0:T(8,128)}, u32[]{:S(2)}) copy-start(s32[128,128]{1,0:T(8,128)} %levels.3) | copy-start | bytes 196612
  0.6 8.9 %copy-start.3 = (bf16[16,128,128]{2,1,0:T(8,128)(2,1)S(1)}, bf16[16,128,128]{2,1,0:T(8,128)(2,1)}, u32[]{:S(2)}) copy-start(bf16[16,128,128]{2,1,0:T(8,128)(2,1)} %north.1) | copy-start | bytes 1572868
  0.7 8.8 %copy-start.2 = (bf16[16,128,128]{2,1,0:T(8,128)(2,1)S(1)}, bf16[16,128,128]{2,1,0:T(8,128)(2,1)}, u32[]{:S(2)}) copy-start(bf16[16,128,128]{2,1,0:T(8,128)(2,1)} %east.1) | copy-start | bytes 1572868
  2.6 14.2 %collective-permute-start.1 = (f32[304,128]{1,0:T(8,128)}, f32[304,128]{1,0:T(8,128)S(1)}, u32[]{:S(2)}, u32[]{:S(2)}) collective-permute-start(f32[304,128]{1,0:T(8,128)} %get-tuple-element.18), channel_id=1, source_target_pairs={{0,120},{8,0},{16,8},{24,16},{32,24},{40,32},{48,40},{56,48},{64,5... | collective-permute-start | bytes 466952 | tf_op jit(solution)/shard_map/ppermute | solution.py:639
  9.5 7.4 %collective-permute-start = (f32[264,128]{1,0:T(8,128)}, f32[264,128]{1,0:T(8,128)S(1)}, u32[]{:S(2)}, u32[]{:S(2)}) collective-permute-start(f32[264,128]{1,0:T(8,128)} %get-tuple-element.17), channel_id=1, source_target_pairs={{0,8},{8,16},{16,24},{24,32},{32,40},{40,48},{48,56},{56,64},{64,7... | collective-permute-start | bytes 405512 | tf_op jit(solution)/shard_map/ppermute | solution.py:639
  9.5 1.6 %copy-start = (f32[2,16,128,128]{3,2,1,0:T(8,128)S(1)}, f32[2,16,128,128]{3,2,1,0:T(8,128)}, u32[]{:S(2)}) copy-start(f32[2,16,128,128]{3,2,1,0:T(8,128)} %tracers.1) | copy-start | bytes 6291460
  11.1 9.6 %copy-start.1 = (f32[2,16,128,128]{3,2,1,0:T(8,128)S(1)}, f32[2,16,128,128]{3,2,1,0:T(8,128)}, u32[]{:S(2)}) copy-start(f32[2,16,128,128]{3,2,1,0:T(8,128)} %tracers.1) | copy-start | bytes 6291460
  17.4 8.2 %collective-permute-start.2 = (f32[3,144,128]{2,1,0:T(8,128)S(1)}, f32[3,144,128]{2,1,0:T(8,128)S(1)}, u32[]{:S(2)}, u32[]{:S(2)}) collective-permute-start(f32[3,144,128]{2,1,0:T(8,128)S(1)} %get-tuple-element.25), channel_id=1, source_target_pairs={{0,1},{1,2},{2,3},{3,4},{4,5},{5,6},{6,7},{7,0},{8,9},{9,10},{10,1... | collective-permute-start | bytes 663560 | tf_op jit(solution)/shard_map/ppermute | solution.py:639
  20.7 5.4 %collective-permute-start.3 = (f32[3,144,128]{2,1,0:T(8,128)S(1)}, f32[3,144,128]{2,1,0:T(8,128)S(1)}, u32[]{:S(2)}, u32[]{:S(2)}) collective-permute-start(f32[3,144,128]{2,1,0:T(8,128)S(1)} %get-tuple-element.26), channel_id=1, source_target_pairs={{0,7},{1,0},{2,1},{3,2},{4,3},{5,4},{6,5},{7,6},{8,15},{9,8},{10,9... | collective-permute-start | bytes 663560 | tf_op jit(solution)/shard_map/ppermute | solution.py:639

commit v4 on v3

--- a/solution.py
+++ b/solution.py
@@ -25,11 +25,10 @@
 OUTSIDE = (LOW - 8, LOW + WIDE)
 BATCHES = (GROUPS[:6], GROUPS[6:12], GROUPS[12:])
 SENT = 3
-FIELDS = 480
-
-
-def params(limit=VMEM):
-    return pltpu.CompilerParams(vmem_limit_bytes=limit)
+
+
+def params():
+    return pltpu.CompilerParams(vmem_limit_bytes=VMEM)
 
 
 def rows_at(row):
@@ -94,16 +93,16 @@
     return pl.pallas_call(
         edges_kernel,
         in_specs=[pl.BlockSpec(memory_space=pltpu.HBM)] * 4,
-        out_shape=[jax.ShapeDtypeStruct((rows, SY), F32) for rows in (BEFORE_ROWS, NEXT_ROWS)],
+        out_shape=[pltpu.VMEM((rows, SY), F32) for rows in (BEFORE_ROWS, NEXT_ROWS)],
         scratch_shapes=[
             pltpu.VMEM((2, 2, KL, 8, SY), F32),
             pltpu.VMEM((2, 2, KL, 16, SY), jnp.bfloat16),
             pltpu.VMEM((2, 8, SY), jnp.int32),
             pltpu.SemaphoreType.DMA((10,)),
         ],
-        compiler_params=params(62 * 1024 * 1024),
+        compiler_params=params(),
         name="edges",
-    )(tracers, east, north, levels)
+    )(*(pltpu.with_memory_space_constraint(x, pltpu.HBM) for x in (tracers, east, north, levels)))
 
 
 def low_tile(ref, a, k):
@@ -120,16 +119,28 @@
     return ref[at : at + 8, :]
 
 
-def pack(source, rows):
+def pack(source, rows, last):
     group = lanes((rows, 128)) // 8
     one = jnp.zeros((rows, 128), F32)
-    two = jnp.zeros((rows, 128), F32)
+    beyond = jnp.zeros((rows, 128), F32)
     for k in range(KL):
         value = source(k)
-        here = group == k
-        one = jnp.where(here, pltpu.roll(value, (8 * k - 124) % 128, 1), one)
-        two = jnp.where(here, pltpu.roll(value, (8 * k - 125) % 128, 1), two)
+        one = jnp.where(group == k, pltpu.roll(value, (8 * k - 124) % 128, 1), one)
+        if last:
+            beyond = jnp.where(group == k, pltpu.roll(value, (8 * k + 3) % 128, 1), beyond)
+    two = pltpu.roll(one, 127, 1)
+    if last:
+        two = jnp.where(lanes((rows, 128)) % 8 == 7, beyond, two)
     return one, two
+
+
+def pack_depth(sources):
+    lane = lanes(sources[0].shape)
+    values = [pltpu.roll(x, turn, 1) for turn in (4, 3) for x in sources]
+    values = [jnp.where(lane < 8, x, 0.0) for x in values]
+    for turn in (8, 16, 32, 64):
+        values = [x + pltpu.roll(x, turn, 1) for x in values]
+    return list(zip(values[: len(sources)], values[len(sources) :], strict=True))
 
 
 def merge_one(t0, t1, e, n, d):
@@ -160,8 +171,8 @@
     return a, b, pltpu.roll(c, 124, 1), c, depth
 
 
-def pack_all(sources, rows, own, own_rows, sent_one, sent_two, sent_rows):
-    packed = [pack(source, rows) for source in sources]
+def pack_all(sources, depths, rows, own, own_rows, sent_one, sent_two, sent_rows):
+    packed = [pack(source, rows, a < 2) for a, source in enumerate(sources)] + [depths]
     for which in range(2):
         for a in range(5):
             own[which, a, own_rows, :] = packed[a][which]
@@ -175,6 +186,10 @@
 
 def pack_rows_kernel(t, e, n, d, own, one, two):
     chunk = 16
+    groups = range(0, SX, 8)
+    for g, pair in zip(groups, pack_depth([d[rows_at(g), :].astype(F32) for g in groups]), strict=True):
+        for which in range(2):
+            own[which, 4, rows_at(g), :] = pair[which]
 
     def body(i, carry):
         rows = pl.ds(pl.multiple_of(i * chunk, chunk), chunk)
@@ -183,9 +198,9 @@
             lambda k: t[1, k, rows, :],
             lambda k: e[k, rows, :].astype(F32),
             lambda k: n[k, rows, :].astype(F32),
-            lambda k: d[rows, :].astype(F32),
         )
-        pack_all(sources, chunk, own, rows, one, two, rows)
+        depths = own[0, 4, rows, :], own[1, 4, rows, :]
+        pack_all(sources, depths, chunk, own, rows, one, two, rows)
         return carry
 
     lax.fori_loop(0, SX // chunk, body, 0)
@@ -210,9 +225,10 @@
         for a in range(SENT):
             one[a, rows_at(g + EDGE), :] = one_rows[a, rows_at(g), :]
             two[a, rows_at(g + EDGE), :] = two_rows[a, rows_at(g), :]
-    for ref, tile, own_at, at in ((low_in, low_tile, 0, 0), (high_in, high_tile, 8, WIDE - EDGE)):
-        sources = [functools.partial(tile, ref, a) for a in range(5)]
-        pack_all(sources, 8, own, rows_at(own_at), one, two, rows_at(at))
+    depths = pack_depth([low_tile(low_in, 4, 0), high_tile(high_in, 4, 0)])
+    for side, (ref, tile, at) in enumerate(((low_in, low_tile, 0), (high_in, high_tile, WIDE - EDGE))):
+        sources = [functools.partial(tile, ref, a) for a in range(4)]
+        pack_all(sources, depths[side], 8, own, rows_at(8 * side), one, two, rows_at(at))
 
 
 def pack_edges(low, high, one, two):
@@ -555,7 +571,7 @@
         row = jnp.where(lane == i, value, row)
     for g in range(0, 128, 8):
         sums[rows_at(g), :] = row
-    pltpu.make_async_copy(field.at[:, 0, PAD : PAD + SX, :], fields.at[0:3], sems.at[1]).wait()
+    pltpu.make_async_copy(field.at[:, 0, PAD : PAD + SX, :], fields, sems.at[1]).wait()
     pltpu.make_async_copy(staged, new, sems.at[0]).wait()
 
 
@@ -578,7 +594,7 @@
         functools.partial(operator_kernel, count=count),
         out_shape=[
             jax.ShapeDtypeStruct(blocked.shape, F32),
-            jax.ShapeDtypeStruct((FIELDS, SX, SY), F32),
+            pltpu.HBM((3, SX, SY), F32),
             jax.ShapeDtypeStruct((128, 128), F32),
         ],
         out_specs=[
@@ -593,9 +609,12 @@
     )(levels, low, high, own_rows, own_edges, one_in, two_in, blocked, wall_total)
 
 
-def finish_kernel(sums, fields_in, out, fields, sem):
-    copy = pltpu.make_async_copy(fields_in.at[0:3], fields, sem)
+def finish_kernel(sums_in, fields_in, out, sums, fields, sems):
+    first_copy = pltpu.make_async_copy(sums_in, sums, sems.at[0])
+    copy = pltpu.make_async_copy(fields_in, fields, sems.at[1])
+    first_copy.start()
     copy.start()
+    first_copy.wait()
     value = sums[0:8, :]
     for g in range(8, 128, 8):
         value = value + sums[rows_at(g), :]
@@ -627,11 +646,15 @@
 def finish(sums, fields):
     return pl.pallas_call(
         finish_kernel,
-        in_specs=[pl.BlockSpec(memory_space=pltpu.VMEM), pl.BlockSpec(memory_space=pltpu.HBM)],
+        in_specs=[pl.BlockSpec(memory_space=pl.ANY)] * 2,
         out_shape=jax.ShapeDtypeStruct((SX, SY), F32),
-        scratch_shapes=[pltpu.VMEM((3, SX, SY), F32), pltpu.SemaphoreType.DMA(())],
+        scratch_shapes=[
+            pltpu.VMEM((128, 128), F32),
+            pltpu.VMEM((3, SX, SY), F32),
+            pltpu.SemaphoreType.DMA((2,)),
+        ],
         name="finish",
-    )(sums, fields)
+    )(sums, pltpu.with_memory_space_constraint(fields, pltpu.HBM))
 
 
 def shift(array, axis, step):

time: 47.2 us -> 45.6 us (0.966)
  local copies, waits for them, and re-layouts: 1.6 us -> 0.02 us
  waiting for transfers between devices: 3.18 us -> 4.14 us
  Pallas kernels: 16.7 us -> 15.8 us
    unnamed x10 -> x8, local copies, waits for them, and re-layouts: 1.6 us -> 0.02 us
    ppermute x4, waiting for transfers between devices: 3.18 us -> 4.14 us  [shift(): lax.ppermute(array, axis, [(i, (i + step) % count) for i in range(count)])]
    pallas_call x1, Pallas kernels: 2.42 us -> 1.63 us  [finish(): pl.pallas_call(finish_kernel, in_specs=[pl.BlockSpec(memory_space=pl.ANY)...]
    pallas_call x1, Pallas kernels: 1.96 us -> 1.34 us  [edges(): pl.pallas_call(edges_kernel, in_specs=[pl.BlockSpec(memory_space=pltpu.HB...]
  transfers between devices with their start and end apart: 4 -> 4, of which waited for: 2 -> 2; matrix products, arithmetic and copies ran while one was open for 0% -> 0% of each run, Pallas kernels for 17% -> 18%
where the time goes in v4:
time: 45.6 us; the launch traced here: 45.4 us
  Pallas kernels  15.8 us (35%)
  blocking collectives  14.6 us (32%)
  starting transfers between devices  10.2 us (22%)
  waiting for transfers between devices  4.14 us (9%)
  between operations  0.72 us (2%)
    all_to_all x1, blocking collectives, on_device(): lax.all_to_all(sums, ('gx', 'gy'), split_axis=0, concat_axis=0, tiled=True)  14.6 us
    ppermute x4, starting transfers between devices, shift(): lax.ppermute(array, axis, [(i, (i + step) % count) for i in range(count)])  10.2 us
    pallas_call x1, Pallas kernels, block_levels(): pl.pallas_call(levels_kernel, out_shape=[jax.ShapeDtypeStruct(tracers.sha...  4.88 us
    ppermute x4, waiting for transfers between devices, shift(): lax.ppermute(array, axis, [(i, (i + step) % count) for i in range(count)])  4.14 us
    pallas_call x1, Pallas kernels, operator(): pl.pallas_call(functools.partial(operator_kernel, count=count), out_shape...  3.89 us
    pallas_call x1, Pallas kernels, pack_rows(): pl.pallas_call(pack_rows_kernel, out_shape=[jax.ShapeDtypeStruct((2, 5, S...  3.47 us
    pallas_call x1, Pallas kernels, finish(): pl.pallas_call(finish_kernel, in_specs=[pl.BlockSpec(memory_space=pl.ANY)...  1.63 us
    pallas_call x1, Pallas kernels, edges(): pl.pallas_call(edges_kernel, in_specs=[pl.BlockSpec(memory_space=pltpu.HB...  1.34 us
  transfers between devices with their start and end apart: 4, of which 2 were waited for; matrix products, arithmetic and copies ran while one was open for 0% of the time, Pallas kernels for 18%

profile of v4, /device:TPU:1, one launch (start us, length us, event | category | flops | bytes accessed | tf_op | source)
XLA Modules:
  0.0 45.4 jit_solution(13511891406187454020)
XLA Ops:
  0.6 0.0 copy-start.3
  0.6 0.0 copy-start.2
  0.7 0.0 copy-start.1
  0.7 0.0 copy-start
  0.7 1.3 %edges.1 = (f32[304,128]{1,0:T(8,128)S(1)}, f32[264,128]{1,0:T(8,128)S(1)}) custom-call(f32[2,16,128,128]{3,2,1,0:T(8,128)} %tracers.1, bf16[16,128,128]{2,1,0:T(8,128)(2,1)} %east.1, bf16[16,128,128]{2,1,0:T(8,128)(2,1)} %north.1, s32[128,128]{1,0:T(8,128)} %levels.3), custom_call_target="tpu_custom_call" | custom-call | tf_op jit(solution)/shard_map/edges/pallas_call | solution.py:93
  2.0 6.8 %collective-permute-start.1 = (f32[304,128]{1,0:T(8,128)S(1)}, f32[304,128]{1,0:T(8,128)S(1)}, u32[]{:S(2)}, u32[]{:S(2)}) collective-permute-start(f32[304,128]{1,0:T(8,128)S(1)} %get-tuple-element.18), channel_id=1, source_target_pairs={{0,120},{8,0},{16,8},{24,16},{32,24},{40,32},{48,40},{56,48},{64,5... | collective-permute-start | bytes 466952 | tf_op jit(solution)/shard_map/ppermute | solution.py:662
  8.9 0.0 collective-permute-start
  8.9 0.0 copy-done.3
  8.9 0.0 copy-done.2
  8.9 0.0 copy-done.1
  8.9 0.0 copy-done
  8.9 3.5 %pack_rows.1 = (f32[2,5,128,128]{3,2,1,0:T(8,128)S(1)}, f32[3,128,128]{2,1,0:T(8,128)S(1)}, f32[3,128,128]{2,1,0:T(8,128)S(1)}) custom-call(f32[2,16,128,128]{3,2,1,0:T(8,128)S(1)} %copy-done, bf16[16,128,128]{2,1,0:T(8,128)(2,1)S(1)} %copy-done.1, bf16[16,128,128]{2,1,0:T(8,128)(2,1)S(1)} %copy-done.2, s32[128,128]{1,0:T(8,128)S(1)} %copy-done.3), custom_call_target="tpu_custom_call" | custom-call | tf_op jit(solution)/shard_map/pack_rows/pallas_call | solution.py:211
  12.4 3.7 %collective-permute-done.low_in = f32[264,128]{1,0:T(8,128)S(1)} collective-permute-done((f32[264,128]{1,0:T(8,128)S(1)}, f32[264,128]{1,0:T(8,128)S(1)}, u32[]{:S(2)}, u32[]{:S(2)}) %collective-permute-start) | collective-permute-done | bytes 135200 | tf_op jit(solution)/shard_map/ppermute | solution.py:662
  16.1 0.0 collective-permute-done.1.high_in
  16.1 0.6 %pack_edges.1 = (f32[2,5,16,128]{3,2,1,0:T(8,128)S(1)}, f32[3,144,128]{2,1,0:T(8,128)S(1)}, f32[3,144,128]{2,1,0:T(8,128)S(1)}, f32[65,8,128]{2,1,0:T(8,128)S(1)}, f32[65,8,128]{2,1,0:T(8,128)S(1)}) custom-call(f32[264,128]{1,0:T(8,128)S(1)} %collective-permute-done.low_in, f32[304,128]{1,0:T(8,128)S(1)} %collective-permute-done.1.high_in, ...), custom_call_target="tpu_custom_call" | custom-call | tf_op jit(solution)/shard_map/pack_edges/pallas_call | solution.py:237
  16.7 3.3 %collective-permute-start.2 = (f32[3,144,128]{2,1,0:T(8,128)S(1)}, f32[3,144,128]{2,1,0:T(8,128)S(1)}, u32[]{:S(2)}, u32[]{:S(2)}) collective-permute-start(f32[3,144,128]{2,1,0:T(8,128)S(1)} %get-tuple-element.25), channel_id=1, source_target_pairs={{0,1},{1,2},{2,3},{3,4},{4,5},{5,6},{6,7},{7,0},{8,9},{9,10},{10,1... | collective-permute-start | bytes 663560 | tf_op jit(solution)/shard_map/ppermute | solution.py:662
  20.0 0.0 collective-permute-start.3
  20.0 4.9 %block_levels.1 = (f32[2,16,128,128]{3,2,1,0:T(8,128)S(1)}, f32[160,128]{1,0:T(8,128)S(1)}) custom-call(f32[2,16,128,128]{3,2,1,0:T(8,128)S(1)} %copy-done, bf16[16,128,128]{2,1,0:T(8,128)(2,1)S(1)} %copy-done.1, bf16[16,128,128]{2,1,0:T(8,128)(2,1)S(1)} %copy-done.2, s32[128,128]{1,0:T(8,128)S(1)} %copy-done.3, f32[65,8,128]{2,1,0:T(8,128)S(1)} %get-tuple-element.21.low, ...), custom_call_target="tpu_custom_call" | custom-call | flops 20000000 | bytes 6000000 | tf_op jit(solution)/shard_map/block_levels/pallas_call | solution.py:358
  24.9 0.0 collective-permute-done.2.one_in
  24.9 0.5 collective-permute-done.3.two_in
  25.4 3.9 %operator.1 = (f32[2,16,128,128]{3,2,1,0:T(8,128)}, f32[3,128,128]{2,1,0:T(8,128)}, f32[128,128]{1,0:T(8,128)S(1)}) custom-call(s32[128,128]{1,0:T(8,128)S(1)} %copy-done.3, f32[65,8,128]{2,1,0:T(8,128)S(1)} %get-tuple-element.21.low, f32[65,8,128]{2,1,0:T(8,128)S(1)} %get-tuple-element.22.high, f32[2,5,128,128]{3,2,1,0:T(8,128)S(1)} %get-tuple-element.23.own_rows, ...), custom_call_target="tpu_custom_call" | custom-call | tf_op jit(solution)/shard_map/operator/pallas_call | solution.py:593
  29.3 14.6 %all_to_all.11 = f32[128,1,128]{2,1,0:T(1,128)} all-to-all(f32[128,1,128]{2,1,0:T(1,128)S(1)} %bitcast.4), channel_id=1, replica_groups=mesh['gx'=16,'gy'=8] {'gx','gy'}, dimensions={0} | all-to-all | bytes 131072 | tf_op jit(solution)/shard_map/all_to_all | solution.py:677
  43.8 1.6 %finish.1 = f32[128,128]{1,0:T(8,128)} custom-call(f32[128,128]{1,0:T(8,128)} %bitcast.5, f32[3,128,128]{2,1,0:T(8,128)} %get-tuple-element.31.fields_in), custom_call_target="tpu_custom_call" | custom-call | tf_op jit(solution)/shard_map/finish/pallas_call | solution.py:647
Async XLA Ops:
  0.6 8.2 %copy-start.3 = (s32[128,128]{1,0:T(8,128)S(1)}, s32[128,128]{1,0:T(8,128)}, u32[]{:S(2)}) copy-start(s32[128,128]{1,0:T(8,128)} %levels.3) | copy-start | bytes 196612
  0.6 8.2 %copy-start.2 = (bf16[16,128,128]{2,1,0:T(8,128)(2,1)S(1)}, bf16[16,128,128]{2,1,0:T(8,128)(2,1)}, u32[]{:S(2)}) copy-start(bf16[16,128,128]{2,1,0:T(8,128)(2,1)} %north.1) | copy-start | bytes 1572868
  0.7 8.2 %copy-start.1 = (bf16[16,128,128]{2,1,0:T(8,128)(2,1)S(1)}, bf16[16,128,128]{2,1,0:T(8,128)(2,1)}, u32[]{:S(2)}) copy-start(bf16[16,128,128]{2,1,0:T(8,128)(2,1)} %east.1) | copy-start | bytes 1572868
  0.7 8.2 %copy-start = (f32[2,16,128,128]{3,2,1,0:T(8,128)S(1)}, f32[2,16,128,128]{3,2,1,0:T(8,128)}, u32[]{:S(2)}) copy-start(f32[2,16,128,128]{3,2,1,0:T(8,128)} %tracers.1) | copy-start | bytes 6291460
  2.0 14.0 %collective-permute-start.1 = (f32[304,128]{1,0:T(8,128)S(1)}, f32[304,128]{1,0:T(8,128)S(1)}, u32[]{:S(2)}, u32[]{:S(2)}) collective-permute-start(f32[304,128]{1,0:T(8,128)S(1)} %get-tuple-element.18), channel_id=1, source_target_pairs={{0,120},{8,0},{16,8},{24,16},{32,24},{40,32},{48,40},{56,48},{64,5... | collective-permute-start | bytes 466952 | tf_op jit(solution)/shard_map/ppermute | solution.py:662
  8.9 7.2 %collective-permute-start = (f32[264,128]{1,0:T(8,128)S(1)}, f32[264,128]{1,0:T(8,128)S(1)}, u32[]{:S(2)}, u32[]{:S(2)}) collective-permute-start(f32[264,128]{1,0:T(8,128)S(1)} %get-tuple-element.17), channel_id=1, source_target_pairs={{0,8},{8,16},{16,24},{24,32},{32,40},{40,48},{48,56},{56,64},{64,7... | collective-permute-start | bytes 405512 | tf_op jit(solution)/shard_map/ppermute | solution.py:662
  16.7 8.2 %collective-permute-start.2 = (f32[3,144,128]{2,1,0:T(8,128)S(1)}, f32[3,144,128]{2,1,0:T(8,128)S(1)}, u32[]{:S(2)}, u32[]{:S(2)}) collective-permute-start(f32[3,144,128]{2,1,0:T(8,128)S(1)} %get-tuple-element.25), channel_id=1, source_target_pairs={{0,1},{1,2},{2,3},{3,4},{4,5},{5,6},{6,7},{7,0},{8,9},{9,10},{10,1... | collective-permute-start | bytes 663560 | tf_op jit(solution)/shard_map/ppermute | solution.py:662
  20.0 5.4 %collective-permute-start.3 = (f32[3,144,128]{2,1,0:T(8,128)S(1)}, f32[3,144,128]{2,1,0:T(8,128)S(1)}, u32[]{:S(2)}, u32[]{:S(2)}) collective-permute-start(f32[3,144,128]{2,1,0:T(8,128)S(1)} %get-tuple-element.26), channel_id=1, source_target_pairs={{0,7},{1,0},{2,1},{3,2},{4,3},{5,4},{6,5},{7,6},{8,15},{9,8},{10,9... | collective-permute-start | bytes 663560 | tf_op jit(solution)/shard_map/ppermute | solution.py:662

commit v5 on v4

--- a/solution.py
+++ b/solution.py
@@ -24,6 +24,11 @@
 GROUPS = tuple(range(LOW, LOW + WIDE, 8))
 OUTSIDE = (LOW - 8, LOW + WIDE)
 BATCHES = (GROUPS[:6], GROUPS[6:12], GROUPS[12:])
+INNER = GROUPS[1:-1]
+INNER_BATCHES = (INNER[:6], INNER[6:11], INNER[11:])
+ENDS = (GROUPS[0], GROUPS[1], GROUPS[-2], GROUPS[-1])
+END_BATCHES = (GROUPS[:3] + GROUPS[-3:],)
+END_OUTSIDE = (GROUPS[0] - 8, GROUPS[3], GROUPS[-4], GROUPS[-1] + 8)
 SENT = 3
 
 
@@ -184,7 +189,7 @@
             sent[a, sent_rows, :] = values[a]
 
 
-def pack_rows_kernel(t, e, n, d, own, one, two):
+def pack_block(t, e, n, d, own, one, two):
     chunk = 16
     groups = range(0, SX, 8)
     for g, pair in zip(groups, pack_depth([d[rows_at(g), :].astype(F32) for g in groups]), strict=True):
@@ -206,40 +211,28 @@
     lax.fori_loop(0, SX // chunk, body, 0)
 
 
-def pack_rows(tracers, east, north, levels):
-    sent = jax.ShapeDtypeStruct((SENT, SX, 128), F32)
-    return pl.pallas_call(
-        pack_rows_kernel,
-        out_shape=[jax.ShapeDtypeStruct((2, 5, SX, 128), F32), sent, sent],
-        compiler_params=params(),
-        name="pack_rows",
-    )(tracers, east, north, levels)
-
-
-def pack_edges_kernel(low_in, high_in, one_rows, two_rows, own, one, two, low, high):
+def pack_edges_kernel(low_in, high_in, after, own, one, two, low, high):
+    del after
     for a in range(5):
         for k in range(KL if a < 4 else 1):
             low[KL * a + k] = low_tile(low_in, a, k)
             high[KL * a + k] = high_tile(high_in, a, k)
-    for g in range(0, SX, 8):
-        for a in range(SENT):
-            one[a, rows_at(g + EDGE), :] = one_rows[a, rows_at(g), :]
-            two[a, rows_at(g + EDGE), :] = two_rows[a, rows_at(g), :]
     depths = pack_depth([low_tile(low_in, 4, 0), high_tile(high_in, 4, 0)])
-    for side, (ref, tile, at) in enumerate(((low_in, low_tile, 0), (high_in, high_tile, WIDE - EDGE))):
+    for side, (ref, tile) in enumerate(((low_in, low_tile), (high_in, high_tile))):
         sources = [functools.partial(tile, ref, a) for a in range(4)]
-        pack_all(sources, depths[side], 8, own, rows_at(8 * side), one, two, rows_at(at))
-
-
-def pack_edges(low, high, one, two):
-    sent = jax.ShapeDtypeStruct((SENT, WIDE, 128), F32)
+        pack_all(sources, depths[side], 8, own, rows_at(8 * side), one, two, rows_at(8 * side))
+
+
+def pack_edges(low, high, after):
+    sent = jax.ShapeDtypeStruct((SENT, 2 * EDGE, 128), F32)
     halo = jax.ShapeDtypeStruct((ARRAYS, EDGE, SY), F32)
     return pl.pallas_call(
         pack_edges_kernel,
+        in_specs=[pl.BlockSpec(memory_space=pltpu.VMEM)] * 2 + [pl.BlockSpec(memory_space=pl.ANY)],
         out_shape=[jax.ShapeDtypeStruct((2, 5, 2 * EDGE, 128), F32), sent, sent, halo, halo],
         compiler_params=params(),
         name="pack_edges",
-    )(low, high, one, two)
+    )(low, high, after)
 
 
 def face_weights(face, flow_value, threshold):
@@ -249,9 +242,8 @@
     return ahead, back
 
 
-def set_weights(depth_at, face_east, face_north, flow, coef, threshold, south):
-    coef[1, rows_at(LOW - 8), :] = jnp.zeros((8, 128), F32)
-    for batch in BATCHES:
+def set_weights(batches, depth_at, face_east, face_north, flow, coef, threshold, south):
+    for batch in batches:
         a_north, b_north = {}, {}
         for g in batch:
             rows = rows_at(g)
@@ -301,72 +293,144 @@
         depth[rows_at(outside), :] = jnp.zeros((8, 128), F32)
 
 
-def levels_kernel(tracers, east, north, levels, low, high, new, total, depth, face, q0, q1, flow, coef):
-    lane = lanes()
-    halo_depth(levels, low, high, depth)
-    for g in GROUPS:
-        rows = rows_at(g)
-        here = depth[rows, :]
-        face[0, rows, :] = jnp.minimum(here, depth[rows_at(g + 1), :])
-        face[1, rows, :] = jnp.where(lane == 127, 0.0, jnp.minimum(here, ahead_one(here)))
-        total[rows, :] = jnp.zeros((8, 128), F32)
-
+def every_level(batches, results, load, store, depth, face, q0, q1, flow, coef):
     def level(k, carry):
-        threshold = k.astype(F32)
-        for g in GROUPS:
-            r = g - LOW
-            rows = rows_at(g)
-            if r < EDGE or r >= WIDE - EDGE:
-                ref = low if r < EDGE else high
-                q0[0, rows, :] = ref[k]
-                q0[1, rows, :] = ref[KL + k]
-                flow[0, rows, :] = ref[2 * KL + k]
-                flow[1, rows, :] = ref[3 * KL + k]
-            else:
-                q0[0, rows, :] = tracers[0, k, rows_at(r - EDGE), :]
-                q0[1, rows, :] = tracers[1, k, rows_at(r - EDGE), :]
-        flow[0, PAD : PAD + SX, :] = east[k].astype(F32)
-        flow[1, PAD : PAD + SX, :] = north[k].astype(F32)
+        load(k)
         set_weights(
+            batches,
             lambda g: depth[rows_at(g), :],
             lambda g: face[0, rows_at(g), :],
             lambda g: face[1, rows_at(g), :],
             flow,
             coef,
-            threshold,
+            k.astype(F32),
             lambda g, a, b: (a, b),
         )
         for tracer in range(2):
-            for batch in BATCHES:
+            for batch in batches:
                 for g, value in update(q0.at[tracer], coef, batch).items():
                     q1[tracer, rows_at(g), :] = value
-        for batch in BATCHES:
+        for batch in results:
             temperature = update(q1.at[0], coef, batch)
             salinity = update(q1.at[1], coef, batch)
             for g in batch:
-                if PAD <= g < PAD + SX:
-                    new[0, k, rows_at(g - PAD), :] = temperature[g]
-                    new[1, k, rows_at(g - PAD), :] = salinity[g]
-                total[rows_at(g), :] += temperature[g] - 0.8 * salinity[g]
+                store(k, g, temperature[g], salinity[g])
         return carry
 
     lax.fori_loop(0, KL, level, 0)
 
 
-def block_levels(tracers, east, north, levels, low, high):
-    tall = (ROWS, 128)
+def set_faces(groups, depth, face):
+    lane = lanes()
+    ahead = {g: ahead_one(depth[rows_at(g), :]) for g in groups}
+    for g in groups:
+        rows = rows_at(g)
+        here = depth[rows, :]
+        face[0, rows, :] = jnp.minimum(here, depth[rows_at(g + 1), :])
+        face[1, rows, :] = jnp.where(lane == 127, 0.0, jnp.minimum(here, ahead[g]))
+
+
+def block_kernel(tracers, east, north, levels, after, own, one, two, new, total, depth, face, q0, q1, flow, coef):
+    del after
+    pack_block(tracers, east, north, levels, own, one, two)
+    blank = jnp.zeros((8, 128), F32)
+    for g in INNER:
+        depth[rows_at(g), :] = levels[rows_at(g - PAD), :].astype(F32)
+        total[rows_at(g), :] = blank
+    for g in (GROUPS[0], GROUPS[-1]):
+        depth[rows_at(g), :] = blank
+        total[rows_at(g), :] = blank
+        for i in range(2):
+            coef[i, rows_at(g), :] = blank
+            q0[i, rows_at(g), :] = blank
+            q1[i, rows_at(g), :] = blank
+    set_faces(INNER, depth, face)
+
+    def load(k):
+        for tracer in range(2):
+            q0[tracer, PAD : PAD + SX, :] = tracers[tracer, k]
+        flow[0, PAD : PAD + SX, :] = east[k].astype(F32)
+        flow[1, PAD : PAD + SX, :] = north[k].astype(F32)
+
+    def store(k, g, temperature, salinity):
+        new[0, k, rows_at(g - PAD), :] = temperature
+        new[1, k, rows_at(g - PAD), :] = salinity
+        total[rows_at(g), :] += temperature - 0.8 * salinity
+
+    every_level(INNER_BATCHES, INNER_BATCHES, load, store, depth, face, q0, q1, flow, coef)
+
+
+LEVEL_SCRATCH = [pltpu.VMEM(shape + (ROWS, 128), F32) for shape in ((), (2,), (2,), (2,), (2,), (5,))]
+
+
+def block(tracers, east, north, levels, after):
+    sent = pltpu.VMEM((SENT, SX, 128), F32)
     return pl.pallas_call(
-        levels_kernel,
-        out_shape=[jax.ShapeDtypeStruct(tracers.shape, F32), jax.ShapeDtypeStruct(tall, F32)],
-        scratch_shapes=[pltpu.VMEM(s + tall, F32) for s in ((), (2,), (2,), (2,), (2,), (5,))],
+        block_kernel,
+        in_specs=[pl.BlockSpec(memory_space=pltpu.VMEM)] * 4 + [pl.BlockSpec(memory_space=pl.ANY)],
+        out_shape=[
+            pltpu.VMEM((2, 5, SX, 128), F32),
+            sent,
+            sent,
+            pltpu.VMEM(tracers.shape, F32),
+            pltpu.VMEM((ROWS, 128), F32),
+        ],
+        scratch_shapes=LEVEL_SCRATCH,
         compiler_params=params(),
-        cost_estimate=pl.CostEstimate(flops=20_000_000, bytes_accessed=6_000_000, transcendentals=0),
-        name="block_levels",
+        cost_estimate=pl.CostEstimate(flops=20_000_000, bytes_accessed=24_000_000, transcendentals=0),
+        name="block",
+    )(tracers, east, north, levels, after)
+
+
+def ends_kernel(tracers, east, north, levels, low, high, new, total, depth, face, q0, q1, flow, coef):
+    blank = jnp.zeros((8, 128), F32)
+    halo_depth(levels, low, high, depth)
+    set_faces(END_BATCHES[0], depth, face)
+    for g in ENDS:
+        total[rows_at(g), :] = blank
+    for at in END_OUTSIDE:
+        for i in range(2):
+            coef[i, rows_at(at), :] = blank
+            q0[i, rows_at(at), :] = blank
+            q1[i, rows_at(at), :] = blank
+
+    def load(k):
+        for g, ref in ((GROUPS[0], low), (GROUPS[-1], high)):
+            for i in range(2):
+                q0[i, rows_at(g), :] = ref[KL * i + k]
+                flow[i, rows_at(g), :] = ref[KL * (2 + i) + k]
+        for at in (0, SX - 16):
+            rows = slice(at, at + 16)
+            out = slice(PAD + at, PAD + at + 16)
+            for tracer in range(2):
+                q0[tracer, out, :] = tracers[tracer, k, rows, :]
+            flow[0, out, :] = east[k, rows, :].astype(F32)
+            flow[1, out, :] = north[k, rows, :].astype(F32)
+
+    def store(k, g, temperature, salinity):
+        if g == ENDS[1] or g == ENDS[2]:
+            rows = rows_at(0 if g == ENDS[1] else 8)
+            new[0, k, rows, :] = temperature
+            new[1, k, rows, :] = salinity
+        total[rows_at(g), :] += temperature - 0.8 * salinity
+
+    every_level(END_BATCHES, (ENDS,), load, store, depth, face, q0, q1, flow, coef)
+
+
+def end_levels(tracers, east, north, levels, low, high):
+    return pl.pallas_call(
+        ends_kernel,
+        out_shape=[pltpu.VMEM((2, KL, 16, SY), F32), pltpu.VMEM((ROWS, 128), F32)],
+        scratch_shapes=LEVEL_SCRATCH,
+        compiler_params=params(),
+        cost_estimate=pl.CostEstimate(flops=5_000_000, bytes_accessed=6_000_000, transcendentals=0),
+        name="end_levels",
     )(tracers, east, north, levels, low, high)
 
 
 def operator_kernel(
-    levels, low, high, own_rows, own_edges, one_in, two_in, blocked, wall_total,
+    levels, low, high, own_rows, own_edges, one_rows, two_rows, one_edges, two_edges,
+    blocked, ends, wall_total, ends_total,
     new, fields, sums,
     depth, strip_q, strip_depth, strip_face, strip_flow, strip_total, first_q, coef, total, field, grid, staged, sems, *, count,
 ):
@@ -385,13 +449,22 @@
             return own_edges[which, a, rows_at(8), :]
         return own_rows[which, a, rows_at(r - EDGE), :]
 
+    def sent(of_rows, of_edges, g):
+        r = g - LOW
+        if r < EDGE:
+            ref, rows = of_edges, rows_at(0)
+        elif r >= WIDE - EDGE:
+            ref, rows = of_edges, rows_at(8)
+        else:
+            ref, rows = of_rows, rows_at(r - EDGE)
+        return [ref[a, rows, :] for a in range(SENT)]
+
     halo_depth(levels, low, high, depth)
     parts = {}
     for g in GROUPS:
-        sent = rows_at(g - LOW)
         parts[g] = (
-            list(split_one(*(one_in[a, sent, :] for a in range(SENT)))),
-            list(split_two(*(two_in[a, sent, :] for a in range(SENT)))),
+            list(split_one(*sent(one_rows, one_edges, g))),
+            list(split_two(*sent(two_rows, two_edges, g))),
         )
     for g in GROUPS:
         rows = rows_at(g)
@@ -429,7 +502,9 @@
                 b_south = jnp.where(member == 0, b_first, b_south)
             return a_south, b_south
 
+        coef[1, rows_at(LOW - 8), :] = blank
         set_weights(
+            BATCHES,
             lambda g, at=at: at[rows_at(g), :],
             lambda g, at=at: jnp.minimum(at[rows_at(g), :], at[rows_at(g + 1), :]),
             lambda g, side=side: strip_face[side, rows_at(g), :],
@@ -479,7 +554,11 @@
             values = {g: pltpu.roll(first_q[tracer, rows_at(g + PAD), :], turn, 1) for g in range(0, SX, 8)}
             for g, value in values.items():
                 rows = rows_at(g)
-                staged[tracer, k, rows, :] = jnp.where(from_strip, value, blocked[tracer, k, rows, :])
+                if g == 0 or g == SX - 8:
+                    here = ends[tracer, k, rows_at(0 if g == 0 else 8), :]
+                else:
+                    here = blocked[tracer, k, rows, :]
+                staged[tracer, k, rows, :] = jnp.where(from_strip, value, here)
         for tracer in range(2):
             pltpu.make_async_copy(staged.at[tracer, k], new.at[tracer, k], sems.at[0]).start()
         return carry
@@ -511,7 +590,8 @@
         low_total = pltpu.roll(strip_total[0, rows, :], 4, 1)
         high_total = pltpu.roll(strip_total[1, rows, :], 5, 1)
         edge_total = jnp.where(lane < 64, low_total, high_total)
-        total[0, rows, :] = jnp.where(from_strip, edge_total, wall_total[rows, :])
+        here = (ends_total if g in ENDS else wall_total)[rows, :]
+        total[0, rows, :] = jnp.where(from_strip, edge_total, here)
         total[1, rows, :] = jnp.where(lane >= 64, low_total, high_total)
     for part in range(2):
         grid[1, part, rows_at(LOW - 8), :] = blank
@@ -575,7 +655,7 @@
     pltpu.make_async_copy(staged, new, sems.at[0]).wait()
 
 
-def operator(levels, low, high, own_rows, own_edges, one_in, two_in, blocked, wall_total, count):
+def operator(*arrays, count):
     tall = (ROWS, 128)
     scratch = (
         (),
@@ -593,7 +673,7 @@
     return pl.pallas_call(
         functools.partial(operator_kernel, count=count),
         out_shape=[
-            jax.ShapeDtypeStruct(blocked.shape, F32),
+            jax.ShapeDtypeStruct((2, KL, SX, SY), F32),
             pltpu.HBM((3, SX, SY), F32),
             jax.ShapeDtypeStruct((128, 128), F32),
         ],
@@ -603,10 +683,10 @@
             pl.BlockSpec(memory_space=pltpu.VMEM),
         ],
         scratch_shapes=[pltpu.VMEM(s + tall, F32) for s in scratch]
-        + [pltpu.VMEM(blocked.shape, F32), pltpu.SemaphoreType.DMA((2,))],
+        + [pltpu.VMEM((2, KL, SX, SY), F32), pltpu.SemaphoreType.DMA((2,))],
         compiler_params=params(),
         name="operator",
-    )(levels, low, high, own_rows, own_edges, one_in, two_in, blocked, wall_total)
+    )(*arrays)
 
 
 def finish_kernel(sums_in, fields_in, out, sums, fields, sems):
@@ -657,22 +737,27 @@
     )(sums, pltpu.with_memory_space_constraint(fields, pltpu.HBM))
 
 
-def shift(array, axis, step):
+def shift(array, axis, step, around):
     count = lax.axis_size(axis)
-    return lax.ppermute(array, axis, [(i, (i + step) % count) for i in range(count)])
+    pairs = [(i, (i + step) % count) for i in range(count) if around or 0 <= i + step < count]
+    return lax.ppermute(array, axis, pairs)
 
 
 def on_device(tracers, east, north, levels):
-    before, after = edges(tracers, east, north, levels)
-    before = shift(before, "gx", -1)
-    after = shift(after, "gx", 1)
-    own_rows, one, two = pack_rows(tracers, east, north, levels)
-    own_edges, one, two, low, high = pack_edges(after, before, one, two)
-    one_in = shift(one, "gy", 1)
-    two_in = shift(two, "gy", -1)
-    blocked, total = block_levels(tracers, east, north, levels, low, high)
+    to_before, to_after = edges(tracers, east, north, levels)
+    before = shift(to_before, "gx", -1, True)
+    after = shift(to_after, "gx", 1, True)
+    own_rows, one, two, blocked, total = block(tracers, east, north, levels, to_before)
+    one, two, after, before = lax.optimization_barrier((one, two, after, before))
+    one_rows = shift(one, "gy", 1, False)
+    two_rows = shift(two, "gy", -1, False)
+    own_edges, one, two, low, high = pack_edges(after, before, total)
+    one_edges = shift(one, "gy", 1, False)
+    two_edges = shift(two, "gy", -1, False)
+    ends, ends_total = end_levels(tracers, east, north, levels, low, high)
     new, fields, sums = operator(
-        levels, low, high, own_rows, own_edges, one_in, two_in, blocked, total, lax.axis_size("gy")
+        levels, low, high, own_rows, own_edges, one_rows, two_rows, one_edges, two_edges,
+        blocked, ends, total, ends_total, count=lax.axis_size("gy"),
     )
     sums = lax.all_to_all(sums, ("gx", "gy"), split_axis=0, concat_axis=0, tiled=True)
     return new, finish(sums, fields)

time: 45.6 us -> 57.1 us (1.25)
  starting transfers between devices: 10.2 us -> 18.5 us
  blocking collectives: 14.6 us -> 18.7 us
  waiting for transfers between devices: 4.14 us -> 0.06 us
  Pallas kernels: 15.8 us -> 18.8 us
    ppermute x4 -> x6, starting transfers between devices: 10.2 us -> 18.5 us  [shift(): return lax.ppermute(array, axis, pairs)]
    all_to_all x1, blocking collectives: 14.6 us -> 18.7 us  [on_device(): lax.all_to_all(sums, ('gx', 'gy'), split_axis=0, concat_axis=0, tiled=True)]
    ppermute x4 -> x6, waiting for transfers between devices: 4.14 us -> 0.06 us  [shift(): return lax.ppermute(array, axis, pairs)]
    pallas_call x3, Pallas kernels: 8.96 us -> 12 us  [the longest x1 8.19 us: block(): pl.pallas_call(block_kernel, in_specs=[pl.BlockSpec(memory_space=pltpu.VM...]
  transfers between devices with their start and end apart: 4 -> 6, of which waited for: 2 -> 0; matrix products, arithmetic and copies ran while one was open for 0% -> 0% of each run, Pallas kernels for 18% -> 21%
where the time goes in v5:
time: 57.1 us; the launch traced here: 56.9 us
  Pallas kernels  18.8 us (33%)
  blocking collectives  18.7 us (33%)
  starting transfers between devices  18.5 us (32%)
  between operations  0.77 us (1%)
    all_to_all x1, blocking collectives, on_device(): lax.all_to_all(sums, ('gx', 'gy'), split_axis=0, concat_axis=0, tiled=True)  18.7 us
    ppermute x6, starting transfers between devices, shift(): return lax.ppermute(array, axis, pairs)  18.5 us
    pallas_call x1, Pallas kernels, block(): pl.pallas_call(block_kernel, in_specs=[pl.BlockSpec(memory_space=pltpu.VM...  8.19 us
    pallas_call x1, Pallas kernels, operator(): pl.pallas_call(functools.partial(operator_kernel, count=count), out_shape...  3.9 us
    pallas_call x1, Pallas kernels, end_levels(): pl.pallas_call(ends_kernel, out_shape=[pltpu.VMEM((2, KL, 16, SY), F32),...  3.15 us
    pallas_call x1, Pallas kernels, finish(): pl.pallas_call(finish_kernel, in_specs=[pl.BlockSpec(memory_space=pl.ANY)...  1.63 us
    pallas_call x1, Pallas kernels, edges(): pl.pallas_call(edges_kernel, in_specs=[pl.BlockSpec(memory_space=pltpu.HB...  1.34 us
  transfers between devices with their start and end apart: 6, of which 0 were waited for; matrix products, arithmetic and copies ran while one was open for 0% of the time, Pallas kernels for 21%

profile of v5, /device:TPU:1, one launch (start us, length us, event | category | flops | bytes accessed | tf_op | source)
XLA Modules:
  0.0 56.9 jit_solution(14018877049923901654)
XLA Ops:
  0.6 0.0 copy-start.3
  0.6 0.0 copy-start.2
  0.7 0.0 copy-start.1
  0.7 0.0 copy-start
  0.7 1.3 %edges.1 = (f32[304,128]{1,0:T(8,128)S(1)}, f32[264,128]{1,0:T(8,128)S(1)}) custom-call(f32[2,16,128,128]{3,2,1,0:T(8,128)} %tracers.3, bf16[16,128,128]{2,1,0:T(8,128)(2,1)} %east.3, bf16[16,128,128]{2,1,0:T(8,128)(2,1)} %north.3, s32[128,128]{1,0:T(8,128)} %levels.5), custom_call_target="tpu_custom_call" | custom-call | tf_op jit(solution)/shard_map/edges/pallas_call | solution.py:98
  2.0 6.8 %collective-permute-start.1 = (f32[304,128]{1,0:T(8,128)S(1)}, f32[304,128]{1,0:T(8,128)S(1)}, u32[]{:S(2)}, u32[]{:S(2)}) collective-permute-start(f32[304,128]{1,0:T(8,128)S(1)} %get-tuple-element.23.after), channel_id=1, source_target_pairs={{0,120},{8,0},{16,8},{24,16},{32,24},{40,32},{48,40},{56,48},{64,5... | collective-permute-start | bytes 466952 | tf_op jit(solution)/shard_map/ppermute | solution.py:743
  8.9 0.0 collective-permute-start
  8.9 0.0 copy-done.3
  8.9 0.0 copy-done.2
  8.9 0.0 copy-done.1
  8.9 0.0 copy-done
  8.9 8.2 %block.1 = (f32[2,5,128,128]{3,2,1,0:T(8,128)S(1)}, f32[3,128,128]{2,1,0:T(8,128)S(1)}, f32[3,128,128]{2,1,0:T(8,128)S(1)}, f32[2,16,128,128]{3,2,1,0:T(8,128)S(1)}, f32[160,128]{1,0:T(8,128)S(1)}) custom-call(f32[2,16,128,128]{3,2,1,0:T(8,128)S(1)} %copy-done, bf16[16,128,128]{2,1,0:T(8,128)(2,1)S(1)} %copy-done.1, bf16[16,128,128]{2,1,0:T(8,128)(2,1)S(1)} %copy-done.2, ...), custom_call_target="tpu_custom_call" | custom-call | flops 20000000 | bytes 24000000 | tf_op jit(solution)/shard_map/block/pallas_call | solution.py:368
  17.1 0.0 collective-permute-done.low_in
  17.1 0.0 collective-permute-done.1.high_in
  17.1 4.2 %collective-permute-start.2 = (f32[3,128,128]{2,1,0:T(8,128)S(1)}, f32[3,128,128]{2,1,0:T(8,128)S(1)}, u32[]{:S(2)}, u32[]{:S(2)}) collective-permute-start(f32[3,128,128]{2,1,0:T(8,128)S(1)} %get-tuple-element.34), channel_id=1, source_target_pairs={{0,1},{1,2},{2,3},{3,4},{4,5},{5,6},{6,7},{8,9},{9,10},{10,11},{11... | collective-permute-start | bytes 589832 | tf_op jit(solution)/shard_map/ppermute | solution.py:743
  21.3 1.9 %collective-permute-start.3 = (f32[3,128,128]{2,1,0:T(8,128)S(1)}, f32[3,128,128]{2,1,0:T(8,128)S(1)}, u32[]{:S(2)}, u32[]{:S(2)}) collective-permute-start(f32[3,128,128]{2,1,0:T(8,128)S(1)} %get-tuple-element.35), channel_id=1, source_target_pairs={{1,0},{2,1},{3,2},{4,3},{5,4},{6,5},{7,6},{9,8},{10,9},{11,10},{12... | collective-permute-start | bytes 589832 | tf_op jit(solution)/shard_map/ppermute | solution.py:743
  23.2 0.6 %pack_edges.1 = (f32[2,5,16,128]{3,2,1,0:T(8,128)S(1)}, f32[3,16,128]{2,1,0:T(8,128)S(1)}, f32[3,16,128]{2,1,0:T(8,128)S(1)}, f32[65,8,128]{2,1,0:T(8,128)S(1)}, f32[65,8,128]{2,1,0:T(8,128)S(1)}) custom-call(f32[264,128]{1,0:T(8,128)S(1)} %collective-permute-done.low_in, f32[304,128]{1,0:T(8,128)S(1)} %collective-permute-done.1.high_in, ...), custom_call_target="tpu_custom_call" | custom-call | tf_op jit(solution)/shard_map/pack_edges/pallas_call | solution.py:229
  23.8 3.6 %collective-permute-start.4 = (f32[3,16,128]{2,1,0:T(8,128)S(1)}, f32[3,16,128]{2,1,0:T(8,128)S(1)}, u32[]{:S(2)}, u32[]{:S(2)}) collective-permute-start(f32[3,16,128]{2,1,0:T(8,128)S(1)} %get-tuple-element.36), channel_id=1, source_target_pairs={{0,1},{1,2},{2,3},{3,4},{4,5},{5,6},{6,7},{8,9},{9,10},{10,11},{11... | collective-permute-start | bytes 73736 | tf_op jit(solution)/shard_map/ppermute | solution.py:743
  27.5 1.9 %collective-permute-start.5 = (f32[3,16,128]{2,1,0:T(8,128)S(1)}, f32[3,16,128]{2,1,0:T(8,128)S(1)}, u32[]{:S(2)}, u32[]{:S(2)}) collective-permute-start(f32[3,16,128]{2,1,0:T(8,128)S(1)} %get-tuple-element.37), channel_id=1, source_target_pairs={{1,0},{2,1},{3,2},{4,3},{5,4},{6,5},{7,6},{9,8},{10,9},{11,10},{12... | collective-permute-start | bytes 73736 | tf_op jit(solution)/shard_map/ppermute | solution.py:743
  29.4 3.2 %end_levels.1 = (f32[2,16,16,128]{3,2,1,0:T(8,128)S(1)}, f32[160,128]{1,0:T(8,128)S(1)}) custom-call(f32[2,16,128,128]{3,2,1,0:T(8,128)S(1)} %copy-done, bf16[16,128,128]{2,1,0:T(8,128)(2,1)S(1)} %copy-done.1, bf16[16,128,128]{2,1,0:T(8,128)(2,1)S(1)} %copy-done.2, s32[128,128]{1,0:T(8,128)S(1)} %copy-done.3, f32[65,8,128]{2,1,0:T(8,128)S(1)} %get-tuple-element.30.low, ...), custom_call_target="tpu_custom_call" | custom-call | flops 5000000 | bytes 6000000 | tf_op jit(solution)/shard_map/end_levels/pallas_call | solution.py:421
  32.6 0.0 collective-permute-done.4.one_edges
  32.6 0.0 collective-permute-done.5.two_edges
  32.6 0.0 collective-permute-done.2.one_rows
  32.6 0.0 collective-permute-done.3.two_rows
  32.6 3.9 %operator.1 = (f32[2,16,128,128]{3,2,1,0:T(8,128)}, f32[3,128,128]{2,1,0:T(8,128)}, f32[128,128]{1,0:T(8,128)S(1)}) custom-call(s32[128,128]{1,0:T(8,128)S(1)} %copy-done.3, f32[65,8,128]{2,1,0:T(8,128)S(1)} %get-tuple-element.30.low, f32[65,8,128]{2,1,0:T(8,128)S(1)} %get-tuple-element.31.high, f32[2,5,128,128]{3,2,1,0:T(8,128)S(1)} %get-tuple-element.32.own_rows, ...), custom_call_target="tpu_custom_call" | custom-call | tf_op jit(solution)/shard_map/operator/pallas_call | solution.py:673
  36.5 18.7 %all_to_all.11 = f32[128,1,128]{2,1,0:T(1,128)} all-to-all(f32[128,1,128]{2,1,0:T(1,128)S(1)} %bitcast.4), channel_id=1, replica_groups=mesh['gx'=16,'gy'=8] {'gx','gy'}, dimensions={0} | all-to-all | bytes 131072 | tf_op jit(solution)/shard_map/all_to_all | solution.py:762
  55.2 1.6 %finish.1 = f32[128,128]{1,0:T(8,128)} custom-call(f32[128,128]{1,0:T(8,128)} %bitcast.5, f32[3,128,128]{2,1,0:T(8,128)} %get-tuple-element.43.fields_in), custom_call_target="tpu_custom_call" | custom-call | tf_op jit(solution)/shard_map/finish/pallas_call | solution.py:727
Async XLA Ops:
  0.6 8.2 %copy-start.3 = (s32[128,128]{1,0:T(8,128)S(1)}, s32[128,128]{1,0:T(8,128)}, u32[]{:S(2)}) copy-start(s32[128,128]{1,0:T(8,128)} %levels.5) | copy-start | bytes 196612
  0.6 8.2 %copy-start.2 = (bf16[16,128,128]{2,1,0:T(8,128)(2,1)S(1)}, bf16[16,128,128]{2,1,0:T(8,128)(2,1)}, u32[]{:S(2)}) copy-start(bf16[16,128,128]{2,1,0:T(8,128)(2,1)} %north.3) | copy-start | bytes 1572868
  0.7 8.2 %copy-start.1 = (bf16[16,128,128]{2,1,0:T(8,128)(2,1)S(1)}, bf16[16,128,128]{2,1,0:T(8,128)(2,1)}, u32[]{:S(2)}) copy-start(bf16[16,128,128]{2,1,0:T(8,128)(2,1)} %east.3) | copy-start | bytes 1572868
  0.7 8.2 %copy-start = (f32[2,16,128,128]{3,2,1,0:T(8,128)S(1)}, f32[2,16,128,128]{3,2,1,0:T(8,128)}, u32[]{:S(2)}) copy-start(f32[2,16,128,128]{3,2,1,0:T(8,128)} %tracers.3) | copy-start | bytes 6291460
  2.0 15.1 %collective-permute-start.1 = (f32[304,128]{1,0:T(8,128)S(1)}, f32[304,128]{1,0:T(8,128)S(1)}, u32[]{:S(2)}, u32[]{:S(2)}) collective-permute-start(f32[304,128]{1,0:T(8,128)S(1)} %get-tuple-element.23.after), channel_id=1, source_target_pairs={{0,120},{8,0},{16,8},{24,16},{32,24},{40,32},{48,40},{56,48},{64,5... | collective-permute-start | bytes 466952 | tf_op jit(solution)/shard_map/ppermute | solution.py:743
  8.9 8.2 %collective-permute-start = (f32[264,128]{1,0:T(8,128)S(1)}, f32[264,128]{1,0:T(8,128)S(1)}, u32[]{:S(2)}, u32[]{:S(2)}) collective-permute-start(f32[264,128]{1,0:T(8,128)S(1)} %get-tuple-element.26), channel_id=1, source_target_pairs={{0,8},{8,16},{16,24},{24,32},{32,40},{40,48},{48,56},{56,64},{64,7... | collective-permute-start | bytes 405512 | tf_op jit(solution)/shard_map/ppermute | solution.py:743
  17.1 15.5 %collective-permute-start.2 = (f32[3,128,128]{2,1,0:T(8,128)S(1)}, f32[3,128,128]{2,1,0:T(8,128)S(1)}, u32[]{:S(2)}, u32[]{:S(2)}) collective-permute-start(f32[3,128,128]{2,1,0:T(8,128)S(1)} %get-tuple-element.34), channel_id=1, source_target_pairs={{0,1},{1,2},{2,3},{3,4},{4,5},{5,6},{6,7},{8,9},{9,10},{10,11},{11... | collective-permute-start | bytes 589832 | tf_op jit(solution)/shard_map/ppermute | solution.py:743
  21.3 11.3 %collective-permute-start.3 = (f32[3,128,128]{2,1,0:T(8,128)S(1)}, f32[3,128,128]{2,1,0:T(8,128)S(1)}, u32[]{:S(2)}, u32[]{:S(2)}) collective-permute-start(f32[3,128,128]{2,1,0:T(8,128)S(1)} %get-tuple-element.35), channel_id=1, source_target_pairs={{1,0},{2,1},{3,2},{4,3},{5,4},{6,5},{7,6},{9,8},{10,9},{11,10},{12... | collective-permute-start | bytes 589832 | tf_op jit(solution)/shard_map/ppermute | solution.py:743
  23.8 8.7 %collective-permute-start.4 = (f32[3,16,128]{2,1,0:T(8,128)S(1)}, f32[3,16,128]{2,1,0:T(8,128)S(1)}, u32[]{:S(2)}, u32[]{:S(2)}) collective-permute-start(f32[3,16,128]{2,1,0:T(8,128)S(1)} %get-tuple-element.36), channel_id=1, source_target_pairs={{0,1},{1,2},{2,3},{3,4},{4,5},{5,6},{6,7},{8,9},{9,10},{10,11},{11... | collective-permute-start | bytes 73736 | tf_op jit(solution)/shard_map/ppermute | solution.py:743
  27.5 5.1 %collective-permute-start.5 = (f32[3,16,128]{2,1,0:T(8,128)S(1)}, f32[3,16,128]{2,1,0:T(8,128)S(1)}, u32[]{:S(2)}, u32[]{:S(2)}) collective-permute-start(f32[3,16,128]{2,1,0:T(8,128)S(1)} %get-tuple-element.37), channel_id=1, source_target_pairs={{1,0},{2,1},{3,2},{4,3},{5,4},{6,5},{7,6},{9,8},{10,9},{11,10},{12... | collective-permute-start | bytes 73736 | tf_op jit(solution)/shard_map/ppermute | solution.py:743

commit v6 on v5

--- a/solution.py
+++ b/solution.py
@@ -23,17 +23,18 @@
 VMEM = 40 * 1024 * 1024
 GROUPS = tuple(range(LOW, LOW + WIDE, 8))
 OUTSIDE = (LOW - 8, LOW + WIDE)
-BATCHES = (GROUPS[:6], GROUPS[6:12], GROUPS[12:])
 INNER = GROUPS[1:-1]
-INNER_BATCHES = (INNER[:6], INNER[6:11], INNER[11:])
-ENDS = (GROUPS[0], GROUPS[1], GROUPS[-2], GROUPS[-1])
-END_BATCHES = (GROUPS[:3] + GROUPS[-3:],)
-END_OUTSIDE = (GROUPS[0] - 8, GROUPS[3], GROUPS[-4], GROUPS[-1] + 8)
+END_GROUPS = (8, 24, 32)
+END_ROWS = 48
 SENT = 3
 
 
 def params():
     return pltpu.CompilerParams(vmem_limit_bytes=VMEM)
+
+
+def is_even(axis):
+    return lax.rem(lax.axis_index(axis), 2) == 0
 
 
 def rows_at(row):
@@ -65,9 +66,10 @@
 NEXT_AT, NEXT_ROWS = offsets(NEXT)
 BEFORE_AT, BEFORE_ROWS = offsets(BEFORE)
 BEFORE_ROWS += 8
-
-
-def edges_kernel(t, e, n, d, before, after, tiles, flows, depths, sems):
+assert NEXT_ROWS <= BEFORE_ROWS
+
+
+def edges_kernel(t, e, n, d, first_pair, second_pair, tiles, flows, depths, sems):
     copies = []
     for side, at in enumerate((0, SX - 8)):
         at16 = 0 if side == 0 else SX - 16
@@ -81,24 +83,35 @@
     copies = [pltpu.make_async_copy(src, dst, sems.at[i]) for i, (src, dst) in enumerate(copies)]
     for copy in copies:
         copy.start()
-    for side, (out, starts, counts) in enumerate(((before, BEFORE_AT, BEFORE), (after, NEXT_AT, NEXT))):
-        for i in range(5):
-            copies[5 * side + i].wait()
-        out[0:8, :] = depths[side].astype(F32)
-        for a in range(4):
-            for k in range(KL):
-                value = tiles[side, a, k] if a < 2 else flows[side, a - 2, k].astype(F32)[8 * side : 8 * side + 8]
-                from_row = 0 if side == 0 else 8 - counts[a]
-                at = starts[a] + counts[a] * k
-                out[at : at + counts[a], :] = value[from_row : from_row + counts[a]]
-    before[BEFORE_ROWS - 8 : BEFORE_ROWS, :] = jnp.zeros((8, 128), F32)
+    for copy in copies:
+        copy.wait()
+
+    def write(before, after):
+        for side, (out, starts, counts) in enumerate(((before, BEFORE_AT, BEFORE), (after, NEXT_AT, NEXT))):
+            out[0:8, :] = depths[side].astype(F32)
+            for a in range(4):
+                for k in range(KL):
+                    value = tiles[side, a, k] if a < 2 else flows[side, a - 2, k].astype(F32)[8 * side : 8 * side + 8]
+                    from_row = 0 if side == 0 else 8 - counts[a]
+                    at = starts[a] + counts[a] * k
+                    out[at : at + counts[a], :] = value[from_row : from_row + counts[a]]
+        before[BEFORE_ROWS - 8 : BEFORE_ROWS, :] = jnp.zeros((8, 128), F32)
+        after[NEXT_ROWS:BEFORE_ROWS, :] = jnp.zeros((BEFORE_ROWS - NEXT_ROWS, 128), F32)
+
+    @pl.when(is_even("gx"))
+    def _():
+        write(second_pair, first_pair)
+
+    @pl.when(~is_even("gx"))
+    def _():
+        write(first_pair, second_pair)
 
 
 def edges(tracers, east, north, levels):
     return pl.pallas_call(
         edges_kernel,
         in_specs=[pl.BlockSpec(memory_space=pltpu.HBM)] * 4,
-        out_shape=[pltpu.VMEM((rows, SY), F32) for rows in (BEFORE_ROWS, NEXT_ROWS)],
+        out_shape=[pltpu.VMEM((BEFORE_ROWS, SY), F32)] * 2,
         scratch_shapes=[
             pltpu.VMEM((2, 2, KL, 8, SY), F32),
             pltpu.VMEM((2, 2, KL, 16, SY), jnp.bfloat16),
@@ -176,21 +189,21 @@
     return a, b, pltpu.roll(c, 124, 1), c, depth
 
 
-def pack_all(sources, depths, rows, own, own_rows, sent_one, sent_two, sent_rows):
+def pack_all(sources, depths, rows, own, own_rows, first_pair, second_pair, sent_rows):
     packed = [pack(source, rows, a < 2) for a, source in enumerate(sources)] + [depths]
     for which in range(2):
         for a in range(5):
             own[which, a, own_rows, :] = packed[a][which]
-    for sent, values in (
-        (sent_one, merge_one(*(p[0] for p in packed))),
-        (sent_two, merge_two(*(p[1] for p in packed))),
-    ):
-        for a in range(SENT):
-            sent[a, sent_rows, :] = values[a]
+    even = is_even("gy")
+    ones = merge_one(*(p[0] for p in packed))
+    twos = merge_two(*(p[1] for p in packed))
+    for a in range(SENT):
+        first_pair[a, sent_rows, :] = jnp.where(even, ones[a], twos[a])
+        second_pair[a, sent_rows, :] = jnp.where(even, twos[a], ones[a])
 
 
 def pack_block(t, e, n, d, own, one, two):
-    chunk = 16
+    chunk = 32
     groups = range(0, SX, 8)
     for g, pair in zip(groups, pack_depth([d[rows_at(g), :].astype(F32) for g in groups]), strict=True):
         for which in range(2):
@@ -211,8 +224,14 @@
     lax.fori_loop(0, SX // chunk, body, 0)
 
 
-def pack_edges_kernel(low_in, high_in, after, own, one, two, low, high):
+def pack_edges_kernel(first_pair, second_pair, after, own, one, two, low, high, low_in, high_in):
     del after
+    even = is_even("gx")
+    for at in range(0, BEFORE_ROWS, 8):
+        rows = rows_at(at)
+        value, other = first_pair[rows, :], second_pair[rows, :]
+        low_in[rows, :] = jnp.where(even, other, value)
+        high_in[rows, :] = jnp.where(even, value, other)
     for a in range(5):
         for k in range(KL if a < 4 else 1):
             low[KL * a + k] = low_tile(low_in, a, k)
@@ -230,6 +249,7 @@
         pack_edges_kernel,
         in_specs=[pl.BlockSpec(memory_space=pltpu.VMEM)] * 2 + [pl.BlockSpec(memory_space=pl.ANY)],
         out_shape=[jax.ShapeDtypeStruct((2, 5, 2 * EDGE, 128), F32), sent, sent, halo, halo],
+        scratch_shapes=[pltpu.VMEM((BEFORE_ROWS, SY), F32)] * 2,
         compiler_params=params(),
         name="pack_edges",
     )(low, high, after)
@@ -242,41 +262,46 @@
     return ahead, back
 
 
-def set_weights(batches, depth_at, face_east, face_north, flow, coef, threshold, south):
-    for batch in batches:
-        a_north, b_north = {}, {}
-        for g in batch:
-            rows = rows_at(g)
-            a_east, b_east = face_weights(face_east(g), flow[0, rows, :], threshold)
-            a_north[g], b_north[g] = face_weights(face_north(g), flow[1, rows, :], threshold)
-            coef[0, rows, :] = a_east
-            coef[1, rows, :] = b_east
-            coef[2, rows, :] = b_north[g]
-        a_south = {g: back_one(a_north[g]) for g in batch}
-        b_south = {g: back_one(b_north[g]) for g in batch}
-        for g in batch:
-            rows = rows_at(g)
-            a_here, b_here = south(g, a_south[g], b_south[g])
-            coef[3, rows, :] = a_here
-            leaving = coef[0, rows, :] + a_north[g] + coef[1, rows_at(g - 1), :] + b_here
-            coef[4, rows, :] = jnp.where(depth_at(g) > threshold, 1.0 - leaving, 0.0)
-
-
-def update(source, coef, batch, south_value=None):
-    ahead = {g: ahead_one(source[rows_at(g), :]) for g in batch}
-    back = {g: back_one(source[rows_at(g), :]) for g in batch}
-    result = {}
-    for g in batch:
-        rows = rows_at(g)
-        south = back[g] if south_value is None else south_value(g, back[g])
-        result[g] = (
-            coef[4, rows, :] * source[rows, :]
-            + coef[1, rows, :] * source[rows_at(g + 1), :]
-            + coef[0, rows_at(g - 1), :] * source[rows_at(g - 1), :]
-            + coef[2, rows, :] * ahead[g]
-            + coef[3, rows, :] * south
+def two_steps(copies, groups, threshold, depth_at, faces, flow, coef, q0, q1, first_row=None):
+    parts = [(c, g) for c in range(copies) for g in groups]
+    every = [(c, t, g) for c, g in parts for t in range(2)]
+    for c, g in parts:
+        rows = rows_at(g)
+        east, north = faces(c, g)
+        coef[c, 0, rows, :], coef[c, 1, rows, :] = face_weights(east, flow[c, 0, rows, :], threshold(c))
+        coef[c, 3, rows, :], coef[c, 2, rows, :] = face_weights(north, flow[c, 1, rows, :], threshold(c))
+    b_south = {(c, g): back_one(coef[c, 2, rows_at(g), :]) for c, g in parts}
+
+    def shifted(source):
+        ahead = {(c, t, g): ahead_one(source[c, t, rows_at(g), :]) for c, t, g in every}
+        behind = {
+            (c, t, g): back_one(coef[c, 3, rows_at(g), :] * source[c, t, rows_at(g), :]) for c, t, g in every
+        }
+        return ahead, behind
+
+    def combine(source, c, t, g, ahead, behind):
+        rows = rows_at(g)
+        return (
+            coef[c, 4, rows, :] * source[c, t, rows, :]
+            + coef[c, 1, rows, :] * source[c, t, rows_at(g + 1), :]
+            + coef[c, 0, rows_at(g - 1), :] * source[c, t, rows_at(g - 1), :]
+            + coef[c, 2, rows, :] * ahead
+            + behind
         )
-    return result
+
+    ahead, behind = shifted(q0)
+    for c, g in parts:
+        rows = rows_at(g)
+        b_here = b_south[c, g]
+        if first_row is not None:
+            b_here, behind[c, 0, g], behind[c, 1, g] = first_row(c, g, b_here, behind[c, 0, g], behind[c, 1, g])
+        leaving = coef[c, 0, rows, :] + coef[c, 3, rows, :] + coef[c, 1, rows_at(g - 1), :] + b_here
+        coef[c, 4, rows, :] = jnp.where(depth_at(c, g) > threshold(c), 1.0 - leaving, 0.0)
+        for t in range(2):
+            q1[c, t, rows, :] = combine(q0, c, t, g, ahead[c, t, g], behind[c, t, g])
+    ahead, behind = shifted(q1)
+    for c, g in parts:
+        yield c, g, *(combine(q1, c, t, g, ahead[c, t, g], behind[c, t, g]) for t in range(2))
 
 
 def halo_depth(levels, low, high, depth):
@@ -293,31 +318,8 @@
         depth[rows_at(outside), :] = jnp.zeros((8, 128), F32)
 
 
-def every_level(batches, results, load, store, depth, face, q0, q1, flow, coef):
-    def level(k, carry):
-        load(k)
-        set_weights(
-            batches,
-            lambda g: depth[rows_at(g), :],
-            lambda g: face[0, rows_at(g), :],
-            lambda g: face[1, rows_at(g), :],
-            flow,
-            coef,
-            k.astype(F32),
-            lambda g, a, b: (a, b),
-        )
-        for tracer in range(2):
-            for batch in batches:
-                for g, value in update(q0.at[tracer], coef, batch).items():
-                    q1[tracer, rows_at(g), :] = value
-        for batch in results:
-            temperature = update(q1.at[0], coef, batch)
-            salinity = update(q1.at[1], coef, batch)
-            for g in batch:
-                store(k, g, temperature[g], salinity[g])
-        return carry
-
-    lax.fori_loop(0, KL, level, 0)
+LEVELS = 2
+END_LEVELS = 4
 
 
 def set_faces(groups, depth, face):
@@ -330,9 +332,11 @@
         face[1, rows, :] = jnp.where(lane == 127, 0.0, jnp.minimum(here, ahead[g]))
 
 
-def block_kernel(tracers, east, north, levels, after, own, one, two, new, total, depth, face, q0, q1, flow, coef):
+def block_kernel(
+    tracers, east, north, levels, after, own, first_pair, second_pair, new, total, depth, face, q0, q1, flow, coef
+):
     del after
-    pack_block(tracers, east, north, levels, own, one, two)
+    pack_block(tracers, east, north, levels, own, first_pair, second_pair)
     blank = jnp.zeros((8, 128), F32)
     for g in INNER:
         depth[rows_at(g), :] = levels[rows_at(g - PAD), :].astype(F32)
@@ -340,27 +344,42 @@
     for g in (GROUPS[0], GROUPS[-1]):
         depth[rows_at(g), :] = blank
         total[rows_at(g), :] = blank
-        for i in range(2):
-            coef[i, rows_at(g), :] = blank
-            q0[i, rows_at(g), :] = blank
-            q1[i, rows_at(g), :] = blank
+        for c in range(LEVELS):
+            for i in range(2):
+                coef[c, i, rows_at(g), :] = blank
+                q0[c, i, rows_at(g), :] = blank
+                q1[c, i, rows_at(g), :] = blank
     set_faces(INNER, depth, face)
 
-    def load(k):
-        for tracer in range(2):
-            q0[tracer, PAD : PAD + SX, :] = tracers[tracer, k]
-        flow[0, PAD : PAD + SX, :] = east[k].astype(F32)
-        flow[1, PAD : PAD + SX, :] = north[k].astype(F32)
-
-    def store(k, g, temperature, salinity):
-        new[0, k, rows_at(g - PAD), :] = temperature
-        new[1, k, rows_at(g - PAD), :] = salinity
-        total[rows_at(g), :] += temperature - 0.8 * salinity
-
-    every_level(INNER_BATCHES, INNER_BATCHES, load, store, depth, face, q0, q1, flow, coef)
-
-
-LEVEL_SCRATCH = [pltpu.VMEM(shape + (ROWS, 128), F32) for shape in ((), (2,), (2,), (2,), (2,), (5,))]
+    def some_levels(i, carry):
+        for c in range(LEVELS):
+            k = LEVELS * i + c
+            for t in range(2):
+                q0[c, t, PAD : PAD + SX, :] = tracers[t, k]
+            flow[c, 0, PAD : PAD + SX, :] = east[k].astype(F32)
+            flow[c, 1, PAD : PAD + SX, :] = north[k].astype(F32)
+        for c, g, temperature, salinity in two_steps(
+            LEVELS,
+            INNER,
+            lambda c: (LEVELS * i + c).astype(F32),
+            lambda c, g: depth[rows_at(g), :],
+            lambda c, g: (face[0, rows_at(g), :], face[1, rows_at(g), :]),
+            flow,
+            coef,
+            q0,
+            q1,
+        ):
+            new[0, LEVELS * i + c, rows_at(g - PAD), :] = temperature
+            new[1, LEVELS * i + c, rows_at(g - PAD), :] = salinity
+            total[rows_at(g), :] += temperature - 0.8 * salinity
+        return carry
+
+    lax.fori_loop(0, KL // LEVELS, some_levels, 0)
+
+
+def level_scratch(rows, copies):
+    shapes = ((), (2,), (copies, 2), (copies, 2), (copies, 2), (copies, 5))
+    return [pltpu.VMEM(shape + (rows, 128), F32) for shape in shapes]
 
 
 def block(tracers, east, north, levels, after):
@@ -375,7 +394,7 @@
             pltpu.VMEM(tracers.shape, F32),
             pltpu.VMEM((ROWS, 128), F32),
         ],
-        scratch_shapes=LEVEL_SCRATCH,
+        scratch_shapes=level_scratch(ROWS, LEVELS),
         compiler_params=params(),
         cost_estimate=pl.CostEstimate(flops=20_000_000, bytes_accessed=24_000_000, transcendentals=0),
         name="block",
@@ -384,44 +403,61 @@
 
 def ends_kernel(tracers, east, north, levels, low, high, new, total, depth, face, q0, q1, flow, coef):
     blank = jnp.zeros((8, 128), F32)
-    halo_depth(levels, low, high, depth)
-    set_faces(END_BATCHES[0], depth, face)
-    for g in ENDS:
-        total[rows_at(g), :] = blank
-    for at in END_OUTSIDE:
-        for i in range(2):
-            coef[i, rows_at(at), :] = blank
-            q0[i, rows_at(at), :] = blank
-            q1[i, rows_at(at), :] = blank
-
-    def load(k):
-        for g, ref in ((GROUPS[0], low), (GROUPS[-1], high)):
-            for i in range(2):
-                q0[i, rows_at(g), :] = ref[KL * i + k]
-                flow[i, rows_at(g), :] = ref[KL * (2 + i) + k]
-        for at in (0, SX - 16):
-            rows = slice(at, at + 16)
-            out = slice(PAD + at, PAD + at + 16)
-            for tracer in range(2):
-                q0[tracer, out, :] = tracers[tracer, k, rows, :]
-            flow[0, out, :] = east[k, rows, :].astype(F32)
-            flow[1, out, :] = north[k, rows, :].astype(F32)
-
-    def store(k, g, temperature, salinity):
-        if g == ENDS[1] or g == ENDS[2]:
-            rows = rows_at(0 if g == ENDS[1] else 8)
-            new[0, k, rows, :] = temperature
-            new[1, k, rows, :] = salinity
-        total[rows_at(g), :] += temperature - 0.8 * salinity
-
-    every_level(END_BATCHES, (ENDS,), load, store, depth, face, q0, q1, flow, coef)
+    for g in range(0, END_ROWS, 8):
+        rows = rows_at(g)
+        depth[rows, :] = blank
+        total[rows, :] = blank
+        if g not in END_GROUPS:
+            for c in range(END_LEVELS):
+                for i in range(2):
+                    coef[c, i, rows, :] = blank
+                    q0[c, i, rows, :] = blank
+                    q1[c, i, rows, :] = blank
+    depth[8:12, :] = low[4 * KL, 4:8, :]
+    depth[12:16, :] = levels[0:8, :].astype(F32)[0:4]
+    depth[24:32, :] = levels[SX - 8 : SX, :].astype(F32)
+    depth[32:40, :] = high[4 * KL]
+    set_faces(END_GROUPS, depth, face)
+
+    def some_levels(i, carry):
+        for c in range(END_LEVELS):
+            k = END_LEVELS * i + c
+            for t in range(2):
+                q0[c, t, 8:12, :] = low[KL * t + k, 4:8, :]
+                q0[c, t, 12:16, :] = tracers[t, k, 0:4, :]
+                q0[c, t, 24:32, :] = tracers[t, k, SX - 8 : SX, :]
+                q0[c, t, 32:40, :] = high[KL * t + k]
+            for t, field in enumerate((east, north)):
+                flow[c, t, 8:12, :] = low[KL * (2 + t) + k, 4:8, :]
+                flow[c, t, 12:16, :] = field[k, 0:16, :].astype(F32)[0:4]
+                flow[c, t, 24:32, :] = field[k, SX - 16 : SX, :].astype(F32)[8:16]
+                flow[c, t, 32:40, :] = high[KL * (2 + t) + k]
+        for c, g, temperature, salinity in two_steps(
+            END_LEVELS,
+            END_GROUPS,
+            lambda c: (END_LEVELS * i + c).astype(F32),
+            lambda c, g: depth[rows_at(g), :],
+            lambda c, g: (face[0, rows_at(g), :], face[1, rows_at(g), :]),
+            flow,
+            coef,
+            q0,
+            q1,
+        ):
+            if g < 32:
+                rows = rows_at(0 if g == 8 else 8)
+                new[0, END_LEVELS * i + c, rows, :] = temperature
+                new[1, END_LEVELS * i + c, rows, :] = salinity
+            total[rows_at(g), :] += temperature - 0.8 * salinity
+        return carry
+
+    lax.fori_loop(0, KL // END_LEVELS, some_levels, 0)
 
 
 def end_levels(tracers, east, north, levels, low, high):
     return pl.pallas_call(
         ends_kernel,
-        out_shape=[pltpu.VMEM((2, KL, 16, SY), F32), pltpu.VMEM((ROWS, 128), F32)],
-        scratch_shapes=LEVEL_SCRATCH,
+        out_shape=[pltpu.VMEM((2, KL, 16, SY), F32), pltpu.VMEM((END_ROWS, 128), F32)],
+        scratch_shapes=level_scratch(END_ROWS, END_LEVELS),
         compiler_params=params(),
         cost_estimate=pl.CostEstimate(flops=5_000_000, bytes_accessed=6_000_000, transcendentals=0),
         name="end_levels",
@@ -429,10 +465,11 @@
 
 
 def operator_kernel(
-    levels, low, high, own_rows, own_edges, one_rows, two_rows, one_edges, two_edges,
+    levels, low, high, own_rows, own_edges, first_rows, second_rows, first_edges, second_edges,
     blocked, ends, wall_total, ends_total,
     new, fields, sums,
-    depth, strip_q, strip_depth, strip_face, strip_flow, strip_total, first_q, coef, total, field, grid, staged, sems, *, count,
+    depth, q0, q1, strip_depth, strip_face, strip_flow, strip_total, first_q, coef, wall, total, field, grid, staged, sems,
+    *, count,
 ):
     lane = lanes()
     member = lane % 8
@@ -449,23 +486,24 @@
             return own_edges[which, a, rows_at(8), :]
         return own_rows[which, a, rows_at(r - EDGE), :]
 
-    def sent(of_rows, of_edges, g):
+    even = is_even("gy")
+
+    def sent(g):
         r = g - LOW
         if r < EDGE:
-            ref, rows = of_edges, rows_at(0)
+            refs, rows = (first_edges, second_edges), rows_at(0)
         elif r >= WIDE - EDGE:
-            ref, rows = of_edges, rows_at(8)
+            refs, rows = (first_edges, second_edges), rows_at(8)
         else:
-            ref, rows = of_rows, rows_at(r - EDGE)
-        return [ref[a, rows, :] for a in range(SENT)]
+            refs, rows = (first_rows, second_rows), rows_at(r - EDGE)
+        pairs = [(refs[0][a, rows, :], refs[1][a, rows, :]) for a in range(SENT)]
+        return [jnp.where(even, b, a) for a, b in pairs], [jnp.where(even, a, b) for a, b in pairs]
 
     halo_depth(levels, low, high, depth)
     parts = {}
     for g in GROUPS:
-        parts[g] = (
-            list(split_one(*sent(one_rows, one_edges, g))),
-            list(split_two(*sent(two_rows, two_edges, g))),
-        )
+        from_low, from_high = sent(g)
+        parts[g] = list(split_one(*from_low)), list(split_two(*from_high))
     for g in GROUPS:
         rows = rows_at(g)
         from_low, from_high = parts[g]
@@ -476,7 +514,7 @@
             high_strip = jnp.where(member >= 3, from_high[a], own(1, a, g))
             for side, value in enumerate((low_strip, high_strip)):
                 if a < 2:
-                    strip_q[side, a, 0, rows, :] = value
+                    q0[side, a, rows, :] = value
                 elif a < 4:
                     strip_flow[side, a - 2, rows, :] = value
                 else:
@@ -492,46 +530,38 @@
         strip_face[side, rows_at(g), :] = jnp.minimum(strip_depth[side, rows_at(g), :], value)
 
     for side in range(2):
-        at = strip_depth.at[side]
-
-        def south(g, a_south, b_south, side=side):
-            if side == 1:
-                face = jnp.minimum(own(0, 4, g), own(1, 4, g))
-                a_first, b_first = face_weights(face, own(0, 3, g), strip_level)
-                a_south = jnp.where(member == 0, a_first, a_south)
-                b_south = jnp.where(member == 0, b_first, b_south)
-            return a_south, b_south
-
-        coef[1, rows_at(LOW - 8), :] = blank
-        set_weights(
-            BATCHES,
-            lambda g, at=at: at[rows_at(g), :],
-            lambda g, at=at: jnp.minimum(at[rows_at(g), :], at[rows_at(g + 1), :]),
-            lambda g, side=side: strip_face[side, rows_at(g), :],
-            strip_flow.at[side],
-            coef,
-            strip_level,
-            south,
+        for i in range(2):
+            coef[side, i, rows_at(LOW - 8), :] = blank
+
+    def first_row(side, g, b_south, *behind):
+        if side == 0:
+            return b_south, *behind
+        face = jnp.minimum(own(0, 4, g), own(1, 4, g))
+        a_first, b_first = face_weights(face, own(0, 3, g), strip_level)
+        return (
+            jnp.where(member == 0, b_first, b_south),
+            *(jnp.where(member == 0, a_first * own(0, t, g), behind[t]) for t in range(2)),
         )
-        for tracer in range(2):
-            source = strip_q.at[side, tracer, 0]
-            from_own = None
-            if side == 1:
-
-                def from_own(g, value, tracer=tracer):
-                    return jnp.where(member == 0, own(0, tracer, g), value)
-
-            for batch in BATCHES:
-                for g, value in update(source, coef, batch, from_own).items():
-                    strip_q[side, tracer, 1, rows_at(g), :] = value
-        for batch in BATCHES:
-            temperature = update(strip_q.at[side, 0, 1], coef, batch)
-            salinity = update(strip_q.at[side, 1, 1], coef, batch)
-            for g in batch:
-                rows = rows_at(g)
-                strip_q[side, 0, 0, rows, :] = temperature[g]
-                strip_q[side, 1, 0, rows, :] = salinity[g]
-                strip_total[side, rows, :] = temperature[g] - 0.8 * salinity[g]
+
+    for side, g, temperature, salinity in two_steps(
+        2,
+        GROUPS,
+        lambda side: strip_level,
+        lambda side, g: strip_depth[side, rows_at(g), :],
+        lambda side, g: (
+            jnp.minimum(strip_depth[side, rows_at(g), :], strip_depth[side, rows_at(g + 1), :]),
+            strip_face[side, rows_at(g), :],
+        ),
+        strip_flow,
+        coef,
+        q0,
+        q1,
+        first_row,
+    ):
+        rows = rows_at(g)
+        q0[side, 0, rows, :] = temperature
+        q0[side, 1, rows, :] = salinity
+        strip_total[side, rows, :] = temperature - 0.8 * salinity
     for turn in (8, 16, 32, 64):
         values = {}
         for side in range(2):
@@ -544,9 +574,10 @@
     for tracer in range(2):
         for g in range(PAD, PAD + SX, 8):
             rows = rows_at(g)
-            high_value = pltpu.roll(strip_q[1, tracer, 0, rows, :], 1, 1)
-            first_q[tracer, rows, :] = jnp.where(member >= 4, strip_q[0, tracer, 0, rows, :], high_value)
+            high_value = pltpu.roll(q0[1, tracer, rows, :], 1, 1)
+            first_q[tracer, rows, :] = jnp.where(member >= 4, q0[0, tracer, rows, :], high_value)
     from_strip = (lane < 2) | (lane >= 126)
+    row = lax.broadcasted_iota(jnp.int32, (8, 128), 0)
 
     def place(k, carry):
         turn = 124 - 8 * k
@@ -554,10 +585,11 @@
             values = {g: pltpu.roll(first_q[tracer, rows_at(g + PAD), :], turn, 1) for g in range(0, SX, 8)}
             for g, value in values.items():
                 rows = rows_at(g)
-                if g == 0 or g == SX - 8:
-                    here = ends[tracer, k, rows_at(0 if g == 0 else 8), :]
-                else:
-                    here = blocked[tracer, k, rows, :]
+                here = blocked[tracer, k, rows, :]
+                if g == 0:
+                    here = jnp.where(row < 2, ends[tracer, k, rows_at(4), :], here)
+                elif g == SX - 8:
+                    here = jnp.where(row >= 6, ends[tracer, k, rows_at(8), :], here)
                 staged[tracer, k, rows, :] = jnp.where(from_strip, value, here)
         for tracer in range(2):
             pltpu.make_async_copy(staged.at[tracer, k], new.at[tracer, k], sems.at[0]).start()
@@ -576,6 +608,10 @@
         a, b = back_one(main), back_one(side)
         return jnp.where(lane == 0, b, a), jnp.where(lane == 0, a, b)
 
+    for g in GROUPS:
+        wall[rows_at(g), :] = wall_total[rows_at(g), :]
+    wall[PAD - 2 : PAD + 2, :] = ends_total[10:14, :]
+    wall[PAD + SX - 2 : PAD + SX + 3, :] = ends_total[30:35, :]
     for g in GROUPS + OUTSIDE:
         rows = rows_at(g)
         grid[0, 0, rows, :] = depth[rows, :]
@@ -590,8 +626,7 @@
         low_total = pltpu.roll(strip_total[0, rows, :], 4, 1)
         high_total = pltpu.roll(strip_total[1, rows, :], 5, 1)
         edge_total = jnp.where(lane < 64, low_total, high_total)
-        here = (ends_total if g in ENDS else wall_total)[rows, :]
-        total[0, rows, :] = jnp.where(from_strip, edge_total, here)
+        total[0, rows, :] = jnp.where(from_strip, edge_total, wall[rows, :])
         total[1, rows, :] = jnp.where(lane >= 64, low_total, high_total)
     for part in range(2):
         grid[1, part, rows_at(LOW - 8), :] = blank
@@ -645,12 +680,12 @@
                     )
                     field[i + 1, part, rows, :] = image * grid[3, part, rows, :]
         pltpu.make_async_copy(field.at[i, 0, PAD : PAD + SX, :], fields.at[i], sems.at[1]).start()
-    row = jnp.zeros((8, 128), F32)
+    sums_row = jnp.zeros((8, 128), F32)
     for i in range(6):
         value = jnp.sum(jnp.sum(moments[i], axis=0, keepdims=True), axis=1, keepdims=True)
-        row = jnp.where(lane == i, value, row)
+        sums_row = jnp.where(lane == i, value, sums_row)
     for g in range(0, 128, 8):
-        sums[rows_at(g), :] = row
+        sums[rows_at(g), :] = sums_row
     pltpu.make_async_copy(field.at[:, 0, PAD : PAD + SX, :], fields, sems.at[1]).wait()
     pltpu.make_async_copy(staged, new, sems.at[0]).wait()
 
@@ -659,13 +694,15 @@
     tall = (ROWS, 128)
     scratch = (
         (),
-        (2, 2, 2),
+        (2, 2),
+        (2, 2),
         (2,),
         (2,),
         (2, 2),
         (2,),
         (2,),
-        (5,),
+        (2, 5),
+        (),
         (2,),
         (3, 2),
         (6, 2),
@@ -737,26 +774,32 @@
     )(sums, pltpu.with_memory_space_constraint(fields, pltpu.HBM))
 
 
-def shift(array, axis, step, around):
+def first_pairs(array, axis):
+    return lax.ppermute(array, axis, [(i, i ^ 1) for i in range(lax.axis_size(axis))])
+
+
+def second_pairs(array, axis, around):
     count = lax.axis_size(axis)
-    pairs = [(i, (i + step) % count) for i in range(count) if around or 0 <= i + step < count]
+    pairs = [] if around else [(0, 0), (count - 1, count - 1)]
+    for i in range(1, count if around else count - 1, 2):
+        pairs += [(i, (i + 1) % count), ((i + 1) % count, i)]
     return lax.ppermute(array, axis, pairs)
 
 
 def on_device(tracers, east, north, levels):
-    to_before, to_after = edges(tracers, east, north, levels)
-    before = shift(to_before, "gx", -1, True)
-    after = shift(to_after, "gx", 1, True)
-    own_rows, one, two, blocked, total = block(tracers, east, north, levels, to_before)
-    one, two, after, before = lax.optimization_barrier((one, two, after, before))
-    one_rows = shift(one, "gy", 1, False)
-    two_rows = shift(two, "gy", -1, False)
-    own_edges, one, two, low, high = pack_edges(after, before, total)
-    one_edges = shift(one, "gy", 1, False)
-    two_edges = shift(two, "gy", -1, False)
+    to_first, to_second = edges(tracers, east, north, levels)
+    first = first_pairs(to_first, "gx")
+    second = second_pairs(to_second, "gx", True)
+    own_rows, one, two, blocked, total = block(tracers, east, north, levels, to_first)
+    one, two, first, second = lax.optimization_barrier((one, two, first, second))
+    first_rows = first_pairs(one, "gy")
+    second_rows = second_pairs(two, "gy", False)
+    own_edges, one, two, low, high = pack_edges(first, second, total)
+    first_edges = first_pairs(one, "gy")
+    second_edges = second_pairs(two, "gy", False)
     ends, ends_total = end_levels(tracers, east, north, levels, low, high)
     new, fields, sums = operator(
-        levels, low, high, own_rows, own_edges, one_rows, two_rows, one_edges, two_edges,
+        levels, low, high, own_rows, own_edges, first_rows, second_rows, first_edges, second_edges,
         blocked, ends, total, ends_total, count=lax.axis_size("gy"),
     )
     sums = lax.all_to_all(sums, ("gx", "gy"), split_axis=0, concat_axis=0, tiled=True)

time: 57.1 us -> 46.7 us (0.82)
  starting transfers between devices: 18.5 us -> 14.6 us
  Pallas kernels: 18.8 us -> 15 us
  blocking collectives: 18.7 us -> 15.6 us
    ppermute x6, starting transfers between devices: 18.5 us -> 14.6 us  [the longest x3 13.5 us: second_pairs(): return lax.ppermute(array, axis, pairs)]
    all_to_all x1, blocking collectives: 18.7 us -> 15.6 us  [on_device(): lax.all_to_all(sums, ('gx', 'gy'), split_axis=0, concat_axis=0, tiled=True)]
    pallas_call x1, Pallas kernels: 3.15 us -> 1.1 us  [end_levels(): pl.pallas_call(ends_kernel, out_shape=[pltpu.VMEM((2, KL, 16, SY), F32),...]
    pallas_call x1, Pallas kernels: 8.19 us -> 6.48 us  [block(): pl.pallas_call(block_kernel, in_specs=[pl.BlockSpec(memory_space=pltpu.VM...]
  transfers between devices with their start and end apart: 6 -> 6, of which waited for: 0 -> 1; matrix products, arithmetic and copies ran while one was open for 0% -> 0% of each run, Pallas kernels for 21% -> 18%
where the time goes in v6:
time: 46.7 us; the launch traced here: 46.5 us
  blocking collectives  15.6 us (33%)
  Pallas kernels  15 us (32%)
  starting transfers between devices  14.6 us (31%)
  between operations  0.76 us (2%)
    all_to_all x1, blocking collectives, on_device(): lax.all_to_all(sums, ('gx', 'gy'), split_axis=0, concat_axis=0, tiled=True)  15.6 us
    ppermute x3, starting transfers between devices, second_pairs(): return lax.ppermute(array, axis, pairs)  13.5 us
    pallas_call x1, Pallas kernels, block(): pl.pallas_call(block_kernel, in_specs=[pl.BlockSpec(memory_space=pltpu.VM...  6.48 us
    pallas_call x1, Pallas kernels, operator(): pl.pallas_call(functools.partial(operator_kernel, count=count), out_shape...  3.87 us
    pallas_call x1, Pallas kernels, finish(): pl.pallas_call(finish_kernel, in_specs=[pl.BlockSpec(memory_space=pl.ANY)...  1.63 us
    pallas_call x1, Pallas kernels, edges(): pl.pallas_call(edges_kernel, in_specs=[pl.BlockSpec(memory_space=pltpu.HB...  1.36 us
    pallas_call x1, Pallas kernels, end_levels(): pl.pallas_call(ends_kernel, out_shape=[pltpu.VMEM((2, KL, 16, SY), F32),...  1.1 us
    ppermute x3, starting transfers between devices, first_pairs(): lax.ppermute(array, axis, [(i, i ^ 1) for i in range(lax.axis_size(axis))])  1.1 us
  transfers between devices with their start and end apart: 6, of which 1 were waited for; matrix products, arithmetic and copies ran while one was open for 0% of the time, Pallas kernels for 18%

profile of v6, /device:TPU:1, one launch (start us, length us, event | category | flops | bytes accessed | tf_op | source)
XLA Modules:
  0.0 46.5 jit_solution(15012989887717289815)
XLA Ops:
  0.6 0.0 copy-start.3
  0.6 0.0 copy-start.2
  0.7 0.0 copy-start.1
  0.7 0.0 copy-start
  0.7 1.4 %edges.1 = (f32[304,128]{1,0:T(8,128)S(1)}, f32[304,128]{1,0:T(8,128)S(1)}) custom-call(f32[2,16,128,128]{3,2,1,0:T(8,128)} %tracers.3, bf16[16,128,128]{2,1,0:T(8,128)(2,1)} %east.3, bf16[16,128,128]{2,1,0:T(8,128)(2,1)} %north.3, s32[128,128]{1,0:T(8,128)} %levels.5), custom_call_target="tpu_custom_call" | custom-call | tf_op jit(solution)/shard_map/edges/pallas_call | solution.py:111
  2.0 6.9 %collective-permute-start.1 = (f32[304,128]{1,0:T(8,128)S(1)}, f32[304,128]{1,0:T(8,128)S(1)}, u32[]{:S(2)}, u32[]{:S(2)}) collective-permute-start(f32[304,128]{1,0:T(8,128)S(1)} %get-tuple-element.26), channel_id=1, source_target_pairs={{8,16},{16,8},{24,32},{32,24},{40,48},{48,40},{56,64},{64,56},{72,... | collective-permute-start | bytes 466952 | tf_op jit(solution)/shard_map/ppermute | solution.py:786
  8.9 0.0 collective-permute-start
  8.9 0.0 copy-done.3
  8.9 0.0 copy-done.2
  8.9 0.0 copy-done.1
  8.9 0.0 copy-done
  8.9 6.5 %block.1 = (f32[2,5,128,128]{3,2,1,0:T(8,128)S(1)}, f32[3,128,128]{2,1,0:T(8,128)S(1)}, f32[3,128,128]{2,1,0:T(8,128)S(1)}, f32[2,16,128,128]{3,2,1,0:T(8,128)S(1)}, f32[160,128]{1,0:T(8,128)S(1)}) custom-call(f32[2,16,128,128]{3,2,1,0:T(8,128)S(1)} %copy-done, bf16[16,128,128]{2,1,0:T(8,128)(2,1)S(1)} %copy-done.1, bf16[16,128,128]{2,1,0:T(8,128)(2,1)S(1)} %copy-done.2, ...), custom_call_target="tpu_custom_call" | custom-call | flops 20000000 | bytes 24000000 | tf_op jit(solution)/shard_map/block/pallas_call | solution.py:387
  15.4 0.0 collective-permute-done.1.second_pair
  15.4 0.0 collective-permute-done.first_pair
  15.4 1.0 %collective-permute-start.2 = (f32[3,128,128]{2,1,0:T(8,128)S(1)}, f32[3,128,128]{2,1,0:T(8,128)S(1)}, u32[]{:S(2)}, u32[]{:S(2)}) collective-permute-start(f32[3,128,128]{2,1,0:T(8,128)S(1)} %get-tuple-element.34), channel_id=1, source_target_pairs={{0,1},{1,0},{2,3},{3,2},{4,5},{5,4},{6,7},{7,6},{8,9},{9,8},{10,11... | collective-permute-start | bytes 589832 | tf_op jit(solution)/shard_map/ppermute | solution.py:778
  16.5 3.1 %collective-permute-start.3 = (f32[3,128,128]{2,1,0:T(8,128)S(1)}, f32[3,128,128]{2,1,0:T(8,128)S(1)}, u32[]{:S(2)}, u32[]{:S(2)}) collective-permute-start(f32[3,128,128]{2,1,0:T(8,128)S(1)} %get-tuple-element.35), channel_id=1, source_target_pairs={{0,0},{7,7},{1,2},{2,1},{3,4},{4,3},{5,6},{6,5},{8,8},{15,15},{9,1... | collective-permute-start | bytes 589832 | tf_op jit(solution)/shard_map/ppermute | solution.py:786
  19.6 0.6 %pack_edges.1 = (f32[2,5,16,128]{3,2,1,0:T(8,128)S(1)}, f32[3,16,128]{2,1,0:T(8,128)S(1)}, f32[3,16,128]{2,1,0:T(8,128)S(1)}, f32[65,8,128]{2,1,0:T(8,128)S(1)}, f32[65,8,128]{2,1,0:T(8,128)S(1)}) custom-call(f32[304,128]{1,0:T(8,128)S(1)} %collective-permute-done.first_pair, f32[304,128]{1,0:T(8,128)S(1)} %collective-permute-done.1.second_pair, ...), custom_call_target="tpu_custom_call" | custom-call | tf_op jit(solution)/shard_map/pack_edges/pallas_call | solution.py:248
  20.2 0.1 collective-permute-start.4
  20.2 3.6 %collective-permute-start.5 = (f32[3,16,128]{2,1,0:T(8,128)S(1)}, f32[3,16,128]{2,1,0:T(8,128)S(1)}, u32[]{:S(2)}, u32[]{:S(2)}) collective-permute-start(f32[3,16,128]{2,1,0:T(8,128)S(1)} %get-tuple-element.37), channel_id=1, source_target_pairs={{0,0},{7,7},{1,2},{2,1},{3,4},{4,3},{5,6},{6,5},{8,8},{15,15},{9,1... | collective-permute-start | bytes 73736 | tf_op jit(solution)/shard_map/ppermute | solution.py:786
  23.8 1.1 %end_levels.1 = (f32[2,16,16,128]{3,2,1,0:T(8,128)S(1)}, f32[48,128]{1,0:T(8,128)S(1)}) custom-call(f32[2,16,128,128]{3,2,1,0:T(8,128)S(1)} %copy-done, bf16[16,128,128]{2,1,0:T(8,128)(2,1)S(1)} %copy-done.1, bf16[16,128,128]{2,1,0:T(8,128)(2,1)S(1)} %copy-done.2, s32[128,128]{1,0:T(8,128)S(1)} %copy-done.3, f32[65,8,128]{2,1,0:T(8,128)S(1)} %get-tuple-element.30.low, ...), custom_call_target="tpu_custom_call" | custom-call | flops 5000000 | bytes 6000000 | tf_op jit(solution)/shard_map/end_levels/pallas_call | solution.py:457
  24.9 0.0 collective-permute-done.4.first_edges
  24.9 0.4 collective-permute-done.5.second_edges
  25.4 0.0 collective-permute-done.2.first_rows
  25.4 0.0 collective-permute-done.3.second_rows
  25.4 3.9 %operator.1 = (f32[2,16,128,128]{3,2,1,0:T(8,128)}, f32[3,128,128]{2,1,0:T(8,128)}, f32[128,128]{1,0:T(8,128)S(1)}) custom-call(s32[128,128]{1,0:T(8,128)S(1)} %copy-done.3, f32[65,8,128]{2,1,0:T(8,128)S(1)} %get-tuple-element.30.low, f32[65,8,128]{2,1,0:T(8,128)S(1)} %get-tuple-element.31.high, f32[2,5,128,128]{3,2,1,0:T(8,128)S(1)} %get-tuple-element.32.own_rows, ...), custom_call_target="tpu_custom_call" | custom-call | tf_op jit(solution)/shard_map/operator/pallas_call | solution.py:710
  29.3 15.6 %all_to_all.11 = f32[128,1,128]{2,1,0:T(1,128)} all-to-all(f32[128,1,128]{2,1,0:T(1,128)S(1)} %bitcast.4), channel_id=1, replica_groups=mesh['gx'=16,'gy'=8] {'gx','gy'}, dimensions={0} | all-to-all | bytes 131072 | tf_op jit(solution)/shard_map/all_to_all | solution.py:805
  44.9 1.6 %finish.1 = f32[128,128]{1,0:T(8,128)} custom-call(f32[128,128]{1,0:T(8,128)} %bitcast.5, f32[3,128,128]{2,1,0:T(8,128)} %get-tuple-element.43.fields_in), custom_call_target="tpu_custom_call" | custom-call | tf_op jit(solution)/shard_map/finish/pallas_call | solution.py:764
Async XLA Ops:
  0.6 8.3 %copy-start.3 = (s32[128,128]{1,0:T(8,128)S(1)}, s32[128,128]{1,0:T(8,128)}, u32[]{:S(2)}) copy-start(s32[128,128]{1,0:T(8,128)} %levels.5) | copy-start | bytes 196612
  0.6 8.3 %copy-start.2 = (bf16[16,128,128]{2,1,0:T(8,128)(2,1)S(1)}, bf16[16,128,128]{2,1,0:T(8,128)(2,1)}, u32[]{:S(2)}) copy-start(bf16[16,128,128]{2,1,0:T(8,128)(2,1)} %north.3) | copy-start | bytes 1572868
  0.7 8.3 %copy-start.1 = (bf16[16,128,128]{2,1,0:T(8,128)(2,1)S(1)}, bf16[16,128,128]{2,1,0:T(8,128)(2,1)}, u32[]{:S(2)}) copy-start(bf16[16,128,128]{2,1,0:T(8,128)(2,1)} %east.3) | copy-start | bytes 1572868
  0.7 8.3 %copy-start = (f32[2,16,128,128]{3,2,1,0:T(8,128)S(1)}, f32[2,16,128,128]{3,2,1,0:T(8,128)}, u32[]{:S(2)}) copy-start(f32[2,16,128,128]{3,2,1,0:T(8,128)} %tracers.3) | copy-start | bytes 6291460
  2.0 13.4 %collective-permute-start.1 = (f32[304,128]{1,0:T(8,128)S(1)}, f32[304,128]{1,0:T(8,128)S(1)}, u32[]{:S(2)}, u32[]{:S(2)}) collective-permute-start(f32[304,128]{1,0:T(8,128)S(1)} %get-tuple-element.26), channel_id=1, source_target_pairs={{8,16},{16,8},{24,32},{32,24},{40,48},{48,40},{56,64},{64,56},{72,... | collective-permute-start | bytes 466952 | tf_op jit(solution)/shard_map/ppermute | solution.py:786
  8.9 6.5 %collective-permute-start = (f32[304,128]{1,0:T(8,128)S(1)}, f32[304,128]{1,0:T(8,128)S(1)}, u32[]{:S(2)}, u32[]{:S(2)}) collective-permute-start(f32[304,128]{1,0:T(8,128)S(1)} %get-tuple-element.23.after), channel_id=1, source_target_pairs={{0,8},{8,0},{16,24},{24,16},{32,40},{40,32},{48,56},{56,48},{64,72... | collective-permute-start | bytes 466952 | tf_op jit(solution)/shard_map/ppermute | solution.py:778
  15.4 9.9 %collective-permute-start.2 = (f32[3,128,128]{2,1,0:T(8,128)S(1)}, f32[3,128,128]{2,1,0:T(8,128)S(1)}, u32[]{:S(2)}, u32[]{:S(2)}) collective-permute-start(f32[3,128,128]{2,1,0:T(8,128)S(1)} %get-tuple-element.34), channel_id=1, source_target_pairs={{0,1},{1,0},{2,3},{3,2},{4,5},{5,4},{6,7},{7,6},{8,9},{9,8},{10,11... | collective-permute-start | bytes 589832 | tf_op jit(solution)/shard_map/ppermute | solution.py:778
  16.5 8.9 %collective-permute-start.3 = (f32[3,128,128]{2,1,0:T(8,128)S(1)}, f32[3,128,128]{2,1,0:T(8,128)S(1)}, u32[]{:S(2)}, u32[]{:S(2)}) collective-permute-start(f32[3,128,128]{2,1,0:T(8,128)S(1)} %get-tuple-element.35), channel_id=1, source_target_pairs={{0,0},{7,7},{1,2},{2,1},{3,4},{4,3},{5,6},{6,5},{8,8},{15,15},{9,1... | collective-permute-start | bytes 589832 | tf_op jit(solution)/shard_map/ppermute | solution.py:786
  20.2 4.8 %collective-permute-start.4 = (f32[3,16,128]{2,1,0:T(8,128)S(1)}, f32[3,16,128]{2,1,0:T(8,128)S(1)}, u32[]{:S(2)}, u32[]{:S(2)}) collective-permute-start(f32[3,16,128]{2,1,0:T(8,128)S(1)} %get-tuple-element.36), channel_id=1, source_target_pairs={{0,1},{1,0},{2,3},{3,2},{4,5},{5,4},{6,7},{7,6},{8,9},{9,8},{10,11... | collective-permute-start | bytes 73736 | tf_op jit(solution)/shard_map/ppermute | solution.py:778
  20.2 5.1 %collective-permute-start.5 = (f32[3,16,128]{2,1,0:T(8,128)S(1)}, f32[3,16,128]{2,1,0:T(8,128)S(1)}, u32[]{:S(2)}, u32[]{:S(2)}) collective-permute-start(f32[3,16,128]{2,1,0:T(8,128)S(1)} %get-tuple-element.37), channel_id=1, source_target_pairs={{0,0},{7,7},{1,2},{2,1},{3,4},{4,3},{5,6},{6,5},{8,8},{15,15},{9,1... | collective-permute-start | bytes 73736 | tf_op jit(solution)/shard_map/ppermute | solution.py:786

commit v7 on v6

--- a/solution.py
+++ b/solution.py
@@ -224,8 +224,11 @@
     lax.fori_loop(0, SX // chunk, body, 0)
 
 
-def pack_edges_kernel(first_pair, second_pair, after, own, one, two, low, high, low_in, high_in):
-    del after
+def pack_edges_kernel(first_pair, second_pair, first_rows, second_rows, own, one, two, low, high, low_in, high_in):
+    for g in range(0, SX, 8):
+        for a in range(SENT):
+            one[a, rows_at(g + EDGE), :] = first_rows[a, rows_at(g), :]
+            two[a, rows_at(g + EDGE), :] = second_rows[a, rows_at(g), :]
     even = is_even("gx")
     for at in range(0, BEFORE_ROWS, 8):
         rows = rows_at(at)
@@ -239,20 +242,20 @@
     depths = pack_depth([low_tile(low_in, 4, 0), high_tile(high_in, 4, 0)])
     for side, (ref, tile) in enumerate(((low_in, low_tile), (high_in, high_tile))):
         sources = [functools.partial(tile, ref, a) for a in range(4)]
-        pack_all(sources, depths[side], 8, own, rows_at(8 * side), one, two, rows_at(8 * side))
-
-
-def pack_edges(low, high, after):
-    sent = jax.ShapeDtypeStruct((SENT, 2 * EDGE, 128), F32)
+        at = 0 if side == 0 else WIDE - EDGE
+        pack_all(sources, depths[side], 8, own, rows_at(8 * side), one, two, rows_at(at))
+
+
+def pack_edges(first, second, first_rows, second_rows):
+    sent = jax.ShapeDtypeStruct((SENT, WIDE, 128), F32)
     halo = jax.ShapeDtypeStruct((ARRAYS, EDGE, SY), F32)
     return pl.pallas_call(
         pack_edges_kernel,
-        in_specs=[pl.BlockSpec(memory_space=pltpu.VMEM)] * 2 + [pl.BlockSpec(memory_space=pl.ANY)],
         out_shape=[jax.ShapeDtypeStruct((2, 5, 2 * EDGE, 128), F32), sent, sent, halo, halo],
         scratch_shapes=[pltpu.VMEM((BEFORE_ROWS, SY), F32)] * 2,
         compiler_params=params(),
         name="pack_edges",
-    )(low, high, after)
+    )(first, second, first_rows, second_rows)
 
 
 def face_weights(face, flow_value, threshold):
@@ -320,6 +323,7 @@
 
 LEVELS = 2
 END_LEVELS = 4
+PLACED = 8
 
 
 def set_faces(groups, depth, face):
@@ -465,8 +469,7 @@
 
 
 def operator_kernel(
-    levels, low, high, own_rows, own_edges, first_rows, second_rows, first_edges, second_edges,
-    blocked, ends, wall_total, ends_total,
+    levels, low, high, own_rows, own_edges, first_pair, second_pair, blocked, ends, wall_total, ends_total,
     new, fields, sums,
     depth, q0, q1, strip_depth, strip_face, strip_flow, strip_total, first_q, coef, wall, total, field, grid, staged, sems,
     *, count,
@@ -489,14 +492,8 @@
     even = is_even("gy")
 
     def sent(g):
-        r = g - LOW
-        if r < EDGE:
-            refs, rows = (first_edges, second_edges), rows_at(0)
-        elif r >= WIDE - EDGE:
-            refs, rows = (first_edges, second_edges), rows_at(8)
-        else:
-            refs, rows = (first_rows, second_rows), rows_at(r - EDGE)
-        pairs = [(refs[0][a, rows, :], refs[1][a, rows, :]) for a in range(SENT)]
+        rows = rows_at(g - LOW)
+        pairs = [(first_pair[a, rows, :], second_pair[a, rows, :]) for a in range(SENT)]
         return [jnp.where(even, b, a) for a, b in pairs], [jnp.where(even, a, b) for a, b in pairs]
 
     halo_depth(levels, low, high, depth)
@@ -572,30 +569,32 @@
             strip_total[side, rows_at(g), :] = value
 
     for tracer in range(2):
-        for g in range(PAD, PAD + SX, 8):
+        high_values = {g: back_one(q0[1, tracer, rows_at(g), :]) for g in INNER}
+        for g in INNER:
             rows = rows_at(g)
-            high_value = pltpu.roll(q0[1, tracer, rows, :], 1, 1)
-            first_q[tracer, rows, :] = jnp.where(member >= 4, q0[0, tracer, rows, :], high_value)
+            first_q[tracer, rows, :] = jnp.where(member >= 4, q0[0, tracer, rows, :], high_values[g])
     from_strip = (lane < 2) | (lane >= 126)
     row = lax.broadcasted_iota(jnp.int32, (8, 128), 0)
 
-    def place(k, carry):
-        turn = 124 - 8 * k
-        for tracer in range(2):
-            values = {g: pltpu.roll(first_q[tracer, rows_at(g + PAD), :], turn, 1) for g in range(0, SX, 8)}
-            for g, value in values.items():
-                rows = rows_at(g)
-                here = blocked[tracer, k, rows, :]
-                if g == 0:
-                    here = jnp.where(row < 2, ends[tracer, k, rows_at(4), :], here)
-                elif g == SX - 8:
-                    here = jnp.where(row >= 6, ends[tracer, k, rows_at(8), :], here)
-                staged[tracer, k, rows, :] = jnp.where(from_strip, value, here)
-        for tracer in range(2):
-            pltpu.make_async_copy(staged.at[tracer, k], new.at[tracer, k], sems.at[0]).start()
+    def place(i, carry):
+        slots = [(t, PLACED * i + c, c, g) for c in range(PLACED) for t in range(2) for g in range(0, SX, 8)]
+        turned = {
+            (t, c, g): pltpu.roll(first_q[t, rows_at(g + PAD), :], 124 - 8 * k, 1) for t, k, c, g in slots
+        }
+        for t, k, c, g in slots:
+            rows = rows_at(g)
+            here = blocked[t, k, rows, :]
+            if g == 0:
+                here = jnp.where(row < 2, ends[t, k, rows_at(4), :], here)
+            elif g == SX - 8:
+                here = jnp.where(row >= 6, ends[t, k, rows_at(8), :], here)
+            staged[t, k, rows, :] = jnp.where(from_strip, turned[t, c, g], here)
+        at = pl.ds(PLACED * i, PLACED)
+        for t in range(2):
+            pltpu.make_async_copy(staged.at[t, at], new.at[t, at], sems.at[0]).start()
         return carry
 
-    lax.fori_loop(0, KL, place, 0)
+    lax.fori_loop(0, KL // PLACED, place, 0)
 
     def beside(low_value, high_value):
         return jnp.where(lane >= 64, pltpu.roll(low_value, 4, 1), pltpu.roll(high_value, 5, 1))
@@ -616,15 +615,19 @@
         rows = rows_at(g)
         grid[0, 0, rows, :] = depth[rows, :]
         grid[0, 1, rows, :] = beside(strip_depth[0, rows, :], strip_depth[1, rows, :])
+    further_all = {g: northward(grid[0, 0, rows_at(g), :], grid[0, 1, rows_at(g), :]) for g in GROUPS}
+    strip_sums = {
+        g: (pltpu.roll(strip_total[0, rows_at(g), :], 4, 1), pltpu.roll(strip_total[1, rows_at(g), :], 5, 1))
+        for g in GROUPS
+    }
     for g in GROUPS:
         rows = rows_at(g)
         both = grid[0, 0, rows, :], grid[0, 1, rows, :]
-        further = northward(*both)
+        further = further_all[g]
         for part in range(2):
             grid[1, part, rows, :] = jnp.minimum(both[part], grid[0, part, rows_at(g + 1), :])
             grid[2, part, rows, :] = jnp.minimum(both[part], further[part])
-        low_total = pltpu.roll(strip_total[0, rows, :], 4, 1)
-        high_total = pltpu.roll(strip_total[1, rows, :], 5, 1)
+        low_total, high_total = strip_sums[g]
         edge_total = jnp.where(lane < 64, low_total, high_total)
         total[0, rows, :] = jnp.where(from_strip, edge_total, wall[rows, :])
         total[1, rows, :] = jnp.where(lane >= 64, low_total, high_total)
@@ -634,10 +637,12 @@
             for i in range(3):
                 field[i, part, rows_at(outside), :] = blank
     scale = 1.0 / KL
+    south_faces = {g: southward(grid[2, 0, rows_at(g), :], grid[2, 1, rows_at(g), :]) for g in GROUPS}
     for g in GROUPS:
         rows = rows_at(g)
-        souths = southward(grid[2, 0, rows, :], grid[2, 1, rows, :])
+        souths = south_faces[g]
         for part in range(2):
+            grid[6, part, rows, :] = souths[part]
             here = grid[0, part, rows, :]
             own_part = ALPHA * scale * here + jnp.where(here == 0.0, 1.0, 0.0)
             faces = grid[1, part, rows, :] + grid[1, part, rows_at(g - 1), :] + grid[2, part, rows, :] + souths[part]
@@ -650,12 +655,14 @@
 
     moments = [blank] * 6
     for i in range(3):
-        for g in GROUPS:
+        groups = GROUPS if i < 2 else INNER
+        pairs = {g: (field[i, 0, rows_at(g), :], field[i, 1, rows_at(g), :]) for g in groups}
+        all_norths = {g: northward(*pairs[g]) for g in groups}
+        all_souths = {g: southward(*pairs[g]) for g in groups} if i < 2 else {}
+        for g in groups:
             rows = rows_at(g)
-            both = field[i, 0, rows, :], field[i, 1, rows, :]
-            norths = northward(*both)
-            souths = southward(*both)
-            south_faces = southward(grid[2, 0, rows, :], grid[2, 1, rows, :])
+            both = pairs[g]
+            norths = all_norths[g]
             for part in range(2):
                 if i == 2 and part == 1:
                     continue
@@ -676,7 +683,7 @@
                         + east_face * east_gap
                         + scale * grid[1, part, rows_at(g - 1), :] * (here - field[i, part, rows_at(g - 1), :])
                         + north_face * north_gap
-                        + scale * south_faces[part] * (here - souths[part])
+                        + scale * grid[6, part, rows, :] * (here - all_souths[g][part])
                     )
                     field[i + 1, part, rows, :] = image * grid[3, part, rows, :]
         pltpu.make_async_copy(field.at[i, 0, PAD : PAD + SX, :], fields.at[i], sems.at[1]).start()
@@ -705,7 +712,7 @@
         (),
         (2,),
         (3, 2),
-        (6, 2),
+        (7, 2),
     )
     return pl.pallas_call(
         functools.partial(operator_kernel, count=count),
@@ -788,19 +795,15 @@
 
 def on_device(tracers, east, north, levels):
     to_first, to_second = edges(tracers, east, north, levels)
+    second = second_pairs(to_second, "gx", True)
     first = first_pairs(to_first, "gx")
-    second = second_pairs(to_second, "gx", True)
     own_rows, one, two, blocked, total = block(tracers, east, north, levels, to_first)
-    one, two, first, second = lax.optimization_barrier((one, two, first, second))
-    first_rows = first_pairs(one, "gy")
-    second_rows = second_pairs(two, "gy", False)
-    own_edges, one, two, low, high = pack_edges(first, second, total)
-    first_edges = first_pairs(one, "gy")
-    second_edges = second_pairs(two, "gy", False)
+    own_edges, one, two, low, high = pack_edges(first, second, one, two)
+    first = first_pairs(one, "gy")
+    second = second_pairs(two, "gy", False)
     ends, ends_total = end_levels(tracers, east, north, levels, low, high)
     new, fields, sums = operator(
-        levels, low, high, own_rows, own_edges, first_rows, second_rows, first_edges, second_edges,
-        blocked, ends, total, ends_total, count=lax.axis_size("gy"),
+        levels, low, high, own_rows, own_edges, first, second, blocked, ends, total, ends_total, count=lax.axis_size("gy")
     )
     sums = lax.all_to_all(sums, ("gx", "gy"), split_axis=0, concat_axis=0, tiled=True)
     return new, finish(sums, fields)

time: 46.7 us -> 44.8 us (0.959)
  starting transfers between devices: 14.6 us -> 11 us
  waiting for transfers between devices: 0.46 us -> 3.02 us
  Pallas kernels: 15 us -> 14.2 us
    ppermute x3 -> x2, starting transfers between devices: 13.5 us -> 9.96 us  [second_pairs(): return lax.ppermute(array, axis, pairs)]
    ppermute x3 -> x2, waiting for transfers between devices: 0.45 us -> 3.02 us  [second_pairs(): return lax.ppermute(array, axis, pairs)]
    pallas_call x1, Pallas kernels: 3.87 us -> 2.97 us  [operator(): pl.pallas_call(functools.partial(operator_kernel, count=count), out_shape...]
    ppermute x3 -> x2, starting transfers between devices: 1.1 us -> 1.02 us  [first_pairs(): lax.ppermute(array, axis, [(i, i ^ 1) for i in range(lax.axis_size(axis))])]
  transfers between devices with their start and end apart: 6 -> 4, of which waited for: 1 -> 1; matrix products, arithmetic and copies ran while one was open for 0% -> 0% of each run, Pallas kernels for 18% -> 17%
where the time goes in v7:
time: 44.8 us; the launch traced here: 44.7 us
  blocking collectives  15.7 us (35%)
  Pallas kernels  14.2 us (32%)
  starting transfers between devices  11 us (25%)
  waiting for transfers between devices  3.02 us (7%)
  between operations  0.75 us (2%)
    all_to_all x1, blocking collectives, on_device(): lax.all_to_all(sums, ('gx', 'gy'), split_axis=0, concat_axis=0, tiled=True)  15.7 us
    ppermute x2, starting transfers between devices, second_pairs(): return lax.ppermute(array, axis, pairs)  9.96 us
    pallas_call x1, Pallas kernels, block(): pl.pallas_call(block_kernel, in_specs=[pl.BlockSpec(memory_space=pltpu.VM...  6.55 us
    ppermute x2, waiting for transfers between devices, second_pairs(): return lax.ppermute(array, axis, pairs)  3.02 us
    pallas_call x1, Pallas kernels, operator(): pl.pallas_call(functools.partial(operator_kernel, count=count), out_shape...  2.97 us
    pallas_call x1, Pallas kernels, finish(): pl.pallas_call(finish_kernel, in_specs=[pl.BlockSpec(memory_space=pl.ANY)...  1.63 us
    pallas_call x1, Pallas kernels, edges(): pl.pallas_call(edges_kernel, in_specs=[pl.BlockSpec(memory_space=pltpu.HB...  1.36 us
    pallas_call x1, Pallas kernels, end_levels(): pl.pallas_call(ends_kernel, out_shape=[pltpu.VMEM((2, KL, 16, SY), F32),...  1.1 us
  transfers between devices with their start and end apart: 4, of which 1 were waited for; matrix products, arithmetic and copies ran while one was open for 0% of the time, Pallas kernels for 17%

profile of v7, /device:TPU:1, one launch (start us, length us, event | category | flops | bytes accessed | tf_op | source)
XLA Modules:
  0.0 44.7 jit_solution(10830848826111692419)
XLA Ops:
  0.6 0.0 copy-start.3
  0.6 0.0 copy-start.2
  0.7 0.0 copy-start.1
  0.7 0.0 copy-start
  0.7 1.4 %edges.1 = (f32[304,128]{1,0:T(8,128)S(1)}, f32[304,128]{1,0:T(8,128)S(1)}) custom-call(f32[2,16,128,128]{3,2,1,0:T(8,128)} %tracers.3, bf16[16,128,128]{2,1,0:T(8,128)(2,1)} %east.3, bf16[16,128,128]{2,1,0:T(8,128)(2,1)} %north.3, s32[128,128]{1,0:T(8,128)} %levels.5), custom_call_target="tpu_custom_call" | custom-call | tf_op jit(solution)/shard_map/edges/pallas_call | solution.py:111
  2.0 6.9 %collective-permute-start.1 = (f32[304,128]{1,0:T(8,128)S(1)}, f32[304,128]{1,0:T(8,128)S(1)}, u32[]{:S(2)}, u32[]{:S(2)}) collective-permute-start(f32[304,128]{1,0:T(8,128)S(1)} %get-tuple-element.20), channel_id=1, source_target_pairs={{8,16},{16,8},{24,32},{32,24},{40,48},{48,40},{56,64},{64,56},{72,... | collective-permute-start | bytes 466952 | tf_op jit(solution)/shard_map/ppermute | solution.py:793
  8.9 0.0 collective-permute-start
  8.9 0.0 copy-done.3
  8.9 0.0 copy-done.2
  8.9 0.0 copy-done.1
  8.9 0.0 copy-done
  8.9 6.6 %block.1 = (f32[2,5,128,128]{3,2,1,0:T(8,128)S(1)}, f32[3,128,128]{2,1,0:T(8,128)S(1)}, f32[3,128,128]{2,1,0:T(8,128)S(1)}, f32[2,16,128,128]{3,2,1,0:T(8,128)S(1)}, f32[160,128]{1,0:T(8,128)S(1)}) custom-call(f32[2,16,128,128]{3,2,1,0:T(8,128)S(1)} %copy-done, bf16[16,128,128]{2,1,0:T(8,128)(2,1)S(1)} %copy-done.1, bf16[16,128,128]{2,1,0:T(8,128)(2,1)S(1)} %copy-done.2, ...), custom_call_target="tpu_custom_call" | custom-call | flops 20000000 | bytes 24000000 | tf_op jit(solution)/shard_map/block/pallas_call | solution.py:391
  15.5 0.0 collective-permute-done.1.second_pair
  15.5 0.0 collective-permute-done.first_pair
  15.5 0.6 %pack_edges.1 = (f32[2,5,16,128]{3,2,1,0:T(8,128)S(1)}, f32[3,144,128]{2,1,0:T(8,128)S(1)}, f32[3,144,128]{2,1,0:T(8,128)S(1)}, f32[65,8,128]{2,1,0:T(8,128)S(1)}, f32[65,8,128]{2,1,0:T(8,128)S(1)}) custom-call(f32[304,128]{1,0:T(8,128)S(1)} %collective-permute-done.first_pair, f32[304,128]{1,0:T(8,128)S(1)} %collective-permute-done.1.second_pair, ...), custom_call_target="tpu_custom_call" | custom-call | tf_op jit(solution)/shard_map/pack_edges/pallas_call | solution.py:252
  16.1 1.0 %collective-permute-start.2 = (f32[3,144,128]{2,1,0:T(8,128)S(1)}, f32[3,144,128]{2,1,0:T(8,128)S(1)}, u32[]{:S(2)}, u32[]{:S(2)}) collective-permute-start(f32[3,144,128]{2,1,0:T(8,128)S(1)} %get-tuple-element.27), channel_id=1, source_target_pairs={{0,1},{1,0},{2,3},{3,2},{4,5},{5,4},{6,7},{7,6},{8,9},{9,8},{10,11... | collective-permute-start | bytes 663560 | tf_op jit(solution)/shard_map/ppermute | solution.py:785
  17.1 3.1 %collective-permute-start.3 = (f32[3,144,128]{2,1,0:T(8,128)S(1)}, f32[3,144,128]{2,1,0:T(8,128)S(1)}, u32[]{:S(2)}, u32[]{:S(2)}) collective-permute-start(f32[3,144,128]{2,1,0:T(8,128)S(1)} %get-tuple-element.28), channel_id=1, source_target_pairs={{0,0},{7,7},{1,2},{2,1},{3,4},{4,3},{5,6},{6,5},{8,8},{15,15},{9,1... | collective-permute-start | bytes 663560 | tf_op jit(solution)/shard_map/ppermute | solution.py:793
  20.2 1.1 %end_levels.1 = (f32[2,16,16,128]{3,2,1,0:T(8,128)S(1)}, f32[48,128]{1,0:T(8,128)S(1)}) custom-call(f32[2,16,128,128]{3,2,1,0:T(8,128)S(1)} %copy-done, bf16[16,128,128]{2,1,0:T(8,128)(2,1)S(1)} %copy-done.1, bf16[16,128,128]{2,1,0:T(8,128)(2,1)S(1)} %copy-done.2, s32[128,128]{1,0:T(8,128)S(1)} %copy-done.3, f32[65,8,128]{2,1,0:T(8,128)S(1)} %get-tuple-element.23.low, ...), custom_call_target="tpu_custom_call" | custom-call | flops 5000000 | bytes 6000000 | tf_op jit(solution)/shard_map/end_levels/pallas_call | solution.py:461
  21.3 0.0 collective-permute-done.2.first_pair
  21.3 3.0 %collective-permute-done.3.second_pair = f32[3,144,128]{2,1,0:T(8,128)S(1)} collective-permute-done((f32[3,144,128]{2,1,0:T(8,128)S(1)}, f32[3,144,128]{2,1,0:T(8,128)S(1)}, u32[]{:S(2)}, u32[]{:S(2)}) %collective-permute-start.3) | collective-permute-done | bytes 221216 | tf_op jit(solution)/shard_map/ppermute | solution.py:793
  24.3 3.0 %operator.1 = (f32[2,16,128,128]{3,2,1,0:T(8,128)}, f32[3,128,128]{2,1,0:T(8,128)}, f32[128,128]{1,0:T(8,128)S(1)}) custom-call(s32[128,128]{1,0:T(8,128)S(1)} %copy-done.3, f32[65,8,128]{2,1,0:T(8,128)S(1)} %get-tuple-element.23.low, f32[65,8,128]{2,1,0:T(8,128)S(1)} %get-tuple-element.24.high, f32[2,5,128,128]{3,2,1,0:T(8,128)S(1)} %get-tuple-element.25.own_rows, ...), custom_call_target="tpu_custom_call" | custom-call | tf_op jit(solution)/shard_map/operator/pallas_call | solution.py:717
  27.3 15.7 %all_to_all.11 = f32[128,1,128]{2,1,0:T(1,128)} all-to-all(f32[128,1,128]{2,1,0:T(1,128)S(1)} %bitcast.4), channel_id=1, replica_groups=mesh['gx'=16,'gy'=8] {'gx','gy'}, dimensions={0} | all-to-all | bytes 131072 | tf_op jit(solution)/shard_map/all_to_all | solution.py:808
  43.0 1.6 %finish.1 = f32[128,128]{1,0:T(8,128)} custom-call(f32[128,128]{1,0:T(8,128)} %bitcast.5, f32[3,128,128]{2,1,0:T(8,128)} %get-tuple-element.35.fields_in), custom_call_target="tpu_custom_call" | custom-call | tf_op jit(solution)/shard_map/finish/pallas_call | solution.py:771
Async XLA Ops:
  0.6 8.3 %copy-start.3 = (s32[128,128]{1,0:T(8,128)S(1)}, s32[128,128]{1,0:T(8,128)}, u32[]{:S(2)}) copy-start(s32[128,128]{1,0:T(8,128)} %levels.5) | copy-start | bytes 196612
  0.6 8.3 %copy-start.2 = (bf16[16,128,128]{2,1,0:T(8,128)(2,1)S(1)}, bf16[16,128,128]{2,1,0:T(8,128)(2,1)}, u32[]{:S(2)}) copy-start(bf16[16,128,128]{2,1,0:T(8,128)(2,1)} %north.3) | copy-start | bytes 1572868
  0.7 8.3 %copy-start.1 = (bf16[16,128,128]{2,1,0:T(8,128)(2,1)S(1)}, bf16[16,128,128]{2,1,0:T(8,128)(2,1)}, u32[]{:S(2)}) copy-start(bf16[16,128,128]{2,1,0:T(8,128)(2,1)} %east.3) | copy-start | bytes 1572868
  0.7 8.3 %copy-start = (f32[2,16,128,128]{3,2,1,0:T(8,128)S(1)}, f32[2,16,128,128]{3,2,1,0:T(8,128)}, u32[]{:S(2)}) copy-start(f32[2,16,128,128]{3,2,1,0:T(8,128)} %tracers.3) | copy-start | bytes 6291460
  2.0 13.5 %collective-permute-start.1 = (f32[304,128]{1,0:T(8,128)S(1)}, f32[304,128]{1,0:T(8,128)S(1)}, u32[]{:S(2)}, u32[]{:S(2)}) collective-permute-start(f32[304,128]{1,0:T(8,128)S(1)} %get-tuple-element.20), channel_id=1, source_target_pairs={{8,16},{16,8},{24,32},{32,24},{40,48},{48,40},{56,64},{64,56},{72,... | collective-permute-start | bytes 466952 | tf_op jit(solution)/shard_map/ppermute | solution.py:793
  8.9 6.6 %collective-permute-start = (f32[304,128]{1,0:T(8,128)S(1)}, f32[304,128]{1,0:T(8,128)S(1)}, u32[]{:S(2)}, u32[]{:S(2)}) collective-permute-start(f32[304,128]{1,0:T(8,128)S(1)} %get-tuple-element.19.after), channel_id=1, source_target_pairs={{0,8},{8,0},{16,24},{24,16},{32,40},{40,32},{48,56},{56,48},{64,72... | collective-permute-start | bytes 466952 | tf_op jit(solution)/shard_map/ppermute | solution.py:785
  16.1 5.2 %collective-permute-start.2 = (f32[3,144,128]{2,1,0:T(8,128)S(1)}, f32[3,144,128]{2,1,0:T(8,128)S(1)}, u32[]{:S(2)}, u32[]{:S(2)}) collective-permute-start(f32[3,144,128]{2,1,0:T(8,128)S(1)} %get-tuple-element.27), channel_id=1, source_target_pairs={{0,1},{1,0},{2,3},{3,2},{4,5},{5,4},{6,7},{7,6},{8,9},{9,8},{10,11... | collective-permute-start | bytes 663560 | tf_op jit(solution)/shard_map/ppermute | solution.py:785
  17.1 7.2 %collective-permute-start.3 = (f32[3,144,128]{2,1,0:T(8,128)S(1)}, f32[3,144,128]{2,1,0:T(8,128)S(1)}, u32[]{:S(2)}, u32[]{:S(2)}) collective-permute-start(f32[3,144,128]{2,1,0:T(8,128)S(1)} %get-tuple-element.28), channel_id=1, source_target_pairs={{0,0},{7,7},{1,2},{2,1},{3,4},{4,3},{5,6},{6,5},{8,8},{15,15},{9,1... | collective-permute-start | bytes 663560 | tf_op jit(solution)/shard_map/ppermute | solution.py:793

commit v8 on v7

--- a/solution.py
+++ b/solution.py
@@ -324,6 +324,7 @@
 LEVELS = 2
 END_LEVELS = 4
 PLACED = 8
+EARLY = 8
 
 
 def set_faces(groups, depth, face):
@@ -336,11 +337,7 @@
         face[1, rows, :] = jnp.where(lane == 127, 0.0, jnp.minimum(here, ahead[g]))
 
 
-def block_kernel(
-    tracers, east, north, levels, after, own, first_pair, second_pair, new, total, depth, face, q0, q1, flow, coef
-):
-    del after
-    pack_block(tracers, east, north, levels, own, first_pair, second_pair)
+def inner_levels(from_level, to_level, tracers, east, north, levels, new, total, depth, face, q0, q1, flow, coef):
     blank = jnp.zeros((8, 128), F32)
     for g in INNER:
         depth[rows_at(g), :] = levels[rows_at(g - PAD), :].astype(F32)
@@ -357,7 +354,7 @@
 
     def some_levels(i, carry):
         for c in range(LEVELS):
-            k = LEVELS * i + c
+            k = from_level + LEVELS * i + c
             for t in range(2):
                 q0[c, t, PAD : PAD + SX, :] = tracers[t, k]
             flow[c, 0, PAD : PAD + SX, :] = east[k].astype(F32)
@@ -365,7 +362,7 @@
         for c, g, temperature, salinity in two_steps(
             LEVELS,
             INNER,
-            lambda c: (LEVELS * i + c).astype(F32),
+            lambda c: (from_level + LEVELS * i + c).astype(F32),
             lambda c, g: depth[rows_at(g), :],
             lambda c, g: (face[0, rows_at(g), :], face[1, rows_at(g), :]),
             flow,
@@ -378,7 +375,13 @@
             total[rows_at(g), :] += temperature - 0.8 * salinity
         return carry
 
-    lax.fori_loop(0, KL // LEVELS, some_levels, 0)
+    lax.fori_loop(0, (to_level - from_level) // LEVELS, some_levels, 0)
+
+
+def block_kernel(tracers, east, north, levels, after, own, first_pair, second_pair, *rest):
+    del after
+    pack_block(tracers, east, north, levels, own, first_pair, second_pair)
+    inner_levels(0, EARLY, tracers, east, north, levels, *rest)
 
 
 def level_scratch(rows, copies):
@@ -395,7 +398,7 @@
             pltpu.VMEM((2, 5, SX, 128), F32),
             sent,
             sent,
-            pltpu.VMEM(tracers.shape, F32),
+            pltpu.VMEM((2, EARLY, SX, SY), F32),
             pltpu.VMEM((ROWS, 128), F32),
         ],
         scratch_shapes=level_scratch(ROWS, LEVELS),
@@ -405,7 +408,12 @@
     )(tracers, east, north, levels, after)
 
 
-def ends_kernel(tracers, east, north, levels, low, high, new, total, depth, face, q0, q1, flow, coef):
+def late_kernel(tracers, east, north, levels, low, high, new, total, ends_new, ends_total, *scratch):
+    ends(tracers, east, north, levels, low, high, ends_new, ends_total, *scratch[6:])
+    inner_levels(EARLY, KL, tracers, east, north, levels, new, total, *scratch[:6])
+
+
+def ends(tracers, east, north, levels, low, high, new, total, depth, face, q0, q1, flow, coef):
     blank = jnp.zeros((8, 128), F32)
     for g in range(0, END_ROWS, 8):
         rows = rows_at(g)
@@ -457,19 +465,25 @@
     lax.fori_loop(0, KL // END_LEVELS, some_levels, 0)
 
 
-def end_levels(tracers, east, north, levels, low, high):
+def late_levels(tracers, east, north, levels, low, high):
     return pl.pallas_call(
-        ends_kernel,
-        out_shape=[pltpu.VMEM((2, KL, 16, SY), F32), pltpu.VMEM((END_ROWS, 128), F32)],
-        scratch_shapes=level_scratch(END_ROWS, END_LEVELS),
+        late_kernel,
+        out_shape=[
+            pltpu.VMEM((2, KL - EARLY, SX, SY), F32),
+            pltpu.VMEM((ROWS, 128), F32),
+            pltpu.VMEM((2, KL, 16, SY), F32),
+            pltpu.VMEM((END_ROWS, 128), F32),
+        ],
+        scratch_shapes=level_scratch(ROWS, LEVELS) + level_scratch(END_ROWS, END_LEVELS),
         compiler_params=params(),
         cost_estimate=pl.CostEstimate(flops=5_000_000, bytes_accessed=6_000_000, transcendentals=0),
-        name="end_levels",
+        name="late_levels",
     )(tracers, east, north, levels, low, high)
 
 
 def operator_kernel(
-    levels, low, high, own_rows, own_edges, first_pair, second_pair, blocked, ends, wall_total, ends_total,
+    levels, low, high, own_rows, own_edges, first_pair, second_pair, early, early_total,
+    late, late_total, ends, ends_total,
     new, fields, sums,
     depth, q0, q1, strip_depth, strip_face, strip_flow, strip_total, first_q, coef, wall, total, field, grid, staged, sems,
     *, count,
@@ -576,25 +590,27 @@
     from_strip = (lane < 2) | (lane >= 126)
     row = lax.broadcasted_iota(jnp.int32, (8, 128), 0)
 
-    def place(i, carry):
-        slots = [(t, PLACED * i + c, c, g) for c in range(PLACED) for t in range(2) for g in range(0, SX, 8)]
+    def place(blocked, first_level):
+        slots = [(t, first_level + c, c, g) for c in range(PLACED) for t in range(2) for g in range(0, SX, 8)]
         turned = {
             (t, c, g): pltpu.roll(first_q[t, rows_at(g + PAD), :], 124 - 8 * k, 1) for t, k, c, g in slots
         }
         for t, k, c, g in slots:
             rows = rows_at(g)
-            here = blocked[t, k, rows, :]
+            here = blocked[t, c, rows, :]
             if g == 0:
                 here = jnp.where(row < 2, ends[t, k, rows_at(4), :], here)
             elif g == SX - 8:
                 here = jnp.where(row >= 6, ends[t, k, rows_at(8), :], here)
             staged[t, k, rows, :] = jnp.where(from_strip, turned[t, c, g], here)
-        at = pl.ds(PLACED * i, PLACED)
+        at = slice(first_level, first_level + PLACED)
         for t in range(2):
             pltpu.make_async_copy(staged.at[t, at], new.at[t, at], sems.at[0]).start()
-        return carry
-
-    lax.fori_loop(0, KL // PLACED, place, 0)
+
+    for first_level in range(0, KL, PLACED):
+        for start, blocked in ((0, early), (EARLY, late)):
+            if start <= first_level < (EARLY if start == 0 else KL):
+                place(blocked.at[:, first_level - start : first_level - start + PLACED], first_level)
 
     def beside(low_value, high_value):
         return jnp.where(lane >= 64, pltpu.roll(low_value, 4, 1), pltpu.roll(high_value, 5, 1))
@@ -608,7 +624,7 @@
         return jnp.where(lane == 0, b, a), jnp.where(lane == 0, a, b)
 
     for g in GROUPS:
-        wall[rows_at(g), :] = wall_total[rows_at(g), :]
+        wall[rows_at(g), :] = early_total[rows_at(g), :] + late_total[rows_at(g), :]
     wall[PAD - 2 : PAD + 2, :] = ends_total[10:14, :]
     wall[PAD + SX - 2 : PAD + SX + 3, :] = ends_total[30:35, :]
     for g in GROUPS + OUTSIDE:
@@ -797,13 +813,13 @@
     to_first, to_second = edges(tracers, east, north, levels)
     second = second_pairs(to_second, "gx", True)
     first = first_pairs(to_first, "gx")
-    own_rows, one, two, blocked, total = block(tracers, east, north, levels, to_first)
+    own_rows, one, two, early, early_total = block(tracers, east, north, levels, to_first)
     own_edges, one, two, low, high = pack_edges(first, second, one, two)
+    second = second_pairs(two, "gy", False)
     first = first_pairs(one, "gy")
-    second = second_pairs(two, "gy", False)
-    ends, ends_total = end_levels(tracers, east, north, levels, low, high)
+    later = late_levels(tracers, east, north, levels, low, high)
     new, fields, sums = operator(
-        levels, low, high, own_rows, own_edges, first, second, blocked, ends, total, ends_total, count=lax.axis_size("gy")
+        levels, low, high, own_rows, own_edges, first, second, early, early_total, *later, count=lax.axis_size("gy")
     )
     sums = lax.all_to_all(sums, ("gx", "gy"), split_axis=0, concat_axis=0, tiled=True)
     return new, finish(sums, fields)

time: 44.8 us -> 44.7 us (level)
  waiting for transfers between devices: 3.02 us -> 1.28 us
  blocking collectives: 15.7 us -> 16.8 us
  starting transfers between devices: 11 us -> 11.5 us
    ppermute x2, waiting for transfers between devices: 3.02 us -> 1.28 us  [second_pairs(): return lax.ppermute(array, axis, pairs)]
    pallas_call x1, Pallas kernels: 1.1 us -> 2.84 us  [late_levels(): pl.pallas_call(late_kernel, out_shape=[pltpu.VMEM((2, KL - EARLY, SX, SY)...]
    pallas_call x1, Pallas kernels: 6.55 us -> 4.89 us  [block(): pl.pallas_call(block_kernel, in_specs=[pl.BlockSpec(memory_space=pltpu.VM...]
    all_to_all x1, blocking collectives: 15.7 us -> 16.8 us  [on_device(): lax.all_to_all(sums, ('gx', 'gy'), split_axis=0, concat_axis=0, tiled=True)]
    ppermute x2, starting transfers between devices: 1.02 us -> 1.55 us  [first_pairs(): lax.ppermute(array, axis, [(i, i ^ 1) for i in range(lax.axis_size(axis))])]
where the time goes in v8:
time: 44.7 us; the launch traced here: 44.5 us
  blocking collectives  16.8 us (38%)
  Pallas kernels  14.1 us (32%)
  starting transfers between devices  11.5 us (26%)
  waiting for transfers between devices  1.28 us (3%)
  between operations  0.75 us (2%)
    all_to_all x1, blocking collectives, on_device(): lax.all_to_all(sums, ('gx', 'gy'), split_axis=0, concat_axis=0, tiled=True)  16.8 us
    ppermute x2, starting transfers between devices, second_pairs(): return lax.ppermute(array, axis, pairs)  9.96 us
    pallas_call x1, Pallas kernels, block(): pl.pallas_call(block_kernel, in_specs=[pl.BlockSpec(memory_space=pltpu.VM...  4.89 us
    pallas_call x1, Pallas kernels, late_levels(): pl.pallas_call(late_kernel, out_shape=[pltpu.VMEM((2, KL - EARLY, SX, SY)...  2.84 us
    pallas_call x1, Pallas kernels, operator(): pl.pallas_call(functools.partial(operator_kernel, count=count), out_shape...  2.81 us
    pallas_call x1, Pallas kernels, finish(): pl.pallas_call(finish_kernel, in_specs=[pl.BlockSpec(memory_space=pl.ANY)...  1.63 us
    ppermute x2, starting transfers between devices, first_pairs(): lax.ppermute(array, axis, [(i, i ^ 1) for i in range(lax.axis_size(axis))])  1.55 us
    pallas_call x1, Pallas kernels, edges(): pl.pallas_call(edges_kernel, in_specs=[pl.BlockSpec(memory_space=pltpu.HB...  1.36 us
  transfers between devices with their start and end apart: 4, of which 1 were waited for; matrix products, arithmetic and copies ran while one was open for 0% of the time, Pallas kernels for 17%

profile of v8, /device:TPU:1, one launch (start us, length us, event | category | flops | bytes accessed | tf_op | source)
XLA Modules:
  0.0 44.5 jit_solution(2380975048250389380)
XLA Ops:
  0.6 0.0 copy-start.3
  0.6 0.0 copy-start.2
  0.7 0.0 copy-start.1
  0.7 0.0 copy-start
  0.7 1.4 %edges.1 = (f32[304,128]{1,0:T(8,128)S(1)}, f32[304,128]{1,0:T(8,128)S(1)}) custom-call(f32[2,16,128,128]{3,2,1,0:T(8,128)} %tracers.3, bf16[16,128,128]{2,1,0:T(8,128)(2,1)} %east.3, bf16[16,128,128]{2,1,0:T(8,128)(2,1)} %north.3, s32[128,128]{1,0:T(8,128)} %levels.5), custom_call_target="tpu_custom_call" | custom-call | tf_op jit(solution)/shard_map/edges/pallas_call | solution.py:111
  2.0 6.9 %collective-permute-start.1 = (f32[304,128]{1,0:T(8,128)S(1)}, f32[304,128]{1,0:T(8,128)S(1)}, u32[]{:S(2)}, u32[]{:S(2)}) collective-permute-start(f32[304,128]{1,0:T(8,128)S(1)} %get-tuple-element.22), channel_id=1, source_target_pairs={{8,16},{16,8},{24,32},{32,24},{40,48},{48,40},{56,64},{64,56},{72,... | collective-permute-start | bytes 466952 | tf_op jit(solution)/shard_map/ppermute | solution.py:809
  8.9 0.0 collective-permute-start
  8.9 0.0 copy-done.3
  8.9 0.0 copy-done.2
  8.9 0.0 copy-done.1
  8.9 0.0 copy-done
  8.9 4.9 %block.1 = (f32[2,5,128,128]{3,2,1,0:T(8,128)S(1)}, f32[3,128,128]{2,1,0:T(8,128)S(1)}, f32[3,128,128]{2,1,0:T(8,128)S(1)}, f32[2,8,128,128]{3,2,1,0:T(8,128)S(1)}, f32[160,128]{1,0:T(8,128)S(1)}) custom-call(f32[2,16,128,128]{3,2,1,0:T(8,128)S(1)} %copy-done, bf16[16,128,128]{2,1,0:T(8,128)(2,1)S(1)} %copy-done.1, bf16[16,128,128]{2,1,0:T(8,128)(2,1)S(1)} %copy-done.2, ...), custom_call_target="tpu_custom_call" | custom-call | flops 20000000 | bytes 24000000 | tf_op jit(solution)/shard_map/block/pallas_call | solution.py:394
  13.8 0.0 collective-permute-done.1.second_pair
  13.8 0.0 collective-permute-done.first_pair
  13.8 0.6 %pack_edges.1 = (f32[2,5,16,128]{3,2,1,0:T(8,128)S(1)}, f32[3,144,128]{2,1,0:T(8,128)S(1)}, f32[3,144,128]{2,1,0:T(8,128)S(1)}, f32[65,8,128]{2,1,0:T(8,128)S(1)}, f32[65,8,128]{2,1,0:T(8,128)S(1)}) custom-call(f32[304,128]{1,0:T(8,128)S(1)} %collective-permute-done.first_pair, f32[304,128]{1,0:T(8,128)S(1)} %collective-permute-done.1.second_pair, ...), custom_call_target="tpu_custom_call" | custom-call | tf_op jit(solution)/shard_map/pack_edges/pallas_call | solution.py:252
  14.4 1.5 %collective-permute-start.2 = (f32[3,144,128]{2,1,0:T(8,128)S(1)}, f32[3,144,128]{2,1,0:T(8,128)S(1)}, u32[]{:S(2)}, u32[]{:S(2)}) collective-permute-start(f32[3,144,128]{2,1,0:T(8,128)S(1)} %get-tuple-element.29), channel_id=1, source_target_pairs={{0,1},{1,0},{2,3},{3,2},{4,5},{5,4},{6,7},{7,6},{8,9},{9,8},{10,11... | collective-permute-start | bytes 663560 | tf_op jit(solution)/shard_map/ppermute | solution.py:801
  16.0 3.1 %collective-permute-start.3 = (f32[3,144,128]{2,1,0:T(8,128)S(1)}, f32[3,144,128]{2,1,0:T(8,128)S(1)}, u32[]{:S(2)}, u32[]{:S(2)}) collective-permute-start(f32[3,144,128]{2,1,0:T(8,128)S(1)} %get-tuple-element.30), channel_id=1, source_target_pairs={{0,0},{7,7},{1,2},{2,1},{3,4},{4,3},{5,6},{6,5},{8,8},{15,15},{9,1... | collective-permute-start | bytes 663560 | tf_op jit(solution)/shard_map/ppermute | solution.py:809
  19.1 2.8 %late_levels.1 = (f32[2,8,128,128]{3,2,1,0:T(8,128)S(1)}, f32[160,128]{1,0:T(8,128)S(1)}, f32[2,16,16,128]{3,2,1,0:T(8,128)S(1)}, f32[48,128]{1,0:T(8,128)S(1)}) custom-call(f32[2,16,128,128]{3,2,1,0:T(8,128)S(1)} %copy-done, bf16[16,128,128]{2,1,0:T(8,128)(2,1)S(1)} %copy-done.1, bf16[16,128,128]{2,1,0:T(8,128)(2,1)S(1)} %copy-done.2, ...), custom_call_target="tpu_custom_call" | custom-call | flops 5000000 | bytes 6000000 | tf_op jit(solution)/shard_map/late_levels/pallas_call | solution.py:469
  21.9 0.0 collective-permute-done.2.first_pair
  21.9 1.3 %collective-permute-done.3.second_pair = f32[3,144,128]{2,1,0:T(8,128)S(1)} collective-permute-done((f32[3,144,128]{2,1,0:T(8,128)S(1)}, f32[3,144,128]{2,1,0:T(8,128)S(1)}, u32[]{:S(2)}, u32[]{:S(2)}) %collective-permute-start.3) | collective-permute-done | bytes 221216 | tf_op jit(solution)/shard_map/ppermute | solution.py:809
  23.2 2.8 %operator.1 = (f32[2,16,128,128]{3,2,1,0:T(8,128)}, f32[3,128,128]{2,1,0:T(8,128)}, f32[128,128]{1,0:T(8,128)S(1)}) custom-call(s32[128,128]{1,0:T(8,128)S(1)} %copy-done.3, f32[65,8,128]{2,1,0:T(8,128)S(1)} %get-tuple-element.25.low, f32[65,8,128]{2,1,0:T(8,128)S(1)} %get-tuple-element.26.high, f32[2,5,128,128]{3,2,1,0:T(8,128)S(1)} %get-tuple-element.27.own_rows, ...), custom_call_target="tpu_custom_call" | custom-call | tf_op jit(solution)/shard_map/operator/pallas_call | solution.py:733
  26.0 16.8 %all_to_all.11 = f32[128,1,128]{2,1,0:T(1,128)} all-to-all(f32[128,1,128]{2,1,0:T(1,128)S(1)} %bitcast.4), channel_id=1, replica_groups=mesh['gx'=16,'gy'=8] {'gx','gy'}, dimensions={0} | all-to-all | bytes 131072 | tf_op jit(solution)/shard_map/all_to_all | solution.py:824
  42.9 1.6 %finish.1 = f32[128,128]{1,0:T(8,128)} custom-call(f32[128,128]{1,0:T(8,128)} %bitcast.5, f32[3,128,128]{2,1,0:T(8,128)} %get-tuple-element.39.fields_in), custom_call_target="tpu_custom_call" | custom-call | tf_op jit(solution)/shard_map/finish/pallas_call | solution.py:787
Async XLA Ops:
  0.6 8.3 %copy-start.3 = (s32[128,128]{1,0:T(8,128)S(1)}, s32[128,128]{1,0:T(8,128)}, u32[]{:S(2)}) copy-start(s32[128,128]{1,0:T(8,128)} %levels.5) | copy-start | bytes 196612
  0.6 8.3 %copy-start.2 = (bf16[16,128,128]{2,1,0:T(8,128)(2,1)S(1)}, bf16[16,128,128]{2,1,0:T(8,128)(2,1)}, u32[]{:S(2)}) copy-start(bf16[16,128,128]{2,1,0:T(8,128)(2,1)} %north.3) | copy-start | bytes 1572868
  0.7 8.3 %copy-start.1 = (bf16[16,128,128]{2,1,0:T(8,128)(2,1)S(1)}, bf16[16,128,128]{2,1,0:T(8,128)(2,1)}, u32[]{:S(2)}) copy-start(bf16[16,128,128]{2,1,0:T(8,128)(2,1)} %east.3) | copy-start | bytes 1572868
  0.7 8.3 %copy-start = (f32[2,16,128,128]{3,2,1,0:T(8,128)S(1)}, f32[2,16,128,128]{3,2,1,0:T(8,128)}, u32[]{:S(2)}) copy-start(f32[2,16,128,128]{3,2,1,0:T(8,128)} %tracers.3) | copy-start | bytes 6291460
  2.0 11.8 %collective-permute-start.1 = (f32[304,128]{1,0:T(8,128)S(1)}, f32[304,128]{1,0:T(8,128)S(1)}, u32[]{:S(2)}, u32[]{:S(2)}) collective-permute-start(f32[304,128]{1,0:T(8,128)S(1)} %get-tuple-element.22), channel_id=1, source_target_pairs={{8,16},{16,8},{24,32},{32,24},{40,48},{48,40},{56,64},{64,56},{72,... | collective-permute-start | bytes 466952 | tf_op jit(solution)/shard_map/ppermute | solution.py:809
  8.9 4.9 %collective-permute-start = (f32[304,128]{1,0:T(8,128)S(1)}, f32[304,128]{1,0:T(8,128)S(1)}, u32[]{:S(2)}, u32[]{:S(2)}) collective-permute-start(f32[304,128]{1,0:T(8,128)S(1)} %get-tuple-element.21.after), channel_id=1, source_target_pairs={{0,8},{8,0},{16,24},{24,16},{32,40},{40,32},{48,56},{56,48},{64,72... | collective-permute-start | bytes 466952 | tf_op jit(solution)/shard_map/ppermute | solution.py:801
  14.4 7.5 %collective-permute-start.2 = (f32[3,144,128]{2,1,0:T(8,128)S(1)}, f32[3,144,128]{2,1,0:T(8,128)S(1)}, u32[]{:S(2)}, u32[]{:S(2)}) collective-permute-start(f32[3,144,128]{2,1,0:T(8,128)S(1)} %get-tuple-element.29), channel_id=1, source_target_pairs={{0,1},{1,0},{2,3},{3,2},{4,5},{5,4},{6,7},{7,6},{8,9},{9,8},{10,11... | collective-permute-start | bytes 663560 | tf_op jit(solution)/shard_map/ppermute | solution.py:801
  16.0 7.2 %collective-permute-start.3 = (f32[3,144,128]{2,1,0:T(8,128)S(1)}, f32[3,144,128]{2,1,0:T(8,128)S(1)}, u32[]{:S(2)}, u32[]{:S(2)}) collective-permute-start(f32[3,144,128]{2,1,0:T(8,128)S(1)} %get-tuple-element.30), channel_id=1, source_target_pairs={{0,0},{7,7},{1,2},{2,1},{3,4},{4,3},{5,6},{6,5},{8,8},{15,15},{9,1... | collective-permute-start | bytes 663560 | tf_op jit(solution)/shard_map/ppermute | solution.py:809

commit v9 on v8

--- a/solution.py
+++ b/solution.py
@@ -702,14 +702,13 @@
                         + scale * grid[6, part, rows, :] * (here - all_souths[g][part])
                     )
                     field[i + 1, part, rows, :] = image * grid[3, part, rows, :]
-        pltpu.make_async_copy(field.at[i, 0, PAD : PAD + SX, :], fields.at[i], sems.at[1]).start()
+        fields[i] = field[i, 0, PAD : PAD + SX, :]
     sums_row = jnp.zeros((8, 128), F32)
     for i in range(6):
         value = jnp.sum(jnp.sum(moments[i], axis=0, keepdims=True), axis=1, keepdims=True)
         sums_row = jnp.where(lane == i, value, sums_row)
     for g in range(0, 128, 8):
         sums[rows_at(g), :] = sums_row
-    pltpu.make_async_copy(field.at[:, 0, PAD : PAD + SX, :], fields, sems.at[1]).wait()
     pltpu.make_async_copy(staged, new, sems.at[0]).wait()
 
 
@@ -734,12 +733,12 @@
         functools.partial(operator_kernel, count=count),
         out_shape=[
             jax.ShapeDtypeStruct((2, KL, SX, SY), F32),
-            pltpu.HBM((3, SX, SY), F32),
+            pltpu.VMEM((3, SX, SY), F32),
             jax.ShapeDtypeStruct((128, 128), F32),
         ],
         out_specs=[
             pl.BlockSpec(memory_space=pltpu.HBM),
-            pl.BlockSpec(memory_space=pltpu.HBM),
+            pl.BlockSpec(memory_space=pltpu.VMEM),
             pl.BlockSpec(memory_space=pltpu.VMEM),
         ],
         scratch_shapes=[pltpu.VMEM(s + tall, F32) for s in scratch]
@@ -749,12 +748,7 @@
     )(*arrays)
 
 
-def finish_kernel(sums_in, fields_in, out, sums, fields, sems):
-    first_copy = pltpu.make_async_copy(sums_in, sums, sems.at[0])
-    copy = pltpu.make_async_copy(fields_in, fields, sems.at[1])
-    first_copy.start()
-    copy.start()
-    first_copy.wait()
+def finish_kernel(sums, fields, out):
     value = sums[0:8, :]
     for g in range(8, 128, 8):
         value = value + sums[rows_at(g), :]
@@ -777,7 +771,6 @@
     c2 = jnp.where(has2, y2 / d2, 0.0)
     c1 = jnp.where(has1, y1 / d1, 0.0) - l21 * c2
     c0 = m0 / m1 - l10 * c1 - l20 * c2
-    copy.wait()
     for g in range(0, SX, 8):
         rows = rows_at(g)
         out[rows, :] = c0 * fields[0, rows, :] + c1 * fields[1, rows, :] + c2 * fields[2, rows, :]
@@ -786,15 +779,9 @@
 def finish(sums, fields):
     return pl.pallas_call(
         finish_kernel,
-        in_specs=[pl.BlockSpec(memory_space=pl.ANY)] * 2,
         out_shape=jax.ShapeDtypeStruct((SX, SY), F32),
-        scratch_shapes=[
-            pltpu.VMEM((128, 128), F32),
-            pltpu.VMEM((3, SX, SY), F32),
-            pltpu.SemaphoreType.DMA((2,)),
-        ],
         name="finish",
-    )(sums, pltpu.with_memory_space_constraint(fields, pltpu.HBM))
+    )(*(pltpu.with_memory_space_constraint(x, pltpu.VMEM) for x in (sums, fields)))
 
 
 def first_pairs(array, axis):

time: 44.7 us -> 43.7 us (0.978)
  Pallas kernels: 14.1 us -> 13.5 us
    pallas_call x1, Pallas kernels: 1.63 us -> 0.77 us  [finish(): pl.pallas_call(finish_kernel, out_shape=jax.ShapeDtypeStruct((SX, SY), F3...]
  transfers between devices with their start and end apart: 4 -> 4, of which waited for: 1 -> 1; matrix products, arithmetic and copies ran while one was open for 0% -> 0% of each run, Pallas kernels for 17% -> 18%
where the time goes in v9:
time: 43.7 us; the launch traced here: 43.6 us
  blocking collectives  16.5 us (38%)
  Pallas kernels  13.5 us (31%)
  starting transfers between devices  11.5 us (26%)
  waiting for transfers between devices  1.28 us (3%)
  between operations  0.75 us (2%)
    all_to_all x1, blocking collectives, on_device(): lax.all_to_all(sums, ('gx', 'gy'), split_axis=0, concat_axis=0, tiled=True)  16.5 us
    ppermute x2, starting transfers between devices, second_pairs(): return lax.ppermute(array, axis, pairs)  9.96 us
    pallas_call x1, Pallas kernels, block(): pl.pallas_call(block_kernel, in_specs=[pl.BlockSpec(memory_space=pltpu.VM...  4.89 us
    pallas_call x1, Pallas kernels, operator(): pl.pallas_call(functools.partial(operator_kernel, count=count), out_shape...  3.1 us
    pallas_call x1, Pallas kernels, late_levels(): pl.pallas_call(late_kernel, out_shape=[pltpu.VMEM((2, KL - EARLY, SX, SY)...  2.84 us
    ppermute x2, starting transfers between devices, first_pairs(): lax.ppermute(array, axis, [(i, i ^ 1) for i in range(lax.axis_size(axis))])  1.55 us
    pallas_call x1, Pallas kernels, edges(): pl.pallas_call(edges_kernel, in_specs=[pl.BlockSpec(memory_space=pltpu.HB...  1.36 us
    ppermute x2, waiting for transfers between devices, second_pairs(): return lax.ppermute(array, axis, pairs)  1.28 us
  transfers between devices with their start and end apart: 4, of which 1 were waited for; matrix products, arithmetic and copies ran while one was open for 0% of the time, Pallas kernels for 18%

profile of v9, /device:TPU:1, one launch (start us, length us, event | category | flops | bytes accessed | tf_op | source)
XLA Modules:
  0.0 43.6 jit_solution(15090056569585897649)
XLA Ops:
  0.6 0.0 copy-start.3
  0.6 0.0 copy-start.2
  0.7 0.0 copy-start.1
  0.7 0.0 copy-start
  0.7 1.4 %edges.1 = (f32[304,128]{1,0:T(8,128)S(1)}, f32[304,128]{1,0:T(8,128)S(1)}) custom-call(f32[2,16,128,128]{3,2,1,0:T(8,128)} %tracers.3, bf16[16,128,128]{2,1,0:T(8,128)(2,1)} %east.3, bf16[16,128,128]{2,1,0:T(8,128)(2,1)} %north.3, s32[128,128]{1,0:T(8,128)} %levels.5), custom_call_target="tpu_custom_call" | custom-call | tf_op jit(solution)/shard_map/edges/pallas_call | solution.py:111
  2.0 6.9 %collective-permute-start.1 = (f32[304,128]{1,0:T(8,128)S(1)}, f32[304,128]{1,0:T(8,128)S(1)}, u32[]{:S(2)}, u32[]{:S(2)}) collective-permute-start(f32[304,128]{1,0:T(8,128)S(1)} %get-tuple-element.22), channel_id=1, source_target_pairs={{8,16},{16,8},{24,32},{32,24},{40,48},{48,40},{56,64},{64,56},{72,... | collective-permute-start | bytes 466952 | tf_op jit(solution)/shard_map/ppermute | solution.py:796
  8.9 0.0 collective-permute-start
  8.9 0.0 copy-done.3
  8.9 0.0 copy-done.2
  8.9 0.0 copy-done.1
  8.9 0.0 copy-done
  8.9 4.9 %block.1 = (f32[2,5,128,128]{3,2,1,0:T(8,128)S(1)}, f32[3,128,128]{2,1,0:T(8,128)S(1)}, f32[3,128,128]{2,1,0:T(8,128)S(1)}, f32[2,8,128,128]{3,2,1,0:T(8,128)S(1)}, f32[160,128]{1,0:T(8,128)S(1)}) custom-call(f32[2,16,128,128]{3,2,1,0:T(8,128)S(1)} %copy-done, bf16[16,128,128]{2,1,0:T(8,128)(2,1)S(1)} %copy-done.1, bf16[16,128,128]{2,1,0:T(8,128)(2,1)S(1)} %copy-done.2, ...), custom_call_target="tpu_custom_call" | custom-call | flops 20000000 | bytes 24000000 | tf_op jit(solution)/shard_map/block/pallas_call | solution.py:394
  13.8 0.0 collective-permute-done.1.second_pair
  13.8 0.0 collective-permute-done.first_pair
  13.8 0.6 %pack_edges.1 = (f32[2,5,16,128]{3,2,1,0:T(8,128)S(1)}, f32[3,144,128]{2,1,0:T(8,128)S(1)}, f32[3,144,128]{2,1,0:T(8,128)S(1)}, f32[65,8,128]{2,1,0:T(8,128)S(1)}, f32[65,8,128]{2,1,0:T(8,128)S(1)}) custom-call(f32[304,128]{1,0:T(8,128)S(1)} %collective-permute-done.first_pair, f32[304,128]{1,0:T(8,128)S(1)} %collective-permute-done.1.second_pair, ...), custom_call_target="tpu_custom_call" | custom-call | tf_op jit(solution)/shard_map/pack_edges/pallas_call | solution.py:252
  14.4 1.5 %collective-permute-start.2 = (f32[3,144,128]{2,1,0:T(8,128)S(1)}, f32[3,144,128]{2,1,0:T(8,128)S(1)}, u32[]{:S(2)}, u32[]{:S(2)}) collective-permute-start(f32[3,144,128]{2,1,0:T(8,128)S(1)} %get-tuple-element.29), channel_id=1, source_target_pairs={{0,1},{1,0},{2,3},{3,2},{4,5},{5,4},{6,7},{7,6},{8,9},{9,8},{10,11... | collective-permute-start | bytes 663560 | tf_op jit(solution)/shard_map/ppermute | solution.py:788
  16.0 3.1 %collective-permute-start.3 = (f32[3,144,128]{2,1,0:T(8,128)S(1)}, f32[3,144,128]{2,1,0:T(8,128)S(1)}, u32[]{:S(2)}, u32[]{:S(2)}) collective-permute-start(f32[3,144,128]{2,1,0:T(8,128)S(1)} %get-tuple-element.30), channel_id=1, source_target_pairs={{0,0},{7,7},{1,2},{2,1},{3,4},{4,3},{5,6},{6,5},{8,8},{15,15},{9,1... | collective-permute-start | bytes 663560 | tf_op jit(solution)/shard_map/ppermute | solution.py:796
  19.1 2.8 %late_levels.1 = (f32[2,8,128,128]{3,2,1,0:T(8,128)S(1)}, f32[160,128]{1,0:T(8,128)S(1)}, f32[2,16,16,128]{3,2,1,0:T(8,128)S(1)}, f32[48,128]{1,0:T(8,128)S(1)}) custom-call(f32[2,16,128,128]{3,2,1,0:T(8,128)S(1)} %copy-done, bf16[16,128,128]{2,1,0:T(8,128)(2,1)S(1)} %copy-done.1, bf16[16,128,128]{2,1,0:T(8,128)(2,1)S(1)} %copy-done.2, ...), custom_call_target="tpu_custom_call" | custom-call | flops 5000000 | bytes 6000000 | tf_op jit(solution)/shard_map/late_levels/pallas_call | solution.py:469
  21.9 0.0 collective-permute-done.2.first_pair
  21.9 1.3 %collective-permute-done.3.second_pair = f32[3,144,128]{2,1,0:T(8,128)S(1)} collective-permute-done((f32[3,144,128]{2,1,0:T(8,128)S(1)}, f32[3,144,128]{2,1,0:T(8,128)S(1)}, u32[]{:S(2)}, u32[]{:S(2)}) %collective-permute-start.3) | collective-permute-done | bytes 221216 | tf_op jit(solution)/shard_map/ppermute | solution.py:796
  23.2 3.1 %operator.1 = (f32[2,16,128,128]{3,2,1,0:T(8,128)}, f32[3,128,128]{2,1,0:T(8,128)S(1)}, f32[128,128]{1,0:T(8,128)S(1)}) custom-call(s32[128,128]{1,0:T(8,128)S(1)} %copy-done.3, f32[65,8,128]{2,1,0:T(8,128)S(1)} %get-tuple-element.25.low, f32[65,8,128]{2,1,0:T(8,128)S(1)} %get-tuple-element.26.high, f32[2,5,128,128]{3,2,1,0:T(8,128)S(1)} %get-tuple-element.27.own_rows, ...), custom_call_target="tpu_custom_call" | custom-call | tf_op jit(solution)/shard_map/operator/pallas_call | solution.py:732
  26.3 16.5 %all_to_all.11 = f32[128,1,128]{2,1,0:T(1,128)S(1)} all-to-all(f32[128,1,128]{2,1,0:T(1,128)S(1)} %bitcast.5), channel_id=1, replica_groups=mesh['gx'=16,'gy'=8] {'gx','gy'}, dimensions={0} | all-to-all | bytes 131072 | tf_op jit(solution)/shard_map/all_to_all | solution.py:811
  42.8 0.8 %finish.1 = f32[128,128]{1,0:T(8,128)} custom-call(f32[128,128]{1,0:T(8,128)S(1)} %bitcast.4, f32[3,128,128]{2,1,0:T(8,128)S(1)} %get-tuple-element.39.fields), custom_call_target="tpu_custom_call" | custom-call | tf_op jit(solution)/shard_map/finish/pallas_call | solution.py:780
Async XLA Ops:
  0.6 8.3 %copy-start.3 = (s32[128,128]{1,0:T(8,128)S(1)}, s32[128,128]{1,0:T(8,128)}, u32[]{:S(2)}) copy-start(s32[128,128]{1,0:T(8,128)} %levels.5) | copy-start | bytes 196612
  0.6 8.3 %copy-start.2 = (bf16[16,128,128]{2,1,0:T(8,128)(2,1)S(1)}, bf16[16,128,128]{2,1,0:T(8,128)(2,1)}, u32[]{:S(2)}) copy-start(bf16[16,128,128]{2,1,0:T(8,128)(2,1)} %north.3) | copy-start | bytes 1572868
  0.7 8.3 %copy-start.1 = (bf16[16,128,128]{2,1,0:T(8,128)(2,1)S(1)}, bf16[16,128,128]{2,1,0:T(8,128)(2,1)}, u32[]{:S(2)}) copy-start(bf16[16,128,128]{2,1,0:T(8,128)(2,1)} %east.3) | copy-start | bytes 1572868
  0.7 8.3 %copy-start = (f32[2,16,128,128]{3,2,1,0:T(8,128)S(1)}, f32[2,16,128,128]{3,2,1,0:T(8,128)}, u32[]{:S(2)}) copy-start(f32[2,16,128,128]{3,2,1,0:T(8,128)} %tracers.3) | copy-start | bytes 6291460
  2.0 11.8 %collective-permute-start.1 = (f32[304,128]{1,0:T(8,128)S(1)}, f32[304,128]{1,0:T(8,128)S(1)}, u32[]{:S(2)}, u32[]{:S(2)}) collective-permute-start(f32[304,128]{1,0:T(8,128)S(1)} %get-tuple-element.22), channel_id=1, source_target_pairs={{8,16},{16,8},{24,32},{32,24},{40,48},{48,40},{56,64},{64,56},{72,... | collective-permute-start | bytes 466952 | tf_op jit(solution)/shard_map/ppermute | solution.py:796
  8.9 4.9 %collective-permute-start = (f32[304,128]{1,0:T(8,128)S(1)}, f32[304,128]{1,0:T(8,128)S(1)}, u32[]{:S(2)}, u32[]{:S(2)}) collective-permute-start(f32[304,128]{1,0:T(8,128)S(1)} %get-tuple-element.21.after), channel_id=1, source_target_pairs={{0,8},{8,0},{16,24},{24,16},{32,40},{40,32},{48,56},{56,48},{64,72... | collective-permute-start | bytes 466952 | tf_op jit(solution)/shard_map/ppermute | solution.py:788
  14.4 7.5 %collective-permute-start.2 = (f32[3,144,128]{2,1,0:T(8,128)S(1)}, f32[3,144,128]{2,1,0:T(8,128)S(1)}, u32[]{:S(2)}, u32[]{:S(2)}) collective-permute-start(f32[3,144,128]{2,1,0:T(8,128)S(1)} %get-tuple-element.29), channel_id=1, source_target_pairs={{0,1},{1,0},{2,3},{3,2},{4,5},{5,4},{6,7},{7,6},{8,9},{9,8},{10,11... | collective-permute-start | bytes 663560 | tf_op jit(solution)/shard_map/ppermute | solution.py:788
  16.0 7.2 %collective-permute-start.3 = (f32[3,144,128]{2,1,0:T(8,128)S(1)}, f32[3,144,128]{2,1,0:T(8,128)S(1)}, u32[]{:S(2)}, u32[]{:S(2)}) collective-permute-start(f32[3,144,128]{2,1,0:T(8,128)S(1)} %get-tuple-element.30), channel_id=1, source_target_pairs={{0,0},{7,7},{1,2},{2,1},{3,4},{4,3},{5,6},{6,5},{8,8},{15,15},{9,1... | collective-permute-start | bytes 663560 | tf_op jit(solution)/shard_map/ppermute | solution.py:796

commit v10 on v9

--- a/solution.py
+++ b/solution.py
@@ -482,11 +482,9 @@
 
 
 def operator_kernel(
-    levels, low, high, own_rows, own_edges, first_pair, second_pair, early, early_total,
-    late, late_total, ends, ends_total,
-    new, fields, sums,
-    depth, q0, q1, strip_depth, strip_face, strip_flow, strip_total, first_q, coef, wall, total, field, grid, staged, sems,
-    *, count,
+    levels, low, high, own_rows, own_edges, first_pair, second_pair, early_total, late_total, ends_total,
+    from_strips, fields, sums,
+    depth, q0, q1, strip_depth, strip_face, strip_flow, strip_total, coef, wall, total, field, grid, *, count,
 ):
     lane = lanes()
     member = lane % 8
@@ -586,31 +584,8 @@
         high_values = {g: back_one(q0[1, tracer, rows_at(g), :]) for g in INNER}
         for g in INNER:
             rows = rows_at(g)
-            first_q[tracer, rows, :] = jnp.where(member >= 4, q0[0, tracer, rows, :], high_values[g])
+            from_strips[tracer, rows, :] = jnp.where(member >= 4, q0[0, tracer, rows, :], high_values[g])
     from_strip = (lane < 2) | (lane >= 126)
-    row = lax.broadcasted_iota(jnp.int32, (8, 128), 0)
-
-    def place(blocked, first_level):
-        slots = [(t, first_level + c, c, g) for c in range(PLACED) for t in range(2) for g in range(0, SX, 8)]
-        turned = {
-            (t, c, g): pltpu.roll(first_q[t, rows_at(g + PAD), :], 124 - 8 * k, 1) for t, k, c, g in slots
-        }
-        for t, k, c, g in slots:
-            rows = rows_at(g)
-            here = blocked[t, c, rows, :]
-            if g == 0:
-                here = jnp.where(row < 2, ends[t, k, rows_at(4), :], here)
-            elif g == SX - 8:
-                here = jnp.where(row >= 6, ends[t, k, rows_at(8), :], here)
-            staged[t, k, rows, :] = jnp.where(from_strip, turned[t, c, g], here)
-        at = slice(first_level, first_level + PLACED)
-        for t in range(2):
-            pltpu.make_async_copy(staged.at[t, at], new.at[t, at], sems.at[0]).start()
-
-    for first_level in range(0, KL, PLACED):
-        for start, blocked in ((0, early), (EARLY, late)):
-            if start <= first_level < (EARLY if start == 0 else KL):
-                place(blocked.at[:, first_level - start : first_level - start + PLACED], first_level)
 
     def beside(low_value, high_value):
         return jnp.where(lane >= 64, pltpu.roll(low_value, 4, 1), pltpu.roll(high_value, 5, 1))
@@ -709,7 +684,6 @@
         sums_row = jnp.where(lane == i, value, sums_row)
     for g in range(0, 128, 8):
         sums[rows_at(g), :] = sums_row
-    pltpu.make_async_copy(staged, new, sems.at[0]).wait()
 
 
 def operator(*arrays, count):
@@ -722,7 +696,6 @@
         (2,),
         (2, 2),
         (2,),
-        (2,),
         (2, 5),
         (),
         (2,),
@@ -732,19 +705,50 @@
     return pl.pallas_call(
         functools.partial(operator_kernel, count=count),
         out_shape=[
-            jax.ShapeDtypeStruct((2, KL, SX, SY), F32),
+            pltpu.VMEM((2,) + tall, F32),
             pltpu.VMEM((3, SX, SY), F32),
             jax.ShapeDtypeStruct((128, 128), F32),
         ],
-        out_specs=[
-            pl.BlockSpec(memory_space=pltpu.HBM),
-            pl.BlockSpec(memory_space=pltpu.VMEM),
-            pl.BlockSpec(memory_space=pltpu.VMEM),
-        ],
-        scratch_shapes=[pltpu.VMEM(s + tall, F32) for s in scratch]
-        + [pltpu.VMEM((2, KL, SX, SY), F32), pltpu.SemaphoreType.DMA((2,))],
+        scratch_shapes=[pltpu.VMEM(s + tall, F32) for s in scratch],
         compiler_params=params(),
         name="operator",
+    )(*arrays)
+
+
+def place_kernel(early, late, ends_new, from_strips, new, staged, sem):
+    lane = lanes()
+    row = lax.broadcasted_iota(jnp.int32, (8, 128), 0)
+    from_strip = (lane < 2) | (lane >= 126)
+    for first_level in range(0, KL, PLACED):
+        blocked, start = (early, 0) if first_level < EARLY else (late, EARLY)
+        slots = [(t, first_level + c, g) for c in range(PLACED) for t in range(2) for g in range(0, SX, 8)]
+        turned = {
+            (t, k, g): pltpu.roll(from_strips[t, rows_at(g + PAD), :], 124 - 8 * k, 1) for t, k, g in slots
+        }
+        for t, k, g in slots:
+            rows = rows_at(g)
+            here = blocked[t, k - start, rows, :]
+            if g == 0:
+                here = jnp.where(row < 2, ends_new[t, k, rows_at(4), :], here)
+            elif g == SX - 8:
+                here = jnp.where(row >= 6, ends_new[t, k, rows_at(8), :], here)
+            staged[t, k, rows, :] = jnp.where(from_strip, turned[t, k, g], here)
+        at = slice(first_level, first_level + PLACED)
+        for t in range(2):
+            pltpu.make_async_copy(staged.at[t, at], new.at[t, at], sem).start()
+    pltpu.make_async_copy(staged, new, sem).wait()
+
+
+def place(*arrays):
+    whole = (2, KL, SX, SY)
+    return pl.pallas_call(
+        place_kernel,
+        out_shape=jax.ShapeDtypeStruct(whole, F32),
+        out_specs=pl.BlockSpec(memory_space=pltpu.HBM),
+        scratch_shapes=[pltpu.VMEM(whole, F32), pltpu.SemaphoreType.DMA(())],
+        compiler_params=params(),
+        cost_estimate=pl.CostEstimate(flops=2_000_000, bytes_accessed=6_000_000, transcendentals=0),
+        name="place",
     )(*arrays)
 
 
@@ -804,11 +808,13 @@
     own_edges, one, two, low, high = pack_edges(first, second, one, two)
     second = second_pairs(two, "gy", False)
     first = first_pairs(one, "gy")
-    later = late_levels(tracers, east, north, levels, low, high)
-    new, fields, sums = operator(
-        levels, low, high, own_rows, own_edges, first, second, early, early_total, *later, count=lax.axis_size("gy")
+    late, late_total, ends_new, ends_total = late_levels(tracers, east, north, levels, low, high)
+    from_strips, fields, sums = operator(
+        levels, low, high, own_rows, own_edges, first, second, early_total, late_total, ends_total,
+        count=lax.axis_size("gy"),
     )
     sums = lax.all_to_all(sums, ("gx", "gy"), split_axis=0, concat_axis=0, tiled=True)
+    new = place(early, late, ends_new, from_strips)
     return new, finish(sums, fields)
 
 

time: 43.7 us -> 43.1 us (0.986)
  blocking collectives: 16.5 us -> 0 us
  waiting for transfers between devices: 1.28 us -> 9.06 us
  starting transfers between devices: 11.5 us -> 18.9 us
  Pallas kernels: 13.5 us -> 14.3 us
    all_to_all x1 -> x0, blocking collectives: 16.5 us -> none  [on_device(): lax.all_to_all(sums, ('gx', 'gy'), split_axis=0, concat_axis=0, tiled=True)]
    all_to_all x0 -> x1, waiting for transfers between devices: none -> 7.76 us  [on_device(): lax.all_to_all(sums, ('gx', 'gy'), split_axis=0, concat_axis=0, tiled=True)]
    all_to_all x0 -> x1, starting transfers between devices: none -> 7.48 us  [on_device(): lax.all_to_all(sums, ('gx', 'gy'), split_axis=0, concat_axis=0, tiled=True)]
    ppermute x2, starting transfers between devices: 9.96 us -> 7.54 us  [second_pairs(): return lax.ppermute(array, axis, pairs)]
    ppermute x2, starting transfers between devices: 1.55 us -> 3.84 us  [first_pairs(): lax.ppermute(array, axis, [(i, i ^ 1) for i in range(lax.axis_size(axis))])]
    pallas_call x0 -> x1, Pallas kernels: none -> 1.66 us  [place(): pl.pallas_call(place_kernel, out_shape=jax.ShapeDtypeStruct(whole, F32),...]
    pallas_call x1, Pallas kernels: 3.1 us -> 2.26 us  [operator(): pl.pallas_call(functools.partial(operator_kernel, count=count), out_shape...]
  transfers between devices with their start and end apart: 4 -> 5, of which waited for: 1 -> 2; matrix products, arithmetic and copies ran while one was open for 0% -> 0% of each run, Pallas kernels for 18% -> 22%
where the time goes in v10:
time: 43.1 us; the launch traced here: 43 us
  starting transfers between devices  18.9 us (44%)
  Pallas kernels  14.3 us (33%)
  waiting for transfers between devices  9.06 us (21%)
  between operations  0.74 us (2%)
    all_to_all x1, waiting for transfers between devices, on_device(): lax.all_to_all(sums, ('gx', 'gy'), split_axis=0, concat_axis=0, tiled=True)  7.76 us
    ppermute x2, starting transfers between devices, second_pairs(): return lax.ppermute(array, axis, pairs)  7.54 us
    all_to_all x1, starting transfers between devices, on_device(): lax.all_to_all(sums, ('gx', 'gy'), split_axis=0, concat_axis=0, tiled=True)  7.48 us
    pallas_call x1, Pallas kernels, block(): pl.pallas_call(block_kernel, in_specs=[pl.BlockSpec(memory_space=pltpu.VM...  4.89 us
    ppermute x2, starting transfers between devices, first_pairs(): lax.ppermute(array, axis, [(i, i ^ 1) for i in range(lax.axis_size(axis))])  3.84 us
    pallas_call x1, Pallas kernels, late_levels(): pl.pallas_call(late_kernel, out_shape=[pltpu.VMEM((2, KL - EARLY, SX, SY)...  2.81 us
    pallas_call x1, Pallas kernels, operator(): pl.pallas_call(functools.partial(operator_kernel, count=count), out_shape...  2.26 us
    pallas_call x1, Pallas kernels, place(): pl.pallas_call(place_kernel, out_shape=jax.ShapeDtypeStruct(whole, F32),...  1.66 us
  transfers between devices with their start and end apart: 5, of which 2 were waited for; matrix products, arithmetic and copies ran while one was open for 0% of the time, Pallas kernels for 22%

profile of v10, /device:TPU:1, one launch (start us, length us, event | category | flops | bytes accessed | tf_op | source)
XLA Modules:
  0.0 43.0 jit_solution(8384803696442159799)
XLA Ops:
  0.6 0.0 copy-start
  0.6 0.0 copy-start.1
  0.7 0.0 copy-start.2
  0.7 0.0 copy-start.3
  0.7 1.3 %edges.1 = (f32[304,128]{1,0:T(8,128)S(1)}, f32[304,128]{1,0:T(8,128)S(1)}) custom-call(f32[2,16,128,128]{3,2,1,0:T(8,128)} %tracers.3, bf16[16,128,128]{2,1,0:T(8,128)(2,1)} %east.3, bf16[16,128,128]{2,1,0:T(8,128)(2,1)} %north.3, s32[128,128]{1,0:T(8,128)} %levels.5), custom_call_target="tpu_custom_call" | custom-call | tf_op jit(solution)/shard_map/edges/pallas_call | solution.py:111
  2.0 2.5 %collective-permute-start = (f32[304,128]{1,0:T(8,128)S(1)}, f32[304,128]{1,0:T(8,128)S(1)}, u32[]{:S(2)}, u32[]{:S(2)}) collective-permute-start(f32[304,128]{1,0:T(8,128)S(1)} %get-tuple-element.21.after), channel_id=1, source_target_pairs={{0,8},{8,0},{16,24},{24,16},{32,40},{40,32},{48,56},{56,48},{64,72... | collective-permute-start | bytes 466952 | tf_op jit(solution)/shard_map/ppermute | solution.py:792
  4.6 4.4 %collective-permute-start.1 = (f32[304,128]{1,0:T(8,128)S(1)}, f32[304,128]{1,0:T(8,128)S(1)}, u32[]{:S(2)}, u32[]{:S(2)}) collective-permute-start(f32[304,128]{1,0:T(8,128)S(1)} %get-tuple-element.23), channel_id=1, source_target_pairs={{8,16},{16,8},{24,32},{32,24},{40,48},{48,40},{56,64},{64,56},{72,... | collective-permute-start | bytes 466952 | tf_op jit(solution)/shard_map/ppermute | solution.py:800
  9.0 0.0 copy-done
  9.0 0.0 copy-done.1
  9.0 0.0 copy-done.2
  9.0 0.0 copy-done.3
  9.0 4.9 %block.1 = (f32[2,5,128,128]{3,2,1,0:T(8,128)S(1)}, f32[3,128,128]{2,1,0:T(8,128)S(1)}, f32[3,128,128]{2,1,0:T(8,128)S(1)}, f32[2,8,128,128]{3,2,1,0:T(8,128)S(1)}, f32[160,128]{1,0:T(8,128)S(1)}) custom-call(f32[2,16,128,128]{3,2,1,0:T(8,128)S(1)} %copy-done, bf16[16,128,128]{2,1,0:T(8,128)(2,1)S(1)} %copy-done.1, bf16[16,128,128]{2,1,0:T(8,128)(2,1)S(1)} %copy-done.2, ...), custom_call_target="tpu_custom_call" | custom-call | flops 20000000 | bytes 24000000 | tf_op jit(solution)/shard_map/block/pallas_call | solution.py:394
  13.9 0.0 collective-permute-done.first_pair
  13.9 0.0 collective-permute-done.1.second_pair
  13.9 0.6 %pack_edges.1 = (f32[2,5,16,128]{3,2,1,0:T(8,128)S(1)}, f32[3,144,128]{2,1,0:T(8,128)S(1)}, f32[3,144,128]{2,1,0:T(8,128)S(1)}, f32[65,8,128]{2,1,0:T(8,128)S(1)}, f32[65,8,128]{2,1,0:T(8,128)S(1)}) custom-call(f32[304,128]{1,0:T(8,128)S(1)} %collective-permute-done.first_pair, f32[304,128]{1,0:T(8,128)S(1)} %collective-permute-done.1.second_pair, ...), custom_call_target="tpu_custom_call" | custom-call | tf_op jit(solution)/shard_map/pack_edges/pallas_call | solution.py:252
  14.5 1.3 %collective-permute-start.2 = (f32[3,144,128]{2,1,0:T(8,128)S(1)}, f32[3,144,128]{2,1,0:T(8,128)S(1)}, u32[]{:S(2)}, u32[]{:S(2)}) collective-permute-start(f32[3,144,128]{2,1,0:T(8,128)S(1)} %get-tuple-element.32), channel_id=1, source_target_pairs={{0,1},{1,0},{2,3},{3,2},{4,5},{5,4},{6,7},{7,6},{8,9},{9,8},{10,11... | collective-permute-start | bytes 663560 | tf_op jit(solution)/shard_map/ppermute | solution.py:792
  15.8 3.1 %collective-permute-start.3 = (f32[3,144,128]{2,1,0:T(8,128)S(1)}, f32[3,144,128]{2,1,0:T(8,128)S(1)}, u32[]{:S(2)}, u32[]{:S(2)}) collective-permute-start(f32[3,144,128]{2,1,0:T(8,128)S(1)} %get-tuple-element.33), channel_id=1, source_target_pairs={{0,0},{7,7},{1,2},{2,1},{3,4},{4,3},{5,6},{6,5},{8,8},{15,15},{9,1... | collective-permute-start | bytes 663560 | tf_op jit(solution)/shard_map/ppermute | solution.py:800
  18.9 2.8 %late_levels.1 = (f32[2,8,128,128]{3,2,1,0:T(8,128)S(1)}, f32[160,128]{1,0:T(8,128)S(1)}, f32[2,16,16,128]{3,2,1,0:T(8,128)S(1)}, f32[48,128]{1,0:T(8,128)S(1)}) custom-call(f32[2,16,128,128]{3,2,1,0:T(8,128)S(1)} %copy-done, bf16[16,128,128]{2,1,0:T(8,128)(2,1)S(1)} %copy-done.1, bf16[16,128,128]{2,1,0:T(8,128)(2,1)S(1)} %copy-done.2, ...), custom_call_target="tpu_custom_call" | custom-call | flops 5000000 | bytes 6000000 | tf_op jit(solution)/shard_map/late_levels/pallas_call | solution.py:469
  21.7 0.0 collective-permute-done.2.first_pair
  21.8 1.3 %collective-permute-done.3.second_pair = f32[3,144,128]{2,1,0:T(8,128)S(1)} collective-permute-done((f32[3,144,128]{2,1,0:T(8,128)S(1)}, f32[3,144,128]{2,1,0:T(8,128)S(1)}, u32[]{:S(2)}, u32[]{:S(2)}) %collective-permute-start.3) | collective-permute-done | bytes 221216 | tf_op jit(solution)/shard_map/ppermute | solution.py:800
  23.0 2.3 %operator.1 = (f32[2,160,128]{2,1,0:T(8,128)S(1)}, f32[3,128,128]{2,1,0:T(8,128)S(1)}, f32[128,128]{1,0:T(8,128)}) custom-call(s32[128,128]{1,0:T(8,128)S(1)} %copy-done.3, f32[65,8,128]{2,1,0:T(8,128)S(1)} %get-tuple-element.26.low, f32[65,8,128]{2,1,0:T(8,128)S(1)} %get-tuple-element.27.high, f32[2,5,128,128]{3,2,1,0:T(8,128)S(1)} %get-tuple-element.30.own_rows, ...), custom_call_target="tpu_custom_call" | custom-call | tf_op jit(solution)/shard_map/operator/pallas_call | solution.py:705
  25.3 7.5 %all-to-all-start = ((f32[128,1,128]{2,1,0:T(1,128)}), f32[128,1,128]{2,1,0:T(1,128)S(1)}, u32[]{:S(2)}, u32[]{:S(2)}) async-start(f32[128,1,128]{2,1,0:T(1,128)} %bitcast.1), calls=%async_computation | async-start | bytes 131072 | tf_op jit(solution)/shard_map/all_to_all | solution.py:816
  32.8 1.7 %place.1 = f32[2,16,128,128]{3,2,1,0:T(8,128)} custom-call(f32[2,8,128,128]{3,2,1,0:T(8,128)S(1)} %get-tuple-element.22.early, f32[2,8,128,128]{3,2,1,0:T(8,128)S(1)} %get-tuple-element.28.late, f32[2,16,16,128]{3,2,1,0:T(8,128)S(1)} %get-tuple-element.29.ends_new, f32[2,160,128]{2,1,0:T(8,128)S(1)} %get-tuple-element.37.from_strips), custom_call_target="tpu_custom_call" | custom-call | flops 2000000 | bytes 6000000 | tf_op jit(solution)/shard_map/place/pallas_call | solution.py:744
  34.5 7.8 %all-to-all-done = f32[128,1,128]{2,1,0:T(1,128)S(1)} async-done(((f32[128,1,128]{2,1,0:T(1,128)}), f32[128,1,128]{2,1,0:T(1,128)S(1)}, u32[]{:S(2)}, u32[]{:S(2)}) %all-to-all-start) | async-done | bytes 65568 | tf_op jit(solution)/shard_map/all_to_all | solution.py:816
  42.2 0.8 %finish.1 = f32[128,128]{1,0:T(8,128)} custom-call(f32[128,128]{1,0:T(8,128)S(1)} %bitcast.4, f32[3,128,128]{2,1,0:T(8,128)S(1)} %get-tuple-element.39.fields), custom_call_target="tpu_custom_call" | custom-call | tf_op jit(solution)/shard_map/finish/pallas_call | solution.py:784
Async XLA Ops:
  0.6 8.4 %copy-start = (f32[2,16,128,128]{3,2,1,0:T(8,128)S(1)}, f32[2,16,128,128]{3,2,1,0:T(8,128)}, u32[]{:S(2)}) copy-start(f32[2,16,128,128]{3,2,1,0:T(8,128)} %tracers.3) | copy-start | bytes 6291460
  0.6 8.4 %copy-start.1 = (bf16[16,128,128]{2,1,0:T(8,128)(2,1)S(1)}, bf16[16,128,128]{2,1,0:T(8,128)(2,1)}, u32[]{:S(2)}) copy-start(bf16[16,128,128]{2,1,0:T(8,128)(2,1)} %east.3) | copy-start | bytes 1572868
  0.7 8.4 %copy-start.2 = (bf16[16,128,128]{2,1,0:T(8,128)(2,1)S(1)}, bf16[16,128,128]{2,1,0:T(8,128)(2,1)}, u32[]{:S(2)}) copy-start(bf16[16,128,128]{2,1,0:T(8,128)(2,1)} %north.3) | copy-start | bytes 1572868
  0.7 8.4 %copy-start.3 = (s32[128,128]{1,0:T(8,128)S(1)}, s32[128,128]{1,0:T(8,128)}, u32[]{:S(2)}) copy-start(s32[128,128]{1,0:T(8,128)} %levels.5) | copy-start | bytes 196612
  2.0 11.9 %collective-permute-start = (f32[304,128]{1,0:T(8,128)S(1)}, f32[304,128]{1,0:T(8,128)S(1)}, u32[]{:S(2)}, u32[]{:S(2)}) collective-permute-start(f32[304,128]{1,0:T(8,128)S(1)} %get-tuple-element.21.after), channel_id=1, source_target_pairs={{0,8},{8,0},{16,24},{24,16},{32,40},{40,32},{48,56},{56,48},{64,72... | collective-permute-start | bytes 466952 | tf_op jit(solution)/shard_map/ppermute | solution.py:792
  4.6 9.4 %collective-permute-start.1 = (f32[304,128]{1,0:T(8,128)S(1)}, f32[304,128]{1,0:T(8,128)S(1)}, u32[]{:S(2)}, u32[]{:S(2)}) collective-permute-start(f32[304,128]{1,0:T(8,128)S(1)} %get-tuple-element.23), channel_id=1, source_target_pairs={{8,16},{16,8},{24,32},{32,24},{40,48},{48,40},{56,64},{64,56},{72,... | collective-permute-start | bytes 466952 | tf_op jit(solution)/shard_map/ppermute | solution.py:800
  14.5 7.2 %collective-permute-start.2 = (f32[3,144,128]{2,1,0:T(8,128)S(1)}, f32[3,144,128]{2,1,0:T(8,128)S(1)}, u32[]{:S(2)}, u32[]{:S(2)}) collective-permute-start(f32[3,144,128]{2,1,0:T(8,128)S(1)} %get-tuple-element.32), channel_id=1, source_target_pairs={{0,1},{1,0},{2,3},{3,2},{4,5},{5,4},{6,7},{7,6},{8,9},{9,8},{10,11... | collective-permute-start | bytes 663560 | tf_op jit(solution)/shard_map/ppermute | solution.py:792
  15.8 7.2 %collective-permute-start.3 = (f32[3,144,128]{2,1,0:T(8,128)S(1)}, f32[3,144,128]{2,1,0:T(8,128)S(1)}, u32[]{:S(2)}, u32[]{:S(2)}) collective-permute-start(f32[3,144,128]{2,1,0:T(8,128)S(1)} %get-tuple-element.33), channel_id=1, source_target_pairs={{0,0},{7,7},{1,2},{2,1},{3,4},{4,3},{5,6},{6,5},{8,8},{15,15},{9,1... | collective-permute-start | bytes 663560 | tf_op jit(solution)/shard_map/ppermute | solution.py:800
  25.3 16.9 %all-to-all-start = ((f32[128,1,128]{2,1,0:T(1,128)}), f32[128,1,128]{2,1,0:T(1,128)S(1)}, u32[]{:S(2)}, u32[]{:S(2)}) async-start(f32[128,1,128]{2,1,0:T(1,128)} %bitcast.1), calls=%async_computation | async-start | bytes 131072 | tf_op jit(solution)/shard_map/all_to_all | solution.py:816

commit v11 on v10

--- a/solution.py
+++ b/solution.py
@@ -752,7 +752,7 @@
     )(*arrays)
 
 
-def finish_kernel(sums, fields, out):
+def finish_kernel(sums, fields, out, sound):
     value = sums[0:8, :]
     for g in range(8, 128, 8):
         value = value + sums[rows_at(g), :]
@@ -761,19 +761,18 @@
     m0, m1, m2, m3, m4, m5 = (
         jnp.sum(jnp.where(lane == i, value, 0.0), axis=1, keepdims=True) for i in range(6)
     )
-    floor = 4e-7
     l10 = m2 / m1
     l20 = m3 / m1
     d1 = m3 - l10 * m2
     t = m4 - l20 * m2
-    has1 = d1 > floor * m3
-    l21 = jnp.where(has1, t / d1, 0.0)
+    l21 = t / d1
     d2 = m5 - l20 * m3 - l21 * t
-    has2 = has1 & (d2 > floor * m5)
+    enough = (d1 > 0.02 * m3) & (d2 > 0.002 * m5)
+    sound[...] = jnp.broadcast_to(jnp.where(enough, 1.0, 0.0), (8, 128))
     y1 = m1 - l10 * m0
     y2 = m2 - l20 * m0 - l21 * y1
-    c2 = jnp.where(has2, y2 / d2, 0.0)
-    c1 = jnp.where(has1, y1 / d1, 0.0) - l21 * c2
+    c2 = y2 / d2
+    c1 = y1 / d1 - l21 * c2
     c0 = m0 / m1 - l10 * c1 - l20 * c2
     for g in range(0, SX, 8):
         rows = rows_at(g)
@@ -783,9 +782,49 @@
 def finish(sums, fields):
     return pl.pallas_call(
         finish_kernel,
-        out_shape=jax.ShapeDtypeStruct((SX, SY), F32),
+        out_shape=[jax.ShapeDtypeStruct((SX, SY), F32), jax.ShapeDtypeStruct((8, 128), F32)],
         name="finish",
     )(*(pltpu.with_memory_space_constraint(x, pltpu.VMEM) for x in (sums, fields)))
+
+
+def careful(levels, planes):
+    def beside(field, axis, dim):
+        count = lax.axis_size(axis)
+        size = field.shape[dim]
+        up = [(i, (i + 1) % count) for i in range(count)]
+        before = lax.ppermute(lax.slice_in_dim(field, size - 1, size, axis=dim), axis, up)
+        after = lax.ppermute(lax.slice_in_dim(field, 0, 1, axis=dim), axis, [(b, a) for a, b in up])
+        whole = jnp.concatenate([before, field, after], axis=dim)
+        return lax.slice_in_dim(whole, 0, size, axis=dim), lax.slice_in_dim(whole, 2, size + 2, axis=dim)
+
+    def total(field):
+        return lax.psum(jnp.sum(field), ("gx", "gy"))
+
+    depth = levels.astype(F32) / KL
+    at_first = (lax.axis_index("gy") == 0) & (lanes(depth.shape) == 0)
+    at_last = (lax.axis_index("gy") == lax.axis_size("gy") - 1) & (lanes(depth.shape) == SY - 1)
+    west, east = (jnp.minimum(depth, x) for x in beside(depth, "gx", 0))
+    south, north = beside(depth, "gy", 1)
+    south = jnp.where(at_first, 0.0, jnp.minimum(depth, south))
+    north = jnp.where(at_last, 0.0, jnp.minimum(depth, north))
+    diagonal = ALPHA * depth + jnp.where(levels == 0, 1.0, 0.0) + east + west + north + south
+    residual = planes[0] * diagonal
+    precond = direction = planes[0]
+    solution = jnp.zeros_like(residual)
+    now = total(residual * precond)
+    for step in range(3):
+        x_low, x_high = beside(direction, "gx", 0)
+        y_low, y_high = beside(direction, "gy", 1)
+        image = diagonal * direction - east * x_high - west * x_low - north * y_high - south * y_low
+        alpha = now / total(direction * image)
+        solution = solution + alpha * direction
+        if step < 2:
+            residual = residual - alpha * image
+            precond = residual / diagonal
+            later = total(residual * precond)
+            direction = precond + later / now * direction
+            now = later
+    return solution
 
 
 def first_pairs(array, axis):
@@ -815,7 +854,9 @@
     )
     sums = lax.all_to_all(sums, ("gx", "gy"), split_axis=0, concat_axis=0, tiled=True)
     new = place(early, late, ends_new, from_strips)
-    return new, finish(sums, fields)
+    pressure, sound = finish(sums, fields)
+    pressure = lax.cond(sound[0, 0] > 0.5, lambda: pressure, lambda: careful(levels, fields))
+    return new, pressure
 
 
 def solution(mesh):

time: 43.1 us -> 45.9 us (1.065)
  local copies, waits for them, and re-layouts: 0.02 us -> 1.87 us
  between operations: 0.74 us -> 1.39 us
    slice x0 -> x1, local copies, waits for them, and re-layouts: none -> 1.23 us  [on_device(): sound[0, 0] > 0.5]
    unnamed x8 -> x10, local copies, waits for them, and re-layouts: 0.02 us -> 0.64 us
  transfers between devices with their start and end apart: 5 -> 5, of which waited for: 2 -> 2; matrix products, arithmetic and copies ran while one was open for 0% -> 0% of each run, Pallas kernels for 22% -> 21%
where the time goes in v11:
time: 45.9 us; the launch traced here: 45.7 us
  starting transfers between devices  18.9 us (41%)
  Pallas kernels  14.3 us (31%)
  waiting for transfers between devices  9.04 us (20%)
  local copies, waits for them, and re-layouts  1.87 us (4%)
  between operations  1.39 us (3%)
    all_to_all x1, waiting for transfers between devices, on_device(): lax.all_to_all(sums, ('gx', 'gy'), split_axis=0, concat_axis=0, tiled=True)  7.76 us
    ppermute x2, starting transfers between devices, second_pairs(): return lax.ppermute(array, axis, pairs)  7.54 us
    all_to_all x1, starting transfers between devices, on_device(): lax.all_to_all(sums, ('gx', 'gy'), split_axis=0, concat_axis=0, tiled=True)  7.48 us
    pallas_call x1, Pallas kernels, block(): pl.pallas_call(block_kernel, in_specs=[pl.BlockSpec(memory_space=pltpu.VM...  4.89 us
    ppermute x2, starting transfers between devices, first_pairs(): lax.ppermute(array, axis, [(i, i ^ 1) for i in range(lax.axis_size(axis))])  3.84 us
    pallas_call x1, Pallas kernels, late_levels(): pl.pallas_call(late_kernel, out_shape=[pltpu.VMEM((2, KL - EARLY, SX, SY)...  2.84 us
    pallas_call x1, Pallas kernels, operator(): pl.pallas_call(functools.partial(operator_kernel, count=count), out_shape...  2.27 us
    pallas_call x1, Pallas kernels, place(): pl.pallas_call(place_kernel, out_shape=jax.ShapeDtypeStruct(whole, F32),...  1.66 us
  transfers between devices with their start and end apart: 5, of which 2 were waited for; matrix products, arithmetic and copies ran while one was open for 0% of the time, Pallas kernels for 21%

profile of v11, /device:TPU:1, one launch (start us, length us, event | category | flops | bytes accessed | tf_op | source)
XLA Modules:
  0.0 45.7 jit_solution(5558091713146599956)
XLA Ops:
  0.6 0.0 copy-start
  0.6 0.0 copy-start.1
  0.7 0.0 copy-start.2
  0.7 0.0 copy-start.3
  0.7 1.3 %edges.1 = (f32[304,128]{1,0:T(8,128)S(1)}, f32[304,128]{1,0:T(8,128)S(1)}) custom-call(f32[2,16,128,128]{3,2,1,0:T(8,128)} %tracers.3, bf16[16,128,128]{2,1,0:T(8,128)(2,1)} %east.3, bf16[16,128,128]{2,1,0:T(8,128)(2,1)} %north.3, s32[128,128]{1,0:T(8,128)} %levels.5), custom_call_target="tpu_custom_call" | custom-call | tf_op jit(solution)/shard_map/edges/pallas_call | solution.py:111
  2.0 2.5 %collective-permute-start.16 = (f32[304,128]{1,0:T(8,128)S(1)}, f32[304,128]{1,0:T(8,128)S(1)}, u32[]{:S(2)}, u32[]{:S(2)}) collective-permute-start(f32[304,128]{1,0:T(8,128)S(1)} %get-tuple-element.33.after), channel_id=1, source_target_pairs={{0,8},{8,0},{16,24},{24,16},{32,40},{40,32},{48,56},{56,48},{64,72... | collective-permute-start | bytes 466952 | tf_op jit(solution)/shard_map/ppermute | solution.py:831
  4.6 4.4 %collective-permute-start.17 = (f32[304,128]{1,0:T(8,128)S(1)}, f32[304,128]{1,0:T(8,128)S(1)}, u32[]{:S(2)}, u32[]{:S(2)}) collective-permute-start(f32[304,128]{1,0:T(8,128)S(1)} %get-tuple-element.35), channel_id=1, source_target_pairs={{8,16},{16,8},{24,32},{32,24},{40,48},{48,40},{56,64},{64,56},{72,... | collective-permute-start | bytes 466952 | tf_op jit(solution)/shard_map/ppermute | solution.py:839
  9.0 0.0 copy-done
  9.0 0.0 copy-done.1
  9.0 0.0 copy-done.2
  9.0 0.0 copy-done.3
  9.0 4.9 %block.1 = (f32[2,5,128,128]{3,2,1,0:T(8,128)S(1)}, f32[3,128,128]{2,1,0:T(8,128)S(1)}, f32[3,128,128]{2,1,0:T(8,128)S(1)}, f32[2,8,128,128]{3,2,1,0:T(8,128)S(1)}, f32[160,128]{1,0:T(8,128)S(1)}) custom-call(f32[2,16,128,128]{3,2,1,0:T(8,128)S(1)} %copy-done, bf16[16,128,128]{2,1,0:T(8,128)(2,1)S(1)} %copy-done.1, bf16[16,128,128]{2,1,0:T(8,128)(2,1)S(1)} %copy-done.2, ...), custom_call_target="tpu_custom_call" | custom-call | flops 20000000 | bytes 24000000 | tf_op jit(solution)/shard_map/block/pallas_call | solution.py:394
  13.9 0.0 collective-permute-done.16.first_pair
  13.9 0.0 collective-permute-done.17.second_pair
  13.9 0.6 %pack_edges.1 = (f32[2,5,16,128]{3,2,1,0:T(8,128)S(1)}, f32[3,144,128]{2,1,0:T(8,128)S(1)}, f32[3,144,128]{2,1,0:T(8,128)S(1)}, f32[65,8,128]{2,1,0:T(8,128)S(1)}, f32[65,8,128]{2,1,0:T(8,128)S(1)}) custom-call(f32[304,128]{1,0:T(8,128)S(1)} %collective-permute-done.16.first_pair, f32[304,128]{1,0:T(8,128)S(1)} %collective-permute-done.17.second_pair, ...), custom_call_target="tpu_custom_call" | custom-call | tf_op jit(solution)/shard_map/pack_edges/pallas_call | solution.py:252
  14.5 1.3 %collective-permute-start.18 = (f32[3,144,128]{2,1,0:T(8,128)S(1)}, f32[3,144,128]{2,1,0:T(8,128)S(1)}, u32[]{:S(2)}, u32[]{:S(2)}) collective-permute-start(f32[3,144,128]{2,1,0:T(8,128)S(1)} %get-tuple-element.44), channel_id=1, source_target_pairs={{0,1},{1,0},{2,3},{3,2},{4,5},{5,4},{6,7},{7,6},{8,9},{9,8},{10,11... | collective-permute-start | bytes 663560 | tf_op jit(solution)/shard_map/ppermute | solution.py:831
  15.8 3.1 %collective-permute-start.19 = (f32[3,144,128]{2,1,0:T(8,128)S(1)}, f32[3,144,128]{2,1,0:T(8,128)S(1)}, u32[]{:S(2)}, u32[]{:S(2)}) collective-permute-start(f32[3,144,128]{2,1,0:T(8,128)S(1)} %get-tuple-element.45), channel_id=1, source_target_pairs={{0,0},{7,7},{1,2},{2,1},{3,4},{4,3},{5,6},{6,5},{8,8},{15,15},{9,1... | collective-permute-start | bytes 663560 | tf_op jit(solution)/shard_map/ppermute | solution.py:839
  18.9 2.8 %late_levels.1 = (f32[2,8,128,128]{3,2,1,0:T(8,128)S(1)}, f32[160,128]{1,0:T(8,128)S(1)}, f32[2,16,16,128]{3,2,1,0:T(8,128)S(1)}, f32[48,128]{1,0:T(8,128)S(1)}) custom-call(f32[2,16,128,128]{3,2,1,0:T(8,128)S(1)} %copy-done, bf16[16,128,128]{2,1,0:T(8,128)(2,1)S(1)} %copy-done.1, bf16[16,128,128]{2,1,0:T(8,128)(2,1)S(1)} %copy-done.2, ...), custom_call_target="tpu_custom_call" | custom-call | flops 5000000 | bytes 6000000 | tf_op jit(solution)/shard_map/late_levels/pallas_call | solution.py:469
  21.8 0.0 collective-permute-done.18.first_pair
  21.8 1.3 %collective-permute-done.19.second_pair = f32[3,144,128]{2,1,0:T(8,128)S(1)} collective-permute-done((f32[3,144,128]{2,1,0:T(8,128)S(1)}, f32[3,144,128]{2,1,0:T(8,128)S(1)}, u32[]{:S(2)}, u32[]{:S(2)}) %collective-permute-start.19) | collective-permute-done | bytes 221216 | tf_op jit(solution)/shard_map/ppermute | solution.py:839
  23.0 2.3 %operator.1 = (f32[2,160,128]{2,1,0:T(8,128)S(1)}, f32[3,128,128]{2,1,0:T(8,128)S(1)}, f32[128,128]{1,0:T(8,128)}) custom-call(s32[128,128]{1,0:T(8,128)S(1)} %copy-done.3, f32[65,8,128]{2,1,0:T(8,128)S(1)} %get-tuple-element.38.low, f32[65,8,128]{2,1,0:T(8,128)S(1)} %get-tuple-element.39.high, f32[2,5,128,128]{3,2,1,0:T(8,128)S(1)} %get-tuple-element.42.own_rows, ...), custom_call_target="tpu_custom_call" | custom-call | tf_op jit(solution)/shard_map/operator/pallas_call | solution.py:705
  25.3 7.5 %all-to-all-start = ((f32[128,1,128]{2,1,0:T(1,128)}), f32[128,1,128]{2,1,0:T(1,128)S(1)}, u32[]{:S(2)}, u32[]{:S(2)}) async-start(f32[128,1,128]{2,1,0:T(1,128)} %bitcast.4), calls=%async_computation | async-start | bytes 131072 | tf_op jit(solution)/shard_map/all_to_all | solution.py:855
  32.8 1.7 %place.1 = f32[2,16,128,128]{3,2,1,0:T(8,128)} custom-call(f32[2,8,128,128]{3,2,1,0:T(8,128)S(1)} %get-tuple-element.34.early, f32[2,8,128,128]{3,2,1,0:T(8,128)S(1)} %get-tuple-element.40.late, f32[2,16,16,128]{3,2,1,0:T(8,128)S(1)} %get-tuple-element.41.ends_new, f32[2,160,128]{2,1,0:T(8,128)S(1)} %get-tuple-element.49.from_strips), custom_call_target="tpu_custom_call" | custom-call | flops 2000000 | bytes 6000000 | tf_op jit(solution)/shard_map/place/pallas_call | solution.py:744
  34.5 7.8 %all-to-all-done = f32[128,1,128]{2,1,0:T(1,128)S(1)} async-done(((f32[128,1,128]{2,1,0:T(1,128)}), f32[128,1,128]{2,1,0:T(1,128)S(1)}, u32[]{:S(2)}, u32[]{:S(2)}) %all-to-all-start) | async-done | bytes 65568 | tf_op jit(solution)/shard_map/all_to_all | solution.py:855
  42.2 0.7 %finish.1 = (f32[128,128]{1,0:T(8,128)S(1)}, f32[8,128]{1,0:T(8,128)}) custom-call(f32[128,128]{1,0:T(8,128)S(1)} %bitcast.36, f32[3,128,128]{2,1,0:T(8,128)S(1)} %get-tuple-element.51.fields), custom_call_target="tpu_custom_call" | custom-call | tf_op jit(solution)/shard_map/finish/pallas_call | solution.py:783
  42.9 1.2 %slice.127 = f32[1,1]{1,0:T(1,128)} slice(f32[8,128]{1,0:T(8,128)} %get-tuple-element.52), slice={[0:1], [0:1]} | slice | bytes 8 | tf_op jit(solution)/shard_map/slice | solution.py:858
  44.8 0.2 conditional.1
  45.0 0.0 copy-start.4
  45.1 0.6 %copy-done.4 = f32[128,128]{1,0:T(8,128)} copy-done((f32[128,128]{1,0:T(8,128)}, f32[128,128]{1,0:T(8,128)S(1)}, u32[]{:S(2)}) %copy-start.4) | copy-done | bytes 65560
Async XLA Ops:
  0.6 8.4 %copy-start = (f32[2,16,128,128]{3,2,1,0:T(8,128)S(1)}, f32[2,16,128,128]{3,2,1,0:T(8,128)}, u32[]{:S(2)}) copy-start(f32[2,16,128,128]{3,2,1,0:T(8,128)} %tracers.3) | copy-start | bytes 6291460
  0.6 8.4 %copy-start.1 = (bf16[16,128,128]{2,1,0:T(8,128)(2,1)S(1)}, bf16[16,128,128]{2,1,0:T(8,128)(2,1)}, u32[]{:S(2)}) copy-start(bf16[16,128,128]{2,1,0:T(8,128)(2,1)} %east.3) | copy-start | bytes 1572868
  0.7 8.4 %copy-start.2 = (bf16[16,128,128]{2,1,0:T(8,128)(2,1)S(1)}, bf16[16,128,128]{2,1,0:T(8,128)(2,1)}, u32[]{:S(2)}) copy-start(bf16[16,128,128]{2,1,0:T(8,128)(2,1)} %north.3) | copy-start | bytes 1572868
  0.7 8.4 %copy-start.3 = (s32[128,128]{1,0:T(8,128)S(1)}, s32[128,128]{1,0:T(8,128)}, u32[]{:S(2)}) copy-start(s32[128,128]{1,0:T(8,128)} %levels.5) | copy-start | bytes 196612
  2.0 11.9 %collective-permute-start.16 = (f32[304,128]{1,0:T(8,128)S(1)}, f32[304,128]{1,0:T(8,128)S(1)}, u32[]{:S(2)}, u32[]{:S(2)}) collective-permute-start(f32[304,128]{1,0:T(8,128)S(1)} %get-tuple-element.33.after), channel_id=1, source_target_pairs={{0,8},{8,0},{16,24},{24,16},{32,40},{40,32},{48,56},{56,48},{64,72... | collective-permute-start | bytes 466952 | tf_op jit(solution)/shard_map/ppermute | solution.py:831
  4.6 9.4 %collective-permute-start.17 = (f32[304,128]{1,0:T(8,128)S(1)}, f32[304,128]{1,0:T(8,128)S(1)}, u32[]{:S(2)}, u32[]{:S(2)}) collective-permute-start(f32[304,128]{1,0:T(8,128)S(1)} %get-tuple-element.35), channel_id=1, source_target_pairs={{8,16},{16,8},{24,32},{32,24},{40,48},{48,40},{56,64},{64,56},{72,... | collective-permute-start | bytes 466952 | tf_op jit(solution)/shard_map/ppermute | solution.py:839
  14.5 7.3 %collective-permute-start.18 = (f32[3,144,128]{2,1,0:T(8,128)S(1)}, f32[3,144,128]{2,1,0:T(8,128)S(1)}, u32[]{:S(2)}, u32[]{:S(2)}) collective-permute-start(f32[3,144,128]{2,1,0:T(8,128)S(1)} %get-tuple-element.44), channel_id=1, source_target_pairs={{0,1},{1,0},{2,3},{3,2},{4,5},{5,4},{6,7},{7,6},{8,9},{9,8},{10,11... | collective-permute-start | bytes 663560 | tf_op jit(solution)/shard_map/ppermute | solution.py:831
  15.8 7.2 %collective-permute-start.19 = (f32[3,144,128]{2,1,0:T(8,128)S(1)}, f32[3,144,128]{2,1,0:T(8,128)S(1)}, u32[]{:S(2)}, u32[]{:S(2)}) collective-permute-start(f32[3,144,128]{2,1,0:T(8,128)S(1)} %get-tuple-element.45), channel_id=1, source_target_pairs={{0,0},{7,7},{1,2},{2,1},{3,4},{4,3},{5,6},{6,5},{8,8},{15,15},{9,1... | collective-permute-start | bytes 663560 | tf_op jit(solution)/shard_map/ppermute | solution.py:839
  25.3 16.9 %all-to-all-start = ((f32[128,1,128]{2,1,0:T(1,128)}), f32[128,1,128]{2,1,0:T(1,128)S(1)}, u32[]{:S(2)}, u32[]{:S(2)}) async-start(f32[128,1,128]{2,1,0:T(1,128)} %bitcast.4), calls=%async_computation | async-start | bytes 131072 | tf_op jit(solution)/shard_map/all_to_all | solution.py:855
  45.0 0.6 %copy-start.4 = (f32[128,128]{1,0:T(8,128)}, f32[128,128]{1,0:T(8,128)S(1)}, u32[]{:S(2)}) copy-start(f32[128,128]{1,0:T(8,128)S(1)} %get-tuple-element.80) | copy-start | bytes 196612

commit v12 on v11

--- a/solution.py
+++ b/solution.py
@@ -768,7 +768,7 @@
     l21 = t / d1
     d2 = m5 - l20 * m3 - l21 * t
     enough = (d1 > 0.02 * m3) & (d2 > 0.002 * m5)
-    sound[...] = jnp.broadcast_to(jnp.where(enough, 1.0, 0.0), (8, 128))
+    sound[0] = jnp.where(enough, 1.0, 0.0)[0, 0]
     y1 = m1 - l10 * m0
     y2 = m2 - l20 * m0 - l21 * y1
     c2 = y2 / d2
@@ -782,7 +782,8 @@
 def finish(sums, fields):
     return pl.pallas_call(
         finish_kernel,
-        out_shape=[jax.ShapeDtypeStruct((SX, SY), F32), jax.ShapeDtypeStruct((8, 128), F32)],
+        out_shape=[jax.ShapeDtypeStruct((SX, SY), F32), jax.ShapeDtypeStruct((1,), F32)],
+        out_specs=[pl.BlockSpec(memory_space=pltpu.VMEM), pl.BlockSpec(memory_space=pltpu.SMEM)],
         name="finish",
     )(*(pltpu.with_memory_space_constraint(x, pltpu.VMEM) for x in (sums, fields)))
 
@@ -855,7 +856,7 @@
     sums = lax.all_to_all(sums, ("gx", "gy"), split_axis=0, concat_axis=0, tiled=True)
     new = place(early, late, ends_new, from_strips)
     pressure, sound = finish(sums, fields)
-    pressure = lax.cond(sound[0, 0] > 0.5, lambda: pressure, lambda: careful(levels, fields))
+    pressure = lax.cond(sound[0] > 0.5, lambda: pressure, lambda: careful(levels, fields))
     return new, pressure
 
 

time: 45.9 us -> 44.6 us (0.972)
  local copies, waits for them, and re-layouts: 1.87 us -> 0.64 us
    slice x1 -> x0, local copies, waits for them, and re-layouts: 1.23 us -> none  [on_device(): sound[0, 0] > 0.5]
where the time goes in v12:
time: 44.6 us; the launch traced here: 44.4 us
  starting transfers between devices  18.9 us (42%)
  Pallas kernels  14.2 us (32%)
  waiting for transfers between devices  9.04 us (20%)
  between operations  1.41 us (3%)
  local copies, waits for them, and re-layouts  0.64 us (1%)
    all_to_all x1, waiting for transfers between devices, on_device(): lax.all_to_all(sums, ('gx', 'gy'), split_axis=0, concat_axis=0, tiled=True)  7.76 us
    ppermute x2, starting transfers between devices, second_pairs(): return lax.ppermute(array, axis, pairs)  7.54 us
    all_to_all x1, starting transfers between devices, on_device(): lax.all_to_all(sums, ('gx', 'gy'), split_axis=0, concat_axis=0, tiled=True)  7.48 us
    pallas_call x1, Pallas kernels, block(): pl.pallas_call(block_kernel, in_specs=[pl.BlockSpec(memory_space=pltpu.VM...  4.89 us
    ppermute x2, starting transfers between devices, first_pairs(): lax.ppermute(array, axis, [(i, i ^ 1) for i in range(lax.axis_size(axis))])  3.84 us
    pallas_call x1, Pallas kernels, late_levels(): pl.pallas_call(late_kernel, out_shape=[pltpu.VMEM((2, KL - EARLY, SX, SY)...  2.84 us
    pallas_call x1, Pallas kernels, operator(): pl.pallas_call(functools.partial(operator_kernel, count=count), out_shape...  2.27 us
    pallas_call x1, Pallas kernels, place(): pl.pallas_call(place_kernel, out_shape=jax.ShapeDtypeStruct(whole, F32),...  1.66 us
  transfers between devices with their start and end apart: 5, of which 2 were waited for; matrix products, arithmetic and copies ran while one was open for 0% of the time, Pallas kernels for 21%

profile of v12, /device:TPU:1, one launch (start us, length us, event | category | flops | bytes accessed | tf_op | source)
XLA Modules:
  0.0 44.4 jit_solution(6926232286699376674)
XLA Ops:
  0.6 0.0 copy-start
  0.6 0.0 copy-start.1
  0.7 0.0 copy-start.2
  0.7 0.0 copy-start.3
  0.7 1.3 %edges.1 = (f32[304,128]{1,0:T(8,128)S(1)}, f32[304,128]{1,0:T(8,128)S(1)}) custom-call(f32[2,16,128,128]{3,2,1,0:T(8,128)} %tracers.3, bf16[16,128,128]{2,1,0:T(8,128)(2,1)} %east.3, bf16[16,128,128]{2,1,0:T(8,128)(2,1)} %north.3, s32[128,128]{1,0:T(8,128)} %levels.5), custom_call_target="tpu_custom_call" | custom-call | tf_op jit(solution)/shard_map/edges/pallas_call | solution.py:111
  2.0 2.5 %collective-permute-start.16 = (f32[304,128]{1,0:T(8,128)S(1)}, f32[304,128]{1,0:T(8,128)S(1)}, u32[]{:S(2)}, u32[]{:S(2)}) collective-permute-start(f32[304,128]{1,0:T(8,128)S(1)} %get-tuple-element.33.after), channel_id=1, source_target_pairs={{0,8},{8,0},{16,24},{24,16},{32,40},{40,32},{48,56},{56,48},{64,72... | collective-permute-start | bytes 466952 | tf_op jit(solution)/shard_map/ppermute | solution.py:832
  4.6 4.4 %collective-permute-start.17 = (f32[304,128]{1,0:T(8,128)S(1)}, f32[304,128]{1,0:T(8,128)S(1)}, u32[]{:S(2)}, u32[]{:S(2)}) collective-permute-start(f32[304,128]{1,0:T(8,128)S(1)} %get-tuple-element.35), channel_id=1, source_target_pairs={{8,16},{16,8},{24,32},{32,24},{40,48},{48,40},{56,64},{64,56},{72,... | collective-permute-start | bytes 466952 | tf_op jit(solution)/shard_map/ppermute | solution.py:840
  9.0 0.0 copy-done
  9.0 0.0 copy-done.1
  9.0 0.0 copy-done.2
  9.0 0.0 copy-done.3
  9.0 4.9 %block.1 = (f32[2,5,128,128]{3,2,1,0:T(8,128)S(1)}, f32[3,128,128]{2,1,0:T(8,128)S(1)}, f32[3,128,128]{2,1,0:T(8,128)S(1)}, f32[2,8,128,128]{3,2,1,0:T(8,128)S(1)}, f32[160,128]{1,0:T(8,128)S(1)}) custom-call(f32[2,16,128,128]{3,2,1,0:T(8,128)S(1)} %copy-done, bf16[16,128,128]{2,1,0:T(8,128)(2,1)S(1)} %copy-done.1, bf16[16,128,128]{2,1,0:T(8,128)(2,1)S(1)} %copy-done.2, ...), custom_call_target="tpu_custom_call" | custom-call | flops 20000000 | bytes 24000000 | tf_op jit(solution)/shard_map/block/pallas_call | solution.py:394
  13.9 0.0 collective-permute-done.16.first_pair
  13.9 0.0 collective-permute-done.17.second_pair
  13.9 0.6 %pack_edges.1 = (f32[2,5,16,128]{3,2,1,0:T(8,128)S(1)}, f32[3,144,128]{2,1,0:T(8,128)S(1)}, f32[3,144,128]{2,1,0:T(8,128)S(1)}, f32[65,8,128]{2,1,0:T(8,128)S(1)}, f32[65,8,128]{2,1,0:T(8,128)S(1)}) custom-call(f32[304,128]{1,0:T(8,128)S(1)} %collective-permute-done.16.first_pair, f32[304,128]{1,0:T(8,128)S(1)} %collective-permute-done.17.second_pair, ...), custom_call_target="tpu_custom_call" | custom-call | tf_op jit(solution)/shard_map/pack_edges/pallas_call | solution.py:252
  14.5 1.3 %collective-permute-start.18 = (f32[3,144,128]{2,1,0:T(8,128)S(1)}, f32[3,144,128]{2,1,0:T(8,128)S(1)}, u32[]{:S(2)}, u32[]{:S(2)}) collective-permute-start(f32[3,144,128]{2,1,0:T(8,128)S(1)} %get-tuple-element.44), channel_id=1, source_target_pairs={{0,1},{1,0},{2,3},{3,2},{4,5},{5,4},{6,7},{7,6},{8,9},{9,8},{10,11... | collective-permute-start | bytes 663560 | tf_op jit(solution)/shard_map/ppermute | solution.py:832
  15.8 3.1 %collective-permute-start.19 = (f32[3,144,128]{2,1,0:T(8,128)S(1)}, f32[3,144,128]{2,1,0:T(8,128)S(1)}, u32[]{:S(2)}, u32[]{:S(2)}) collective-permute-start(f32[3,144,128]{2,1,0:T(8,128)S(1)} %get-tuple-element.45), channel_id=1, source_target_pairs={{0,0},{7,7},{1,2},{2,1},{3,4},{4,3},{5,6},{6,5},{8,8},{15,15},{9,1... | collective-permute-start | bytes 663560 | tf_op jit(solution)/shard_map/ppermute | solution.py:840
  18.9 2.8 %late_levels.1 = (f32[2,8,128,128]{3,2,1,0:T(8,128)S(1)}, f32[160,128]{1,0:T(8,128)S(1)}, f32[2,16,16,128]{3,2,1,0:T(8,128)S(1)}, f32[48,128]{1,0:T(8,128)S(1)}) custom-call(f32[2,16,128,128]{3,2,1,0:T(8,128)S(1)} %copy-done, bf16[16,128,128]{2,1,0:T(8,128)(2,1)S(1)} %copy-done.1, bf16[16,128,128]{2,1,0:T(8,128)(2,1)S(1)} %copy-done.2, ...), custom_call_target="tpu_custom_call" | custom-call | flops 5000000 | bytes 6000000 | tf_op jit(solution)/shard_map/late_levels/pallas_call | solution.py:469
  21.8 0.0 collective-permute-done.18.first_pair
  21.8 1.3 %collective-permute-done.19.second_pair = f32[3,144,128]{2,1,0:T(8,128)S(1)} collective-permute-done((f32[3,144,128]{2,1,0:T(8,128)S(1)}, f32[3,144,128]{2,1,0:T(8,128)S(1)}, u32[]{:S(2)}, u32[]{:S(2)}) %collective-permute-start.19) | collective-permute-done | bytes 221216 | tf_op jit(solution)/shard_map/ppermute | solution.py:840
  23.0 2.3 %operator.1 = (f32[2,160,128]{2,1,0:T(8,128)S(1)}, f32[3,128,128]{2,1,0:T(8,128)S(1)}, f32[128,128]{1,0:T(8,128)}) custom-call(s32[128,128]{1,0:T(8,128)S(1)} %copy-done.3, f32[65,8,128]{2,1,0:T(8,128)S(1)} %get-tuple-element.38.low, f32[65,8,128]{2,1,0:T(8,128)S(1)} %get-tuple-element.39.high, f32[2,5,128,128]{3,2,1,0:T(8,128)S(1)} %get-tuple-element.42.own_rows, ...), custom_call_target="tpu_custom_call" | custom-call | tf_op jit(solution)/shard_map/operator/pallas_call | solution.py:705
  25.3 7.5 %all-to-all-start = ((f32[128,1,128]{2,1,0:T(1,128)}), f32[128,1,128]{2,1,0:T(1,128)S(1)}, u32[]{:S(2)}, u32[]{:S(2)}) async-start(f32[128,1,128]{2,1,0:T(1,128)} %bitcast.4), calls=%async_computation | async-start | bytes 131072 | tf_op jit(solution)/shard_map/all_to_all | solution.py:856
  32.8 1.7 %place.1 = f32[2,16,128,128]{3,2,1,0:T(8,128)} custom-call(f32[2,8,128,128]{3,2,1,0:T(8,128)S(1)} %get-tuple-element.34.early, f32[2,8,128,128]{3,2,1,0:T(8,128)S(1)} %get-tuple-element.40.late, f32[2,16,16,128]{3,2,1,0:T(8,128)S(1)} %get-tuple-element.41.ends_new, f32[2,160,128]{2,1,0:T(8,128)S(1)} %get-tuple-element.49.from_strips), custom_call_target="tpu_custom_call" | custom-call | flops 2000000 | bytes 6000000 | tf_op jit(solution)/shard_map/place/pallas_call | solution.py:744
  34.5 7.8 %all-to-all-done = f32[128,1,128]{2,1,0:T(1,128)S(1)} async-done(((f32[128,1,128]{2,1,0:T(1,128)}), f32[128,1,128]{2,1,0:T(1,128)S(1)}, u32[]{:S(2)}, u32[]{:S(2)}) %all-to-all-start) | async-done | bytes 65568 | tf_op jit(solution)/shard_map/all_to_all | solution.py:856
  42.2 0.7 %finish.1 = (f32[128,128]{1,0:T(8,128)S(1)}, f32[1]{0:T(128)}) custom-call(f32[128,128]{1,0:T(8,128)S(1)} %bitcast.36, f32[3,128,128]{2,1,0:T(8,128)S(1)} %get-tuple-element.51.fields), custom_call_target="tpu_custom_call" | custom-call | tf_op jit(solution)/shard_map/finish/pallas_call | solution.py:783
  43.5 0.2 conditional.1
  43.8 0.0 copy-start.4
  43.8 0.6 %copy-done.4 = f32[128,128]{1,0:T(8,128)} copy-done((f32[128,128]{1,0:T(8,128)}, f32[128,128]{1,0:T(8,128)S(1)}, u32[]{:S(2)}) %copy-start.4) | copy-done | bytes 65560
Async XLA Ops:
  0.6 8.4 %copy-start = (f32[2,16,128,128]{3,2,1,0:T(8,128)S(1)}, f32[2,16,128,128]{3,2,1,0:T(8,128)}, u32[]{:S(2)}) copy-start(f32[2,16,128,128]{3,2,1,0:T(8,128)} %tracers.3) | copy-start | bytes 6291460
  0.6 8.4 %copy-start.1 = (bf16[16,128,128]{2,1,0:T(8,128)(2,1)S(1)}, bf16[16,128,128]{2,1,0:T(8,128)(2,1)}, u32[]{:S(2)}) copy-start(bf16[16,128,128]{2,1,0:T(8,128)(2,1)} %east.3) | copy-start | bytes 1572868
  0.7 8.4 %copy-start.2 = (bf16[16,128,128]{2,1,0:T(8,128)(2,1)S(1)}, bf16[16,128,128]{2,1,0:T(8,128)(2,1)}, u32[]{:S(2)}) copy-start(bf16[16,128,128]{2,1,0:T(8,128)(2,1)} %north.3) | copy-start | bytes 1572868
  0.7 8.4 %copy-start.3 = (s32[128,128]{1,0:T(8,128)S(1)}, s32[128,128]{1,0:T(8,128)}, u32[]{:S(2)}) copy-start(s32[128,128]{1,0:T(8,128)} %levels.5) | copy-start | bytes 196612
  2.0 11.9 %collective-permute-start.16 = (f32[304,128]{1,0:T(8,128)S(1)}, f32[304,128]{1,0:T(8,128)S(1)}, u32[]{:S(2)}, u32[]{:S(2)}) collective-permute-start(f32[304,128]{1,0:T(8,128)S(1)} %get-tuple-element.33.after), channel_id=1, source_target_pairs={{0,8},{8,0},{16,24},{24,16},{32,40},{40,32},{48,56},{56,48},{64,72... | collective-permute-start | bytes 466952 | tf_op jit(solution)/shard_map/ppermute | solution.py:832
  4.6 9.4 %collective-permute-start.17 = (f32[304,128]{1,0:T(8,128)S(1)}, f32[304,128]{1,0:T(8,128)S(1)}, u32[]{:S(2)}, u32[]{:S(2)}) collective-permute-start(f32[304,128]{1,0:T(8,128)S(1)} %get-tuple-element.35), channel_id=1, source_target_pairs={{8,16},{16,8},{24,32},{32,24},{40,48},{48,40},{56,64},{64,56},{72,... | collective-permute-start | bytes 466952 | tf_op jit(solution)/shard_map/ppermute | solution.py:840
  14.5 7.3 %collective-permute-start.18 = (f32[3,144,128]{2,1,0:T(8,128)S(1)}, f32[3,144,128]{2,1,0:T(8,128)S(1)}, u32[]{:S(2)}, u32[]{:S(2)}) collective-permute-start(f32[3,144,128]{2,1,0:T(8,128)S(1)} %get-tuple-element.44), channel_id=1, source_target_pairs={{0,1},{1,0},{2,3},{3,2},{4,5},{5,4},{6,7},{7,6},{8,9},{9,8},{10,11... | collective-permute-start | bytes 663560 | tf_op jit(solution)/shard_map/ppermute | solution.py:832
  15.8 7.2 %collective-permute-start.19 = (f32[3,144,128]{2,1,0:T(8,128)S(1)}, f32[3,144,128]{2,1,0:T(8,128)S(1)}, u32[]{:S(2)}, u32[]{:S(2)}) collective-permute-start(f32[3,144,128]{2,1,0:T(8,128)S(1)} %get-tuple-element.45), channel_id=1, source_target_pairs={{0,0},{7,7},{1,2},{2,1},{3,4},{4,3},{5,6},{6,5},{8,8},{15,15},{9,1... | collective-permute-start | bytes 663560 | tf_op jit(solution)/shard_map/ppermute | solution.py:840
  25.3 16.9 %all-to-all-start = ((f32[128,1,128]{2,1,0:T(1,128)}), f32[128,1,128]{2,1,0:T(1,128)S(1)}, u32[]{:S(2)}, u32[]{:S(2)}) async-start(f32[128,1,128]{2,1,0:T(1,128)} %bitcast.4), calls=%async_computation | async-start | bytes 131072 | tf_op jit(solution)/shard_map/all_to_all | solution.py:856
  43.8 0.6 %copy-start.4 = (f32[128,128]{1,0:T(8,128)}, f32[128,128]{1,0:T(8,128)S(1)}, u32[]{:S(2)}) copy-start(f32[128,128]{1,0:T(8,128)S(1)} %get-tuple-element.80) | copy-start | bytes 196612
